TPU v7x, 32 devices: a whole 2x2x4 slice. The times are simulated.
32 devices in a mesh: rows: 8 (over y, x, core), cols: 4 (over z).
Axes of the slice: x: 2, y: 2, z: 4, core: 2. Of those that a mesh axis runs over, the one named last changes fastest.
Arguments:
- anomalies: bfloat16 [16384, 64], P(('rows', 'cols')), may hold values from -6 to 6
- innovations: bfloat16 [16384, 64], P(('rows', 'cols')), may hold values from -3 to 3
- pair_rows: int32 [8, 2048], P('rows', 'cols'), may hold values from 0 to 15, as said below
- pair_cols: int32 [8, 2048], P('rows', 'cols'), may hold values from 0 to 31
- pair_dist: int32 [8, 2048], P('rows', 'cols'), may hold values from 0 to 7
- pair_counts: int32 [8, 4], P('rows', 'cols'), may hold values from 64 to 512, as said below
Outputs:
- increment: float32 [16384, 64], P(('rows', 'cols'))
Inputs may be any that keep to these rules, and one draw needn't show every extreme that they name: In the 512 slots of one device the pairs (pair_rows, pair_cols) are distinct, and each row block stands in at most 32 of them. `pair_counts`: some device has all its slots live in every draw.
All inputs are finite; a program needn't handle non-finite values.
Results may differ from a plain program's by a relative error of at most 0.005.
Values may be sent and summed in bfloat16 or wider, within the bound.
No kernel may reach another device: no remote copies, remote signals or barrier semaphores. Data moves between devices by JAX's collectives and lax.ppermute only.
A program may use at most 128 MiB of HBM per device.

v0:
```python
import math

import jax
import jax.numpy as jnp
from jax import lax
from jax.sharding import PartitionSpec as P

BLK = 128
M = 64
TAPER_CELLS = 8


DIST_SCALE = 4.0


def local(anomalies, innovations, pair_rows, pair_cols, pair_dist, pair_counts):
    members = anomalies.shape[1]
    columns = innovations.shape[1]
    row_anom = lax.all_gather(anomalies, "cols", axis=0, tiled=True)
    col_anom, col_innov = (
        lax.all_gather(anomalies, "rows", axis=0, tiled=True),
        lax.all_gather(innovations, "rows", axis=0, tiled=True),
    )
    row_blocks = row_anom.reshape(-1, BLK, members)
    col_blocks = col_anom.reshape(-1, BLK, members)
    innov_blocks = col_innov.reshape(-1, BLK, columns)
    block_total = row_blocks.shape[0]
    slots = pair_rows.shape[1]
    group_size = math.gcd(128, slots)
    offsets = jnp.arange(BLK)
    kernel = jnp.exp(
        -jnp.abs(offsets[:, None] - offsets[None, :]).astype(jnp.float32) / TAPER_CELLS
    )
    block_index = jnp.arange(block_total)
    slot_offsets = jnp.arange(group_size)
    filled = pair_counts[0, 0]
    loop_turns = (filled + group_size - 1) // group_size
    row_list = pair_rows[0]
    col_list = pair_cols[0]
    dist_list = pair_dist[0]

    def one_group(turn_index, totals):
        first_slot = turn_index * group_size
        local_rows = lax.dynamic_slice_in_dim(row_list, first_slot, group_size)
        col_local = lax.dynamic_slice_in_dim(col_list, first_slot, group_size)
        distances = lax.dynamic_slice_in_dim(dist_list, first_slot, group_size)
        live_slot = first_slot + slot_offsets < filled
        left = jnp.take(row_blocks, local_rows, axis=0)
        right = jnp.take(col_blocks, col_local, axis=0)
        innov = jnp.take(innov_blocks, col_local, axis=0)
        products = jnp.einsum("pim,pjm->pij", left, right, preferred_element_type=jnp.float32)
        block_weight = jnp.where(
            live_slot, jnp.exp(-distances.astype(jnp.float32) / DIST_SCALE), 0.0
        )
        tapered = (products * (1.0 / (M - 1)) * block_weight[:, None, None] * kernel).astype(
            jnp.bfloat16
        )
        applied = jnp.einsum("pij,pjk->pik", tapered, innov, preferred_element_type=jnp.float32)
        onehot = (local_rows[:, None] == block_index[None, :]).astype(jnp.float32)
        return totals + jnp.einsum("pr,pik->rik", onehot, applied)

    totals = jnp.zeros((block_total, BLK, columns), jnp.float32)
    totals = lax.fori_loop(0, loop_turns, one_group, totals)
    partial_rows = totals.reshape(block_total * BLK, columns)
    return lax.psum_scatter(partial_rows, "cols", scatter_dimension=0, tiled=True)


def solution(mesh):
    in_specs = (
        P(("rows", "cols"), None),
        P(("rows", "cols"), None),
        P("rows", "cols"),
        P("rows", "cols"),
        P("rows", "cols"),
        P("rows", "cols"),
    )
    out_specs = P(("rows", "cols"), None)
    return jax.shard_map(local, mesh=mesh, in_specs=in_specs, out_specs=out_specs, check_vma=False)
```

profile of v0, /device:TPU:0, one launch (start us, length us, event | category | flops | bytes accessed | tf_op | source)
XLA Modules:
  0.0 170.2 jit_solution(13304662093454672357)
XLA Ops:
  7.2 15.8 %all_gather.9 = bf16[2048,64]{0,1:T(8,128)(2,1)S(1)} all-gather(bf16[512,64]{0,1:T(8,128)(2,1)} %param.10), channel_id=1, replica_groups=mesh['rows'=8,'cols'=4] {'cols'}, dimensions={0}, use_global_device_ids=true | all-gather | bytes 327680 | tf_op jit(solution)/shard_map/all_gather | solution.py:19
  23.0 10.1 %all_gather.10 = bf16[4096,64]{0,1:T(8,128)(2,1)S(1)} all-gather(bf16[512,64]{0,1:T(8,128)(2,1)} %param.10), channel_id=1, replica_groups=mesh['rows'=8,'cols'=4] {'rows'}, dimensions={0}, use_global_device_ids=true | all-gather | bytes 589824 | tf_op jit(solution)/shard_map/all_gather | solution.py:21
  33.5 9.6 %all_gather.11 = bf16[4096,64]{0,1:T(8,128)(2,1)S(1)} all-gather(bf16[512,64]{0,1:T(8,128)(2,1)} %param.11), channel_id=1, replica_groups=mesh['rows'=8,'cols'=4] {'rows'}, dimensions={0}, use_global_device_ids=true | all-gather | bytes 589824 | tf_op jit(solution)/shard_map/all_gather | solution.py:22
  44.0 72.7 %while.11 = (s32[]{:T(128)}, f32[16,128,64]{1,0,2:T(8,128)S(1)}, s32[]{:T(128)}, s32[512]{0:T(512)}, bf16[16,128,64]{2,1,0:T(8,128)(2,1)S(1)}, /*index=5*/s32[51...) while((s32[]{:T(128)}, f32[16,128,64]{1,0,2:T(8,128)S(1)}, ...), condition=%wide.region_1.3_spmd.clone, body=%wide.region_0.2_spmd.clone.sunk | while | flops 580082432 | bytes 24264900 | solution.py:63
  44.1 1.4 fusion.50
  46.3 3.0 %gather_fusion.2 = bf16[128,128,64]{2,1,0:T(8,128)(2,1)} fusion(bf16[16,128,64]{2,1,0:T(8,128)(2,1)S(1)} %get-tuple-element.228, s32[1024]{0:T(1024)S(1)} %pad_clamp_fusion.5), kind=kCustom, calls=%fused_computation.2.clone.clone.1 | custom fusion | bytes 4194816 | tf_op jit(solution)/shard_map/while/body/jit(_take)/gather | solution.py:48
  49.4 3.1 %gather_fusion.1 = bf16[128,128,64]{2,1,0:T(8,128)(2,1)} fusion(bf16[32,128,64]{2,1,0:T(8,128)(2,1)S(1)} %get-tuple-element.230, s32[1024]{0:T(1024)S(1)} %pad_clamp_fusion.4), kind=kCustom, calls=%fused_computation.clone.clone.1 | custom fusion | bytes 4194816 | tf_op jit(solution)/shard_map/while/body/jit(_take)/gather | solution.py:49
  52.4 3.0 %gather_fusion = bf16[128,128,64]{2,1,0:T(8,128)(2,1)} fusion(bf16[32,128,64]{2,1,0:T(8,128)(2,1)S(1)} %get-tuple-element.233, s32[1024]{0:T(1024)S(1)} %pad_clamp_fusion.4), kind=kCustom, calls=%fused_computation.1.clone.clone.1 | custom fusion | bytes 4194816 | tf_op jit(solution)/shard_map/while/body/jit(_take)/gather | solution.py:50
  55.4 10.0 %fusion.51 = bf16[128,128,64]{1,2,0:T(8,128)(2,1)} fusion(bf16[128,128,64]{2,1,0:T(8,128)(2,1)} %gather_fusion, f32[128,128]{1,0:T(8,128)S(1)} %multiply_exponential_fusion.2, f32[128]{0:T(128)S(1)} %fusion.50, pred[128]{0:T(512)(128)(4,1)S(1)} %get-tuple-element.193, bf16[128,128,64]{2,1,0:T(8,128)(2,1)} %gather_fusion.1, ...), kind=kOutput, calls=%fused_computation.7.clone.1 | convolution fusion | flops 546308096 | bytes 8454912 | tf_op jit(solution)/shard_map/while/body/pij,pjk->pik/dot_general | solution.py:58
  65.4 2.8 %fusion.52 = f32[16,128,64]{1,0,2:T(8,128)S(1)} fusion(f32[16,128,64]{1,0,2:T(8,128)S(1)} %get-tuple-element.211, bf16[128,128,64]{1,2,0:T(8,128)(2,1)} %fusion.51, s32[128]{0:T(128)S(1)} %get-tuple-element.194), kind=kOutput, calls=%fused_computation.20.clone.1 | convolution fusion | flops 33687552 | bytes 3146240 | tf_op jit(solution)/shard_map/while/body/pr,pik->rik/dot_general | solution.py:60
  68.3 1.4 fusion.50
  70.6 3.0 %gather_fusion.2 = bf16[128,128,64]{2,1,0:T(8,128)(2,1)} fusion(bf16[16,128,64]{2,1,0:T(8,128)(2,1)S(1)} %get-tuple-element.228, s32[1024]{0:T(1024)S(1)} %pad_clamp_fusion.5), kind=kCustom, calls=%fused_computation.2.clone.clone.1 | custom fusion | bytes 4194816 | tf_op jit(solution)/shard_map/while/body/jit(_take)/gather | solution.py:48
  73.6 3.1 %gather_fusion.1 = bf16[128,128,64]{2,1,0:T(8,128)(2,1)} fusion(bf16[32,128,64]{2,1,0:T(8,128)(2,1)S(1)} %get-tuple-element.230, s32[1024]{0:T(1024)S(1)} %pad_clamp_fusion.4), kind=kCustom, calls=%fused_computation.clone.clone.1 | custom fusion | bytes 4194816 | tf_op jit(solution)/shard_map/while/body/jit(_take)/gather | solution.py:49
  76.6 3.0 %gather_fusion = bf16[128,128,64]{2,1,0:T(8,128)(2,1)} fusion(bf16[32,128,64]{2,1,0:T(8,128)(2,1)S(1)} %get-tuple-element.233, s32[1024]{0:T(1024)S(1)} %pad_clamp_fusion.4), kind=kCustom, calls=%fused_computation.1.clone.clone.1 | custom fusion | bytes 4194816 | tf_op jit(solution)/shard_map/while/body/jit(_take)/gather | solution.py:50
  79.7 10.0 %fusion.51 = bf16[128,128,64]{1,2,0:T(8,128)(2,1)} fusion(bf16[128,128,64]{2,1,0:T(8,128)(2,1)} %gather_fusion, f32[128,128]{1,0:T(8,128)S(1)} %multiply_exponential_fusion.2, f32[128]{0:T(128)S(1)} %fusion.50, pred[128]{0:T(512)(128)(4,1)S(1)} %get-tuple-element.193, bf16[128,128,64]{2,1,0:T(8,128)(2,1)} %gather_fusion.1, ...), kind=kOutput, calls=%fused_computation.7.clone.1 | convolution fusion | flops 546308096 | bytes 8454912 | tf_op jit(solution)/shard_map/while/body/pij,pjk->pik/dot_general | solution.py:58
  89.7 2.8 %fusion.52 = f32[16,128,64]{1,0,2:T(8,128)S(1)} fusion(f32[16,128,64]{1,0,2:T(8,128)S(1)} %get-tuple-element.211, bf16[128,128,64]{1,2,0:T(8,128)(2,1)} %fusion.51, s32[128]{0:T(128)S(1)} %get-tuple-element.194), kind=kOutput, calls=%fused_computation.20.clone.1 | convolution fusion | flops 33687552 | bytes 3146240 | tf_op jit(solution)/shard_map/while/body/pr,pik->rik/dot_general | solution.py:60
  92.5 1.4 fusion.50
  94.8 3.0 %gather_fusion.2 = bf16[128,128,64]{2,1,0:T(8,128)(2,1)} fusion(bf16[16,128,64]{2,1,0:T(8,128)(2,1)S(1)} %get-tuple-element.228, s32[1024]{0:T(1024)S(1)} %pad_clamp_fusion.5), kind=kCustom, calls=%fused_computation.2.clone.clone.1 | custom fusion | bytes 4194816 | tf_op jit(solution)/shard_map/while/body/jit(_take)/gather | solution.py:48
  97.8 3.1 %gather_fusion.1 = bf16[128,128,64]{2,1,0:T(8,128)(2,1)} fusion(bf16[32,128,64]{2,1,0:T(8,128)(2,1)S(1)} %get-tuple-element.230, s32[1024]{0:T(1024)S(1)} %pad_clamp_fusion.4), kind=kCustom, calls=%fused_computation.clone.clone.1 | custom fusion | bytes 4194816 | tf_op jit(solution)/shard_map/while/body/jit(_take)/gather | solution.py:49
  100.9 3.0 %gather_fusion = bf16[128,128,64]{2,1,0:T(8,128)(2,1)} fusion(bf16[32,128,64]{2,1,0:T(8,128)(2,1)S(1)} %get-tuple-element.233, s32[1024]{0:T(1024)S(1)} %pad_clamp_fusion.4), kind=kCustom, calls=%fused_computation.1.clone.clone.1 | custom fusion | bytes 4194816 | tf_op jit(solution)/shard_map/while/body/jit(_take)/gather | solution.py:50
  103.9 10.0 %fusion.51 = bf16[128,128,64]{1,2,0:T(8,128)(2,1)} fusion(bf16[128,128,64]{2,1,0:T(8,128)(2,1)} %gather_fusion, f32[128,128]{1,0:T(8,128)S(1)} %multiply_exponential_fusion.2, f32[128]{0:T(128)S(1)} %fusion.50, pred[128]{0:T(512)(128)(4,1)S(1)} %get-tuple-element.193, bf16[128,128,64]{2,1,0:T(8,128)(2,1)} %gather_fusion.1, ...), kind=kOutput, calls=%fused_computation.7.clone.1 | convolution fusion | flops 546308096 | bytes 8454912 | tf_op jit(solution)/shard_map/while/body/pij,pjk->pik/dot_general | solution.py:58
  113.9 2.8 %fusion.52 = f32[16,128,64]{1,0,2:T(8,128)S(1)} fusion(f32[16,128,64]{1,0,2:T(8,128)S(1)} %get-tuple-element.211, bf16[128,128,64]{1,2,0:T(8,128)(2,1)} %fusion.51, s32[128]{0:T(128)S(1)} %get-tuple-element.194), kind=kOutput, calls=%fused_computation.20.clone.1 | convolution fusion | flops 33687552 | bytes 3146240 | tf_op jit(solution)/shard_map/while/body/pr,pik->rik/dot_general | solution.py:60
  116.7 1.0 copy.17
  117.7 45.7 %reduce-scatter.2.cloned.1.call-done = f32[512,64]{0,1:T(8,128)} async-done(((f32[2048,64]{0,1:T(8,128)}), f32[512,64]{0,1:T(8,128)}) %reduce-scatter.2.cloned.1.call-update) | async-done | bytes 131088 | tf_op jit(solution)/shard_map/reduce_scatter | solution.py:65
  (21 shorter events, 3.8 us)
Async XLA Ops:
  6.5 156.8 %reduce-scatter.2.cloned.1.call-start = ((), (), s32[]{:S(2)}) async-start(), calls=%async_computation.1 | async-start | bytes 655360 | tf_op jit(solution)/shard_map/reduce_scatter | solution.py:65
Sparse Core Ops, SparseCore 0:
  117.8 45.5 reduce-scatter.1
where the time goes:
time: 171 us; the launch traced here: 170 us
  waiting for transfers between devices  45.7 us (27%)
  matrix products  38.5 us (23%)
  blocking collectives  35.5 us (21%)
  local copies, waits for them, and re-layouts  29.6 us (17%)
  between operations  14.1 us (8%)
  other arithmetic  6.71 us (4%)
    reduce_scatter x1, waiting for transfers between devices, local(): lax.psum_scatter(partial_rows, 'cols', scatter_dimension=0, tiled=True)  45.7 us
    dot_general x3, matrix products, one_group(): jnp.einsum('pij,pjk->pik', tapered, innov, preferred_element_type=jnp.flo...  30 us
    all_gather x1, blocking collectives, local(): row_anom = lax.all_gather(anomalies, 'cols', axis=0, tiled=True)  15.8 us
    all_gather x1, blocking collectives, local(): lax.all_gather(anomalies, 'rows', axis=0, tiled=True)  10.1 us
    all_gather x1, blocking collectives, local(): lax.all_gather(innovations, 'rows', axis=0, tiled=True)  9.55 us
    gather x3, local copies, waits for them, and re-layouts, one_group(): right = jnp.take(col_blocks, col_local, axis=0)  9.17 us
    gather x3, local copies, waits for them, and re-layouts, one_group(): left = jnp.take(row_blocks, local_rows, axis=0)  9.12 us
    gather x3, local copies, waits for them, and re-layouts, one_group(): innov = jnp.take(innov_blocks, col_local, axis=0)  9.05 us
  transfers between devices with their start and end apart: 1, of which 1 were waited for; matrix products, arithmetic and copies ran while one was open for 0% of the time, Pallas kernels for 0%

commit v1 on v0

v1 whole, which is shorter than its diff:
```python
import jax
import jax.numpy as jnp
from jax import lax
from jax.experimental import pallas as pl
from jax.experimental.pallas import tpu as pltpu
from jax.sharding import PartitionSpec as P

BLK = 128
TAPER_CELLS = 8
DIST_SCALE = 4.0
DMAX = 8
HALF = 256

F32 = jnp.float32
BF16 = jnp.bfloat16
VMEM = pl.BlockSpec(memory_space=pltpu.VMEM)
SMEM = pl.BlockSpec(memory_space=pltpu.SMEM)


def table_kernel(per_dev, rows_ref, cols_ref, dist_ref, count_ref, table_ref):
    slots = rows_ref.shape[1]
    row_blocks, col_blocks = table_ref.shape
    row_flip = lax.axis_index("cols") * per_dev
    col_flip = lax.axis_index("rows") * per_dev
    live = lax.broadcasted_iota(jnp.int32, (1, slots), 1) < count_ref[0, 0]
    code = jnp.where(live, dist_ref[...] + 1, 0).astype(F32)
    row_place = lax.broadcasted_iota(jnp.int32, (row_blocks, slots), 0)
    col_place = lax.broadcasted_iota(jnp.int32, (col_blocks, slots), 0)
    left = jnp.where(row_place == (rows_ref[...] ^ row_flip), code, 0.0).astype(BF16)
    right = jnp.where(col_place == (cols_ref[...] ^ col_flip), 1.0, 0.0).astype(BF16)
    table = lax.dot_general(left, right, (((1,), (1,)), ((), ())), preferred_element_type=F32)
    table_ref[...] = table.astype(jnp.int32)


def pair_table(pair_rows, pair_cols, pair_dist, pair_counts, row_blocks, col_blocks, per_dev):
    def kernel(*refs):
        table_kernel(per_dev, *refs)

    return pl.pallas_call(
        kernel,
        out_shape=jax.ShapeDtypeStruct((row_blocks, col_blocks), jnp.int32),
        in_specs=[VMEM, VMEM, VMEM, SMEM],
        out_specs=VMEM,
        name="pair_table",
    )(pair_rows, pair_cols, pair_dist, pair_counts)


def increment_rows(table, first, row_part, col_parts, out_dtype):
    members, cells = row_part.shape
    columns = col_parts[0].shape[0] - members
    blocks = cells // BLK
    halves = cells // HALF
    per_half = HALF // BLK

    def kernel(table_ref, row_ref, *refs):
        col_refs, out_ref, taper_ref = refs[:-2], refs[-2], refs[-1]
        gap = lax.broadcasted_iota(jnp.int32, (BLK, BLK), 0) - lax.broadcasted_iota(jnp.int32, (BLK, BLK), 1)
        base = jnp.exp(-jnp.abs(gap).astype(F32) / TAPER_CELLS) * (1.0 / (members - 1))
        taper_ref[0] = jnp.zeros((BLK, BLK), F32)
        for dist in range(DMAX):
            taper_ref[dist + 1] = base * jnp.exp(jnp.full((1, 1), -dist / DIST_SCALE, F32))
        left = row_ref[...].T
        total = jnp.zeros((cells, columns), F32)
        for part, col_ref in enumerate(col_refs):
            for half in range(halves):
                span = pl.ds(half * HALF, HALF)
                right = col_ref[pl.ds(0, members), span]
                innov = col_ref[pl.ds(members, columns), span]
                products = jnp.dot(left, right, preferred_element_type=F32)
                first_col = part * blocks + half * per_half
                tapered = jnp.concatenate(
                    [
                        jnp.concatenate(
                            [
                                products[a * BLK : (a + 1) * BLK, q * BLK : (q + 1) * BLK]
                                * taper_ref[table_ref[first + a, first_col + q]]
                                for q in range(per_half)
                            ],
                            axis=1,
                        ).astype(BF16)
                        for a in range(blocks)
                    ],
                    axis=0,
                )
                total = total + lax.dot_general(
                    tapered, innov, (((1,), (1,)), ((), ())), preferred_element_type=F32
                )
        out_ref[...] = total.T.astype(out_dtype)

    count = len(col_parts)
    pairs = blocks * blocks * count
    return pl.pallas_call(
        kernel,
        out_shape=jax.ShapeDtypeStruct((columns, cells), out_dtype),
        in_specs=[SMEM] + [VMEM] * (1 + count),
        out_specs=VMEM,
        scratch_shapes=[pltpu.VMEM((DMAX + 1, BLK, BLK), F32)],
        cost_estimate=pl.CostEstimate(
            flops=4 * pairs * BLK * BLK * members,
            bytes_accessed=count * (members + columns) * cells * 2,
            transcendentals=BLK * BLK,
        ),
        name="increment_rows",
    )(table, row_part, *col_parts)


def swap(x, axis, size, flip):
    return lax.ppermute(x, axis, [(i, i ^ flip) for i in range(size)])


def solution(mesh):
    n_rows, n_cols = mesh.shape["rows"], mesh.shape["cols"]

    def local(anomalies, innovations, pair_rows, pair_cols, pair_dist, pair_counts):
        per_dev = anomalies.shape[0] // BLK
        anom, innov = anomalies.T, innovations.T
        packed = jnp.concatenate([anom, innov], axis=0)
        table = pair_table(
            pair_rows, pair_cols, pair_dist, pair_counts, n_cols * per_dev, n_rows * per_dev, per_dev
        )
        col_parts = [None] * n_rows
        for flip in range(0, n_rows, 2):
            col_parts[flip] = packed if flip == 0 else swap(packed, "rows", n_rows, flip)
        for flip in range(0, n_rows, 2):
            col_parts[flip + 1] = swap(col_parts[flip], "rows", n_rows, 1)
        row_parts = [anom if flip == 0 else swap(anom, "cols", n_cols, flip) for flip in range(n_cols)]
        received = []
        for flip in range(n_cols - 1, 0, -1):
            part = increment_rows(table, flip * per_dev, row_parts[flip], col_parts, BF16)
            received.append(swap(part, "cols", n_cols, flip))
        total = increment_rows(table, 0, row_parts[0], col_parts, F32)
        for part in received:
            total = total + part.astype(F32)
        return total.T

    spread = P(("rows", "cols"), None)
    pairs = P("rows", "cols")
    return jax.shard_map(
        local,
        mesh=mesh,
        in_specs=(spread, spread, pairs, pairs, pairs, pairs),
        out_specs=spread,
        check_vma=False,
    )
```

time: 171 us -> 51.2 us (0.30)
  matrix products: 38.5 us -> 0 us
  waiting for transfers between devices: 45.7 us -> 8.35 us
  blocking collectives: 35.5 us -> 0 us
  local copies, waits for them, and re-layouts: 29.6 us -> 2.56 us
  Pallas kernels: 0 us -> 19.4 us
  starting transfers between devices: 0.01 us -> 17.3 us
  between operations: 14.1 us -> 0.76 us
  other arithmetic: 6.71 us -> 2.51 us
    reduce_scatter x1 -> x0, waiting for transfers between devices: 45.7 us -> none  [local(): lax.psum_scatter(partial_rows, 'cols', scatter_dimension=0, tiled=True)]
    dot_general x6 -> x0, matrix products: 38.5 us -> none  [the longest x3 30 us: one_group(): jnp.einsum('pij,pjk->pik', tapered, innov, preferred_element_type=jnp.flo...]
    all_gather x3 -> x0, blocking collectives: 35.5 us -> none  [the longest x1 15.8 us: local(): row_anom = lax.all_gather(anomalies, 'cols', axis=0, tiled=True)]
    gather x9 -> x0, local copies, waits for them, and re-layouts: 27.3 us -> none  [the longest x3 9.17 us: one_group(): right = jnp.take(col_blocks, col_local, axis=0)]
    pallas_call x0 -> x5, Pallas kernels: none -> 19.4 us  [the longest x4 18 us: increment_rows(): pl.pallas_call(kernel, out_shape=jax.ShapeDtypeStruct((columns, cells), o...]
    ppermute x0 -> x13, starting transfers between devices: none -> 17.3 us  [swap(): return lax.ppermute(x, axis, [(i, i ^ flip) for i in range(size)])]
    ppermute x0 -> x13, waiting for transfers between devices: none -> 8.35 us  [swap(): return lax.ppermute(x, axis, [(i, i ^ flip) for i in range(size)])]
    mul x3 -> x0, other arithmetic: 4.23 us -> none  [one_group(): products * (1.0 / (M - 1)) * block_weight[:, None, None] * kernel]
  transfers between devices with their start and end apart: 1 -> 13, of which waited for: 1 -> 4; matrix products, arithmetic and copies ran while one was open for 0% -> 0% of each run, Pallas kernels for 0% -> 38%
where the time goes in v1:
time: 51.2 us; the launch traced here: 50.9 us
  Pallas kernels  19.4 us (38%)
  starting transfers between devices  17.3 us (34%)
  waiting for transfers between devices  8.35 us (16%)
  local copies, waits for them, and re-layouts  2.56 us (5%)
  other arithmetic  2.51 us (5%)
  between operations  0.76 us (1%)
    pallas_call x4, Pallas kernels, increment_rows(): pl.pallas_call(kernel, out_shape=jax.ShapeDtypeStruct((columns, cells), o...  18 us
    ppermute x13, starting transfers between devices, swap(): return lax.ppermute(x, axis, [(i, i ^ flip) for i in range(size)])  17.3 us
    ppermute x13, waiting for transfers between devices, swap(): return lax.ppermute(x, axis, [(i, i ^ flip) for i in range(size)])  8.35 us
    unnamed x24, local copies, waits for them, and re-layouts  2.56 us
    transpose x1, other arithmetic, local(): return total.T  1.59 us
    pallas_call x1, Pallas kernels, pair_table(): pl.pallas_call(kernel, out_shape=jax.ShapeDtypeStruct((row_blocks, col_bl...  1.45 us
  transfers between devices with their start and end apart: 13, of which 4 were waited for; matrix products, arithmetic and copies ran while one was open for 0% of the time, Pallas kernels for 38%

profile of v1, /device:TPU:0, one launch (start us, length us, event | category | flops | bytes accessed | tf_op | source)
XLA Modules:
  0.0 50.9 jit_solution(11403755846809791114)
XLA Ops:
  0.0 0.9 %pad_maximum_fusion.refs_0_ = bf16[128,512]{1,0:T(8,128)(2,1)S(1)} fusion(bf16[64,512]{1,0:T(8,128)(2,1)} %bitcast.4, bf16[64,512]{1,0:T(8,128)(2,1)} %bitcast.5), kind=kLoop, calls=%fused_computation | loop fusion | flops 262144 | bytes 262144 | tf_op jit(solution)/shard_map/concatenate | solution.py:117
  0.9 4.0 %collective-permute-start.5 = (bf16[128,512]{1,0:T(8,128)(2,1)S(1)}, bf16[128,512]{1,0:T(8,128)(2,1)S(1)}, u32[]{:S(2)}, u32[]{:S(2)}) collective-permute-start(bf16[128,512]{1,0:T(8,128)(2,1)S(1)} %pad_maximum_fusion.refs_0_), channel_id=1, source_target_pairs={{0,24},{4,28},{8,16},{12,20},{16,8},{20,12},{24,0},{28,4},{1,25},{... | collective-permute-start | bytes 393224 | tf_op jit(solution)/shard_map/ppermute | solution.py:108
  4.9 0.5 collective-permute-start.3
  5.5 3.3 %collective-permute-done.5.refs_6_ = bf16[128,512]{1,0:T(8,128)(2,1)S(1)} collective-permute-done((bf16[128,512]{1,0:T(8,128)(2,1)S(1)}, bf16[128,512]{1,0:T(8,128)(2,1)S(1)}, u32[]{:S(2)}, u32[]{:S(2)}) %collective-permute-start.5) | collective-permute-done | bytes 131104 | tf_op jit(solution)/shard_map/ppermute | solution.py:108
  8.8 2.4 %collective-permute-done.3.refs_4_ = bf16[128,512]{1,0:T(8,128)(2,1)S(1)} collective-permute-done((bf16[128,512]{1,0:T(8,128)(2,1)S(1)}, bf16[128,512]{1,0:T(8,128)(2,1)S(1)}, u32[]{:S(2)}, u32[]{:S(2)}) %collective-permute-start.3) | collective-permute-done | bytes 131104 | tf_op jit(solution)/shard_map/ppermute | solution.py:108
  11.2 0.2 collective-permute-done.1.refs_2_
  11.5 0.3 collective-permute-start.2
  11.7 3.8 %collective-permute-start.7 = (bf16[64,512]{1,0:T(8,128)(2,1)S(1)}, bf16[64,512]{1,0:T(8,128)(2,1)S(1)}, u32[]{:S(2)}, u32[]{:S(2)}) collective-permute-start(bf16[64,512]{1,0:T(8,128)(2,1)S(1)} %bitcast.7), channel_id=1, source_target_pairs={{0,3},{1,2},{2,1},{3,0},{4,7},{5,6},{6,5},{7,4},{8,11},{9,10},{10,... | collective-permute-start | bytes 196616 | tf_op jit(solution)/shard_map/ppermute | solution.py:108
  15.5 2.4 %collective-permute-done.7.row_ref = bf16[64,512]{1,0:T(8,128)(2,1)S(1)} collective-permute-done((bf16[64,512]{1,0:T(8,128)(2,1)S(1)}, bf16[64,512]{1,0:T(8,128)(2,1)S(1)}, u32[]{:S(2)}, u32[]{:S(2)}) %collective-permute-start.7) | collective-permute-done | bytes 65568 | tf_op jit(solution)/shard_map/ppermute | solution.py:108
  18.0 0.8 %collective-permute-start.9 = (bf16[64,512]{1,0:T(8,128)(2,1)S(1)}, bf16[64,512]{1,0:T(8,128)(2,1)S(1)}, u32[]{:S(2)}, u32[]{:S(2)}) collective-permute-start(bf16[64,512]{1,0:T(8,128)(2,1)S(1)} %bitcast.8), channel_id=1, source_target_pairs={{0,2},{1,3},{2,0},{3,1},{4,6},{5,7},{6,4},{7,5},{8,10},{9,11},{10,... | collective-permute-start | bytes 196616 | tf_op jit(solution)/shard_map/ppermute | solution.py:108
  19.4 1.4 %pair_table.1.table_ref = s32[16,32]{1,0:T(8,128)} custom-call(s32[1,512]{1,0:T(1,128)} %refs_0_.1, s32[1,512]{1,0:T(1,128)} %refs_1_.1, s32[1,512]{1,0:T(1,128)} %refs_2_.1, s32[1,1]{1,0:T(1,128)S(6)} %copy.7.refs_3_), custom_call_target="tpu_custom_call" | custom-call | tf_op jit(solution)/shard_map/pair_table/pallas_call | solution.py:39
  20.9 3.4 %collective-permute-start.11 = (bf16[64,512]{1,0:T(8,128)(2,1)S(1)}, bf16[64,512]{1,0:T(8,128)(2,1)S(1)}, u32[]{:S(2)}, u32[]{:S(2)}) collective-permute-start(bf16[64,512]{1,0:T(8,128)(2,1)S(1)} %bitcast.9), channel_id=1, source_target_pairs={{0,1},{1,0},{2,3},{3,2},{4,5},{5,4},{6,7},{7,6},{8,9},{9,8},{10,11... | collective-permute-start | bytes 196616 | tf_op jit(solution)/shard_map/ppermute | solution.py:108
  24.3 0.6 %copy-done.6 = bf16[128,512]{1,0:T(8,128)(2,1)} copy-done((bf16[128,512]{1,0:T(8,128)(2,1)}, bf16[128,512]{1,0:T(8,128)(2,1)S(1)}, u32[]{:S(2)}) %copy-start.6) | copy-done | bytes 131096
  25.0 0.7 %copy-done.8 = bf16[128,512]{1,0:T(8,128)(2,1)} copy-done((bf16[128,512]{1,0:T(8,128)(2,1)}, bf16[128,512]{1,0:T(8,128)(2,1)S(1)}, u32[]{:S(2)}) %copy-start.8) | copy-done | bytes 131096
  25.6 4.5 %increment_rows.5 = bf16[64,512]{1,0:T(8,128)(2,1)} custom-call(s32[16,32]{1,0:T(8,128)} %pair_table.1.table_ref, bf16[64,512]{1,0:T(8,128)(2,1)} %copy-done.11, bf16[128,512]{1,0:T(8,128)(2,1)} %copy-done, bf16[128,512]{1,0:T(8,128)(2,1)} %copy-done.5, bf16[128,512]{1,0:T(8,128)(2,1)} %copy-done.4, bf16[128,512]{1,0:T(8,128)(2,1)} %copy-done.8, ...), custom_call_target="tpu_custom_call" | custom-call | flops 536870912 | bytes 1048576 | tf_op jit(solution)/shard_map/increment_rows/pallas_call | solution.py:92
  30.1 0.2 collective-permute-start.8
  30.3 0.6 %copy-done.9 = bf16[64,512]{1,0:T(8,128)(2,1)} copy-done((bf16[64,512]{1,0:T(8,128)(2,1)}, bf16[64,512]{1,0:T(8,128)(2,1)S(1)}, u32[]{:S(2)}) %copy-start.9) | copy-done | bytes 65560
  30.9 4.5 %increment_rows.6 = bf16[64,512]{1,0:T(8,128)(2,1)} custom-call(s32[16,32]{1,0:T(8,128)} %pair_table.1.table_ref, bf16[64,512]{1,0:T(8,128)(2,1)} %copy-done.9, bf16[128,512]{1,0:T(8,128)(2,1)} %copy-done, bf16[128,512]{1,0:T(8,128)(2,1)} %copy-done.5, bf16[128,512]{1,0:T(8,128)(2,1)} %copy-done.4, bf16[128,512]{1,0:T(8,128)(2,1)} %copy-done.8, ...), custom_call_target="tpu_custom_call" | custom-call | flops 536870912 | bytes 1048576 | tf_op jit(solution)/shard_map/increment_rows/pallas_call | solution.py:92
  35.4 1.3 %collective-permute-start.10 = (bf16[64,512]{1,0:T(8,128)(2,1)}, bf16[64,512]{1,0:T(8,128)(2,1)S(1)}, u32[]{:S(2)}, u32[]{:S(2)}) collective-permute-start(bf16[64,512]{1,0:T(8,128)(2,1)} %increment_rows.6), channel_id=1, source_target_pairs={{0,2},{1,3},{2,0},{3,1},{4,6},{5,7},{6,4},{7,5},{8,10},{9,11},{10,... | collective-permute-start | bytes 196616 | tf_op jit(solution)/shard_map/ppermute | solution.py:108
  36.7 0.6 %copy-done.10 = bf16[64,512]{1,0:T(8,128)(2,1)} copy-done((bf16[64,512]{1,0:T(8,128)(2,1)}, bf16[64,512]{1,0:T(8,128)(2,1)S(1)}, u32[]{:S(2)}) %copy-start.10) | copy-done | bytes 65560
  37.4 4.5 %increment_rows.7 = bf16[64,512]{1,0:T(8,128)(2,1)} custom-call(s32[16,32]{1,0:T(8,128)} %pair_table.1.table_ref, bf16[64,512]{1,0:T(8,128)(2,1)} %copy-done.10, bf16[128,512]{1,0:T(8,128)(2,1)} %copy-done, bf16[128,512]{1,0:T(8,128)(2,1)} %copy-done.5, bf16[128,512]{1,0:T(8,128)(2,1)} %copy-done.4, bf16[128,512]{1,0:T(8,128)(2,1)} %copy-done.8, ...), custom_call_target="tpu_custom_call" | custom-call | flops 536870912 | bytes 1048576 | tf_op jit(solution)/shard_map/increment_rows/pallas_call | solution.py:92
  41.9 2.9 %collective-permute-start.12 = (bf16[64,512]{1,0:T(8,128)(2,1)}, bf16[64,512]{1,0:T(8,128)(2,1)S(1)}, u32[]{:S(2)}, u32[]{:S(2)}) collective-permute-start(bf16[64,512]{1,0:T(8,128)(2,1)} %increment_rows.7), channel_id=1, source_target_pairs={{0,1},{1,0},{2,3},{3,2},{4,5},{5,4},{6,7},{7,6},{8,9},{9,8},{10,11... | collective-permute-start | bytes 196616 | tf_op jit(solution)/shard_map/ppermute | solution.py:108
  44.7 4.5 %increment_rows.4 = f32[64,512]{1,0:T(8,128)} custom-call(s32[16,32]{1,0:T(8,128)} %pair_table.1.table_ref, bf16[64,512]{1,0:T(8,128)(2,1)} %bitcast.6, bf16[128,512]{1,0:T(8,128)(2,1)} %copy-done, bf16[128,512]{1,0:T(8,128)(2,1)} %copy-done.5, bf16[128,512]{1,0:T(8,128)(2,1)} %copy-done.4, bf16[128,512]{1,0:T(8,128)(2,1)} %copy-done.8, ...), custom_call_target="tpu_custom_call" | custom-call | flops 536870912 | bytes 1048576 | tf_op jit(solution)/shard_map/increment_rows/pallas_call | solution.py:92
  49.3 1.6 %add_bitcast_fusion = f32[512,64]{0,1:T(8,128)} fusion(bf16[64,512]{1,0:T(8,128)(2,1)S(1)} %collective-permute-done.12, bf16[64,512]{1,0:T(8,128)(2,1)S(1)} %collective-permute-done.10, f32[64,512]{1,0:T(8,128)} %increment_rows.4, bf16[64,512]{1,0:T(8,128)(2,1)S(1)} %collective-permute-done.8), kind=kLoop, calls=%fused_computation.1 | loop fusion | flops 196608 | bytes 458752 | tf_op jit(solution)/shard_map/transpose | solution.py:134
  (33 shorter events, 0.3 us)
Async XLA Ops:
  0.0 11.7 %copy-start.1 = (bf16[512,64]{0,1:T(8,128)(2,1)S(1)}, bf16[512,64]{0,1:T(8,128)(2,1)}, u32[]{:S(2)}) copy-start(bf16[512,64]{0,1:T(8,128)(2,1)} %param.6) | copy-start | bytes 196612
  0.9 23.4 %copy-start = (bf16[128,512]{1,0:T(8,128)(2,1)}, bf16[128,512]{1,0:T(8,128)(2,1)S(1)}, u32[]{:S(2)}) copy-start(bf16[128,512]{1,0:T(8,128)(2,1)S(1)} %pad_maximum_fusion.refs_0_) | copy-start | bytes 393220
  0.9 7.9 %collective-permute-start.5 = (bf16[128,512]{1,0:T(8,128)(2,1)S(1)}, bf16[128,512]{1,0:T(8,128)(2,1)S(1)}, u32[]{:S(2)}, u32[]{:S(2)}) collective-permute-start(bf16[128,512]{1,0:T(8,128)(2,1)S(1)} %pad_maximum_fusion.refs_0_), channel_id=1, source_target_pairs={{0,24},{4,28},{8,16},{12,20},{16,8},{20,12},{24,0},{28,4},{1,25},{... | collective-permute-start | bytes 393224 | tf_op jit(solution)/shard_map/ppermute | solution.py:108
  4.9 6.3 %collective-permute-start.3 = (bf16[128,512]{1,0:T(8,128)(2,1)S(1)}, bf16[128,512]{1,0:T(8,128)(2,1)S(1)}, u32[]{:S(2)}, u32[]{:S(2)}) collective-permute-start(bf16[128,512]{1,0:T(8,128)(2,1)S(1)} %pad_maximum_fusion.refs_0_), channel_id=1, source_target_pairs={{0,16},{4,20},{8,24},{12,28},{16,0},{20,4},{24,8},{28,12},{1,17},{... | collective-permute-start | bytes 393224 | tf_op jit(solution)/shard_map/ppermute | solution.py:108
  5.4 6.0 %collective-permute-start.1 = (bf16[128,512]{1,0:T(8,128)(2,1)S(1)}, bf16[128,512]{1,0:T(8,128)(2,1)S(1)}, u32[]{:S(2)}, u32[]{:S(2)}) collective-permute-start(bf16[128,512]{1,0:T(8,128)(2,1)S(1)} %pad_maximum_fusion.refs_0_), channel_id=1, source_target_pairs={{0,8},{4,12},{8,0},{12,4},{16,24},{20,28},{24,16},{28,20},{1,9},{5... | collective-permute-start | bytes 393224 | tf_op jit(solution)/shard_map/ppermute | solution.py:108
  5.5 15.3 %collective-permute-start = (bf16[128,512]{1,0:T(8,128)(2,1)S(1)}, bf16[128,512]{1,0:T(8,128)(2,1)S(1)}, u32[]{:S(2)}, u32[]{:S(2)}) collective-permute-start(bf16[128,512]{1,0:T(8,128)(2,1)S(1)} %pad_maximum_fusion.refs_0_), channel_id=1, source_target_pairs={{0,4},{4,0},{8,12},{12,8},{16,20},{20,16},{24,28},{28,24},{1,5},{5... | collective-permute-start | bytes 393224 | tf_op jit(solution)/shard_map/ppermute | solution.py:108
  8.8 15.5 %copy-start.2 = (bf16[128,512]{1,0:T(8,128)(2,1)}, bf16[128,512]{1,0:T(8,128)(2,1)S(1)}, u32[]{:S(2)}) copy-start(bf16[128,512]{1,0:T(8,128)(2,1)S(1)} %collective-permute-done.5.refs_6_) | copy-start | bytes 393220
  8.8 15.5 %collective-permute-start.6 = (bf16[128,512]{1,0:T(8,128)(2,1)S(1)}, bf16[128,512]{1,0:T(8,128)(2,1)S(1)}, u32[]{:S(2)}, u32[]{:S(2)}) collective-permute-start(bf16[128,512]{1,0:T(8,128)(2,1)S(1)} %collective-permute-done.5.refs_6_), channel_id=1, source_target_pairs={{0,4},{4,0},{8,12},{12,8},{16,20},{20,16},{24,28},{28,24},{1,5},{5... | collective-permute-start | bytes 393224 | tf_op jit(solution)/shard_map/ppermute | solution.py:108
  11.2 13.1 %copy-start.3 = (bf16[128,512]{1,0:T(8,128)(2,1)}, bf16[128,512]{1,0:T(8,128)(2,1)S(1)}, u32[]{:S(2)}) copy-start(bf16[128,512]{1,0:T(8,128)(2,1)S(1)} %collective-permute-done.3.refs_4_) | copy-start | bytes 393220
  11.2 13.1 %collective-permute-start.4 = (bf16[128,512]{1,0:T(8,128)(2,1)S(1)}, bf16[128,512]{1,0:T(8,128)(2,1)S(1)}, u32[]{:S(2)}, u32[]{:S(2)}) collective-permute-start(bf16[128,512]{1,0:T(8,128)(2,1)S(1)} %collective-permute-done.3.refs_4_), channel_id=1, source_target_pairs={{0,4},{4,0},{8,12},{12,8},{16,20},{20,16},{24,28},{28,24},{1,5},{5... | collective-permute-start | bytes 393224 | tf_op jit(solution)/shard_map/ppermute | solution.py:108
  11.5 12.9 %copy-start.4 = (bf16[128,512]{1,0:T(8,128)(2,1)}, bf16[128,512]{1,0:T(8,128)(2,1)S(1)}, u32[]{:S(2)}) copy-start(bf16[128,512]{1,0:T(8,128)(2,1)S(1)} %collective-permute-done.1.refs_2_) | copy-start | bytes 393220
  11.5 12.8 %collective-permute-start.2 = (bf16[128,512]{1,0:T(8,128)(2,1)S(1)}, bf16[128,512]{1,0:T(8,128)(2,1)S(1)}, u32[]{:S(2)}, u32[]{:S(2)}) collective-permute-start(bf16[128,512]{1,0:T(8,128)(2,1)S(1)} %collective-permute-done.1.refs_2_), channel_id=1, source_target_pairs={{0,4},{4,0},{8,12},{12,8},{16,20},{20,16},{24,28},{28,24},{1,5},{5... | collective-permute-start | bytes 393224 | tf_op jit(solution)/shard_map/ppermute | solution.py:108
  11.7 6.2 %collective-permute-start.7 = (bf16[64,512]{1,0:T(8,128)(2,1)S(1)}, bf16[64,512]{1,0:T(8,128)(2,1)S(1)}, u32[]{:S(2)}, u32[]{:S(2)}) collective-permute-start(bf16[64,512]{1,0:T(8,128)(2,1)S(1)} %bitcast.7), channel_id=1, source_target_pairs={{0,3},{1,2},{2,1},{3,0},{4,7},{5,6},{6,5},{7,4},{8,11},{9,10},{10,... | collective-permute-start | bytes 196616 | tf_op jit(solution)/shard_map/ppermute | solution.py:108
  18.0 6.4 %copy-start.11 = (bf16[64,512]{1,0:T(8,128)(2,1)}, bf16[64,512]{1,0:T(8,128)(2,1)S(1)}, u32[]{:S(2)}) copy-start(bf16[64,512]{1,0:T(8,128)(2,1)S(1)} %collective-permute-done.7.row_ref) | copy-start | bytes 196612
  18.0 12.4 %collective-permute-start.9 = (bf16[64,512]{1,0:T(8,128)(2,1)S(1)}, bf16[64,512]{1,0:T(8,128)(2,1)S(1)}, u32[]{:S(2)}, u32[]{:S(2)}) collective-permute-start(bf16[64,512]{1,0:T(8,128)(2,1)S(1)} %bitcast.8), channel_id=1, source_target_pairs={{0,2},{1,3},{2,0},{3,1},{4,6},{5,7},{6,4},{7,5},{8,10},{9,11},{10,... | collective-permute-start | bytes 196616 | tf_op jit(solution)/shard_map/ppermute | solution.py:108
  20.9 3.5 %copy-start.5 = (bf16[128,512]{1,0:T(8,128)(2,1)}, bf16[128,512]{1,0:T(8,128)(2,1)S(1)}, u32[]{:S(2)}) copy-start(bf16[128,512]{1,0:T(8,128)(2,1)S(1)} %collective-permute-done.refs_1_) | copy-start | bytes 393220
  20.9 15.9 %collective-permute-start.11 = (bf16[64,512]{1,0:T(8,128)(2,1)S(1)}, bf16[64,512]{1,0:T(8,128)(2,1)S(1)}, u32[]{:S(2)}, u32[]{:S(2)}) collective-permute-start(bf16[64,512]{1,0:T(8,128)(2,1)S(1)} %bitcast.9), channel_id=1, source_target_pairs={{0,1},{1,0},{2,3},{3,2},{4,5},{5,4},{6,7},{7,6},{8,9},{9,8},{10,11... | collective-permute-start | bytes 196616 | tf_op jit(solution)/shard_map/ppermute | solution.py:108
  24.3 0.7 %copy-start.6 = (bf16[128,512]{1,0:T(8,128)(2,1)}, bf16[128,512]{1,0:T(8,128)(2,1)S(1)}, u32[]{:S(2)}) copy-start(bf16[128,512]{1,0:T(8,128)(2,1)S(1)} %collective-permute-done.6.refs_7_) | copy-start | bytes 393220
  24.3 0.7 %copy-start.7 = (bf16[128,512]{1,0:T(8,128)(2,1)}, bf16[128,512]{1,0:T(8,128)(2,1)S(1)}, u32[]{:S(2)}) copy-start(bf16[128,512]{1,0:T(8,128)(2,1)S(1)} %collective-permute-done.4.refs_5_) | copy-start | bytes 393220
  25.0 0.7 %copy-start.8 = (bf16[128,512]{1,0:T(8,128)(2,1)}, bf16[128,512]{1,0:T(8,128)(2,1)S(1)}, u32[]{:S(2)}) copy-start(bf16[128,512]{1,0:T(8,128)(2,1)S(1)} %collective-permute-done.2.refs_3_) | copy-start | bytes 393220
  30.1 19.1 %collective-permute-start.8 = (bf16[64,512]{1,0:T(8,128)(2,1)}, bf16[64,512]{1,0:T(8,128)(2,1)S(1)}, u32[]{:S(2)}, u32[]{:S(2)}) collective-permute-start(bf16[64,512]{1,0:T(8,128)(2,1)} %increment_rows.5), channel_id=1, source_target_pairs={{0,3},{1,2},{2,1},{3,0},{4,7},{5,6},{6,5},{7,4},{8,11},{9,10},{10,... | collective-permute-start | bytes 196616 | tf_op jit(solution)/shard_map/ppermute | solution.py:108
  30.3 0.6 %copy-start.9 = (bf16[64,512]{1,0:T(8,128)(2,1)}, bf16[64,512]{1,0:T(8,128)(2,1)S(1)}, u32[]{:S(2)}) copy-start(bf16[64,512]{1,0:T(8,128)(2,1)S(1)} %collective-permute-done.9.row_ref) | copy-start | bytes 196612
  35.4 13.8 %collective-permute-start.10 = (bf16[64,512]{1,0:T(8,128)(2,1)}, bf16[64,512]{1,0:T(8,128)(2,1)S(1)}, u32[]{:S(2)}, u32[]{:S(2)}) collective-permute-start(bf16[64,512]{1,0:T(8,128)(2,1)} %increment_rows.6), channel_id=1, source_target_pairs={{0,2},{1,3},{2,0},{3,1},{4,6},{5,7},{6,4},{7,5},{8,10},{9,11},{10,... | collective-permute-start | bytes 196616 | tf_op jit(solution)/shard_map/ppermute | solution.py:108
  41.9 7.4 %collective-permute-start.12 = (bf16[64,512]{1,0:T(8,128)(2,1)}, bf16[64,512]{1,0:T(8,128)(2,1)S(1)}, u32[]{:S(2)}, u32[]{:S(2)}) collective-permute-start(bf16[64,512]{1,0:T(8,128)(2,1)} %increment_rows.7), channel_id=1, source_target_pairs={{0,1},{1,0},{2,3},{3,2},{4,5},{5,4},{6,7},{7,6},{8,9},{9,8},{10,11... | collective-permute-start | bytes 196616 | tf_op jit(solution)/shard_map/ppermute | solution.py:108
  (1 other events, 0.6 us)

commit v2 on v1

v2 whole, which is shorter than its diff:
```python
import jax
import jax.numpy as jnp
from jax import lax
from jax.experimental import pallas as pl
from jax.experimental.pallas import tpu as pltpu
from jax.sharding import PartitionSpec as P

BLK = 128
TAPER_CELLS = 8
DIST_SCALE = 4.0
DMAX = 8
HALF = 256

F32 = jnp.float32
BF16 = jnp.bfloat16
VMEM = pl.BlockSpec(memory_space=pltpu.VMEM)
SMEM = pl.BlockSpec(memory_space=pltpu.SMEM)


def pair_table(pair_rows, pair_cols, pair_dist, pair_counts, row_blocks, col_blocks, per_dev):
    def kernel(rows_ref, cols_ref, dist_ref, count_ref, table_ref):
        slots = rows_ref.shape[1]
        row_flip = lax.axis_index("cols") * per_dev
        col_flip = lax.axis_index("rows") * per_dev
        live = lax.broadcasted_iota(jnp.int32, (1, slots), 1) < count_ref[0, 0]
        code = jnp.where(live, dist_ref[...] + 1, 0).astype(F32)
        row_place = lax.broadcasted_iota(jnp.int32, (row_blocks, slots), 0)
        col_place = lax.broadcasted_iota(jnp.int32, (col_blocks, slots), 0)
        left = jnp.where(row_place == (rows_ref[...] ^ row_flip), code, 0.0).astype(BF16)
        right = jnp.where(col_place == (cols_ref[...] ^ col_flip), 1.0, 0.0).astype(BF16)
        table = lax.dot_general(left, right, (((1,), (1,)), ((), ())), preferred_element_type=F32)
        table_ref[...] = table.astype(jnp.int32)

    return pl.pallas_call(
        kernel,
        out_shape=jax.ShapeDtypeStruct((row_blocks, col_blocks), jnp.int32),
        in_specs=[VMEM, VMEM, VMEM, SMEM],
        out_specs=VMEM,
        name="pair_table",
    )(pair_rows, pair_cols, pair_dist, pair_counts)


def increment_rows(table, row_parts, col_parts, row_flips, col_flips, before, send):
    members, cells = row_parts[0].shape
    columns = col_parts[0].shape[0] - members
    blocks = cells // BLK
    halves = cells // HALF
    per_half = HALF // BLK
    n_row, n_col, n_before = len(row_parts), len(col_parts), len(before)

    def kernel(table_ref, *refs):
        refs = list(refs)
        row_refs, col_refs, before_refs, out_refs = (
            [refs.pop(0) for _ in range(n)] for n in (n_row, n_col, n_before, n_row)
        )
        taper_ref, left_ref, total_ref = refs
        gap = lax.broadcasted_iota(jnp.int32, (BLK, BLK), 0) - lax.broadcasted_iota(jnp.int32, (BLK, BLK), 1)
        base = jnp.exp(-jnp.abs(gap).astype(F32) / TAPER_CELLS) * (1.0 / (members - 1))
        weights = jnp.exp(lax.broadcasted_iota(jnp.int32, (1, BLK), 1).astype(F32) / -DIST_SCALE)
        taper_ref[0] = jnp.zeros((BLK, BLK), F32)
        for dist in range(DMAX):
            taper_ref[dist + 1] = base * weights[0:1, dist : dist + 1]
        for row in range(n_row):
            left_ref[...] = row_refs[row][...].T
            sum_ref = total_ref if send is not None else out_refs[row]
            for col in range(n_col):
                total = None
                for half in range(halves):
                    span = pl.ds(half * HALF, HALF)
                    right = col_refs[col][pl.ds(0, members), span]
                    innov = col_refs[col][pl.ds(members, columns), span]
                    products = jnp.dot(left_ref[...], right, preferred_element_type=F32)
                    first_row = row_flips[row] * blocks
                    first_col = col_flips[col] * blocks + half * per_half
                    tapered = jnp.concatenate(
                        [
                            jnp.concatenate(
                                [
                                    products[a * BLK : (a + 1) * BLK, q * BLK : (q + 1) * BLK]
                                    * taper_ref[table_ref[first_row + a, first_col + q]]
                                    for q in range(per_half)
                                ],
                                axis=1,
                            ).astype(BF16)
                            for a in range(blocks)
                        ],
                        axis=0,
                    )
                    applied = lax.dot_general(
                        tapered, innov, (((1,), (1,)), ((), ())), preferred_element_type=F32
                    )
                    total = applied if total is None else total + applied
                if col > 0:
                    total = total + sum_ref[...]
                elif n_before > 0:
                    total = total + before_refs[row][...]
                sum_ref[...] = total
            if send is not None:
                out_refs[row][...] = sum_ref[...].astype(send).T

    pairs = blocks * blocks * n_row * n_col
    out = (cells, columns) if send is None else (columns, cells)
    return pl.pallas_call(
        kernel,
        out_shape=[jax.ShapeDtypeStruct(out, F32 if send is None else send)] * n_row,
        in_specs=[SMEM] + [VMEM] * (n_row + n_col + n_before),
        out_specs=[VMEM] * n_row,
        scratch_shapes=[
            pltpu.VMEM((DMAX + 1, BLK, BLK), F32),
            pltpu.VMEM((cells, members), BF16),
            pltpu.VMEM((cells, columns), F32),
        ],
        compiler_params=pltpu.CompilerParams(vmem_limit_bytes=24 * 2**20),
        cost_estimate=pl.CostEstimate(
            flops=16 * pairs * BLK * BLK * members,
            bytes_accessed=n_col * (members + columns) * cells * 2,
            transcendentals=BLK * BLK,
        ),
        name="increment_rows",
    )(table, *row_parts, *col_parts, *before)


def add_up(own, received):
    def kernel(*refs):
        total = refs[0][...]
        for ref in refs[1:-1]:
            total = total + ref[...].astype(F32)
        refs[-1][...] = total

    return pl.pallas_call(
        kernel,
        out_shape=jax.ShapeDtypeStruct(own.shape, F32),
        in_specs=[VMEM] * (1 + len(received)),
        out_specs=VMEM,
        name="add_up",
    )(own, *received)


def swap(x, axis, size, flip):
    return lax.ppermute(x, axis, [(i, i ^ flip) for i in range(size)])


def solution(mesh):
    n_rows, n_cols = mesh.shape["rows"], mesh.shape["cols"]

    def local(anomalies, innovations, pair_rows, pair_cols, pair_dist, pair_counts):
        per_dev = anomalies.shape[0] // BLK
        anom, innov = anomalies.T, innovations.T
        packed = jnp.concatenate([anom, innov], axis=0)
        near = list(range(0, n_rows, 2))
        far = [flip + 1 for flip in near]
        near_parts = [packed] + [swap(packed, "rows", n_rows, flip) for flip in near[1:]]
        others = list(range(n_cols - 1, 0, -1))
        row_parts = [swap(anom, "cols", n_cols, flip) for flip in others]
        table = pair_table(
            pair_rows, pair_cols, pair_dist, pair_counts, n_cols * per_dev, n_rows * per_dev, per_dev
        )
        *near_parts, table = lax.optimization_barrier((*near_parts, *row_parts, table))
        near_parts, row_parts = near_parts[: len(near)], near_parts[len(near) :]
        far_parts = [swap(part, "rows", n_rows, 1) for part in near_parts]
        before = increment_rows(table, row_parts, near_parts, others, near, [], None)
        received = []
        for i, flip in enumerate(others):
            (part,) = increment_rows(table, [row_parts[i]], far_parts, [flip], far, [before[i]], BF16)
            received.append(swap(part, "cols", n_cols, flip))
        (own,) = increment_rows(table, [anom], near_parts + far_parts, [0], near + far, [], F32)
        return add_up(own, received).T

    spread = P(("rows", "cols"), None)
    pairs = P("rows", "cols")
    return jax.shard_map(
        local,
        mesh=mesh,
        in_specs=(spread, spread, pairs, pairs, pairs, pairs),
        out_specs=spread,
        check_vma=False,
    )
```

time: 51.2 us -> 38.9 us (0.76)
  waiting for transfers between devices: 8.35 us -> 3.12 us
  Pallas kernels: 19.4 us -> 16.6 us
  starting transfers between devices: 17.3 us -> 14.7 us
  other arithmetic: 2.51 us -> 0.92 us
    ppermute x13, waiting for transfers between devices: 8.35 us -> 3.12 us  [swap(): return lax.ppermute(x, axis, [(i, i ^ flip) for i in range(size)])]
    pallas_call x4 -> x6, Pallas kernels: 18 us -> 15.1 us  [the longest x5 13.5 us: increment_rows(): pl.pallas_call(kernel, out_shape=[jax.ShapeDtypeStruct(out, F32 if send i...]
    ppermute x13, starting transfers between devices: 17.3 us -> 14.7 us  [swap(): return lax.ppermute(x, axis, [(i, i ^ flip) for i in range(size)])]
    transpose x1 -> x0, other arithmetic: 1.59 us -> none  [local(): return total.T]
    unnamed x24 -> x12, local copies, waits for them, and re-layouts: 2.56 us -> 2.6 us
  transfers between devices with their start and end apart: 13 -> 13, of which waited for: 4 -> 2; matrix products, arithmetic and copies ran while one was open for 0% -> 2% of each run, Pallas kernels for 38% -> 33%
where the time goes in v2:
time: 38.9 us; the launch traced here: 38.6 us
  Pallas kernels  16.6 us (43%)
  starting transfers between devices  14.7 us (38%)
  waiting for transfers between devices  3.12 us (8%)
  local copies, waits for them, and re-layouts  2.6 us (7%)
  other arithmetic  0.92 us (2%)
  between operations  0.74 us (2%)
    ppermute x13, starting transfers between devices, swap(): return lax.ppermute(x, axis, [(i, i ^ flip) for i in range(size)])  14.7 us
    pallas_call x5, Pallas kernels, increment_rows(): pl.pallas_call(kernel, out_shape=[jax.ShapeDtypeStruct(out, F32 if send i...  13.5 us
    ppermute x13, waiting for transfers between devices, swap(): return lax.ppermute(x, axis, [(i, i ^ flip) for i in range(size)])  3.12 us
    unnamed x12, local copies, waits for them, and re-layouts  2.6 us
    pallas_call x1, Pallas kernels, add_up(): pl.pallas_call(kernel, out_shape=jax.ShapeDtypeStruct(own.shape, F32), in...  1.65 us
    pallas_call x1, Pallas kernels, pair_table(): pl.pallas_call(kernel, out_shape=jax.ShapeDtypeStruct((row_blocks, col_bl...  1.45 us
    concatenate x1, other arithmetic, local(): packed = jnp.concatenate([anom, innov], axis=0)  0.92 us
  transfers between devices with their start and end apart: 13, of which 2 were waited for; matrix products, arithmetic and copies ran while one was open for 2% of the time, Pallas kernels for 33%

profile of v2, /device:TPU:0, one launch (start us, length us, event | category | flops | bytes accessed | tf_op | source)
XLA Modules:
  0.0 38.6 jit_solution(11616401530944085376)
XLA Ops:
  0.0 5.0 %collective-permute-start.3 = (bf16[64,512]{1,0:T(8,128)(2,1)}, bf16[64,512]{1,0:T(8,128)(2,1)S(1)}, u32[]{:S(2)}, u32[]{:S(2)}) collective-permute-start(bf16[64,512]{1,0:T(8,128)(2,1)} %bitcast.3), channel_id=1, source_target_pairs={{0,3},{1,2},{2,1},{3,0},{4,7},{5,6},{6,5},{7,4},{8,11},{9,10},{10,... | collective-permute-start | bytes 196616 | tf_op jit(solution)/shard_map/ppermute | solution.py:140
  5.1 0.9 %pad_maximum_fusion.refs_1_.refs_3_ = bf16[128,512]{1,0:T(8,128)(2,1)S(1)} fusion(bf16[64,512]{1,0:T(8,128)(2,1)} %bitcast.8, bf16[64,512]{1,0:T(8,128)(2,1)} %bitcast.4), kind=kLoop, calls=%fused_computation | loop fusion | flops 262144 | bytes 262144 | tf_op jit(solution)/shard_map/concatenate | solution.py:149
  6.0 1.6 %collective-permute-start = (bf16[128,512]{1,0:T(8,128)(2,1)S(1)}, bf16[128,512]{1,0:T(8,128)(2,1)S(1)}, u32[]{:S(2)}, u32[]{:S(2)}) collective-permute-start(bf16[128,512]{1,0:T(8,128)(2,1)S(1)} %pad_maximum_fusion.refs_1_.refs_3_), channel_id=1, source_target_pairs={{0,8},{4,12},{8,0},{12,4},{16,24},{20,28},{24,16},{28,20},{1,9},{5... | collective-permute-start | bytes 393224 | tf_op jit(solution)/shard_map/ppermute | solution.py:140
  7.5 1.5 %collective-permute-start.1 = (bf16[128,512]{1,0:T(8,128)(2,1)S(1)}, bf16[128,512]{1,0:T(8,128)(2,1)S(1)}, u32[]{:S(2)}, u32[]{:S(2)}) collective-permute-start(bf16[128,512]{1,0:T(8,128)(2,1)S(1)} %pad_maximum_fusion.refs_1_.refs_3_), channel_id=1, source_target_pairs={{0,16},{4,20},{8,24},{12,28},{16,0},{20,4},{24,8},{28,12},{1,17},{... | collective-permute-start | bytes 393224 | tf_op jit(solution)/shard_map/ppermute | solution.py:140
  9.0 0.5 %collective-permute-start.2 = (bf16[128,512]{1,0:T(8,128)(2,1)S(1)}, bf16[128,512]{1,0:T(8,128)(2,1)S(1)}, u32[]{:S(2)}, u32[]{:S(2)}) collective-permute-start(bf16[128,512]{1,0:T(8,128)(2,1)S(1)} %pad_maximum_fusion.refs_1_.refs_3_), channel_id=1, source_target_pairs={{0,24},{4,28},{8,16},{12,20},{16,8},{20,12},{24,0},{28,4},{1,25},{... | collective-permute-start | bytes 393224 | tf_op jit(solution)/shard_map/ppermute | solution.py:140
  9.5 0.6 %collective-permute-start.5 = (bf16[64,512]{1,0:T(8,128)(2,1)S(1)}, bf16[64,512]{1,0:T(8,128)(2,1)S(1)}, u32[]{:S(2)}, u32[]{:S(2)}) collective-permute-start(bf16[64,512]{1,0:T(8,128)(2,1)S(1)} %bitcast.6), channel_id=1, source_target_pairs={{0,1},{1,0},{2,3},{3,2},{4,5},{5,4},{6,7},{7,6},{8,9},{9,8},{10,11... | collective-permute-start | bytes 196616 | tf_op jit(solution)/shard_map/ppermute | solution.py:140
  10.8 1.5 %pair_table.1.table_ref = s32[16,32]{1,0:T(8,128)} custom-call(s32[1,512]{1,0:T(1,128)} %rows_ref.1, s32[1,512]{1,0:T(1,128)} %cols_ref.1, s32[1,512]{1,0:T(1,128)} %dist_ref.1, s32[1,1]{1,0:T(1,128)S(6)} %copy.7.count_ref), custom_call_target="tpu_custom_call" | custom-call | tf_op jit(solution)/shard_map/pair_table/pallas_call | solution.py:34
  12.2 2.7 %collective-permute-done.4.refs_1_.refs_0_ = bf16[64,512]{1,0:T(8,128)(2,1)S(1)} collective-permute-done((bf16[64,512]{1,0:T(8,128)(2,1)S(1)}, bf16[64,512]{1,0:T(8,128)(2,1)S(1)}, u32[]{:S(2)}, u32[]{:S(2)}) %collective-permute-start.4) | collective-permute-done | bytes 65568 | tf_op jit(solution)/shard_map/ppermute | solution.py:140
  14.9 0.4 %collective-permute-done.1.refs_3_.refs_5_ = bf16[128,512]{1,0:T(8,128)(2,1)S(1)} collective-permute-done((bf16[128,512]{1,0:T(8,128)(2,1)S(1)}, bf16[128,512]{1,0:T(8,128)(2,1)S(1)}, u32[]{:S(2)}, u32[]{:S(2)}) %collective-permute-start.1) | collective-permute-done | bytes 131104 | tf_op jit(solution)/shard_map/ppermute | solution.py:140
  15.3 0.5 %collective-permute-start.7 = (bf16[128,512]{1,0:T(8,128)(2,1)S(1)}, bf16[128,512]{1,0:T(8,128)(2,1)S(1)}, u32[]{:S(2)}, u32[]{:S(2)}) collective-permute-start(bf16[128,512]{1,0:T(8,128)(2,1)S(1)} %collective-permute-done.refs_2_.refs_4_), channel_id=1, source_target_pairs={{0,4},{4,0},{8,12},{12,8},{16,20},{20,16},{24,28},{28,24},{1,5},{5... | collective-permute-start | bytes 393224 | tf_op jit(solution)/shard_map/ppermute | solution.py:140
  15.8 0.5 %collective-permute-start.9 = (bf16[128,512]{1,0:T(8,128)(2,1)S(1)}, bf16[128,512]{1,0:T(8,128)(2,1)S(1)}, u32[]{:S(2)}, u32[]{:S(2)}) collective-permute-start(bf16[128,512]{1,0:T(8,128)(2,1)S(1)} %collective-permute-done.2.refs_4_.refs_6_), channel_id=1, source_target_pairs={{0,4},{4,0},{8,12},{12,8},{16,20},{20,16},{24,28},{28,24},{1,5},{5... | collective-permute-start | bytes 393224 | tf_op jit(solution)/shard_map/ppermute | solution.py:140
  16.3 0.7 %copy-done.2 = s32[16,32]{1,0:T(8,128)S(1)} copy-done((s32[16,32]{1,0:T(8,128)S(1)}, s32[16,32]{1,0:T(8,128)}, u32[]{:S(2)}) %copy-start.2) | copy-done | bytes 2072
  17.0 4.2 %increment_rows.6 = (f32[512,64]{1,0:T(8,128)S(1)}, f32[512,64]{1,0:T(8,128)S(1)}, f32[512,64]{1,0:T(8,128)S(1)}) custom-call(s32[16,32]{1,0:T(8,128)S(1)} %copy-done.2, bf16[64,512]{1,0:T(8,128)(2,1)S(1)} %collective-permute-done.3.refs_0_, bf16[64,512]{1,0:T(8,128)(2,1)S(1)} %collective-permute-done.4.refs_1_.refs_0_, ...), custom_call_target="tpu_custom_call" | custom-call | flops 3221225472 | bytes 524288 | tf_op jit(solution)/shard_map/increment_rows/pallas_call | solution.py:103
  21.2 2.1 %increment_rows.9 = bf16[64,512]{1,0:T(8,128)(2,1)S(1)} custom-call(s32[16,32]{1,0:T(8,128)S(1)} %copy-done.2, bf16[64,512]{1,0:T(8,128)(2,1)S(1)} %collective-permute-done.5.refs_2_.refs_0_, bf16[128,512]{1,0:T(8,128)(2,1)S(1)} %collective-permute-done.6.refs_5_.refs_1_, bf16[128,512]{1,0:T(8,128)(2,1)S(1)} %collective-permute-done.7.refs_6_.refs_2_, ...), custom_call_target="tpu_custom_call" | custom-call | flops 1073741824 | bytes 524288 | tf_op jit(solution)/shard_map/increment_rows/pallas_call | solution.py:103
  23.3 0.0 collective-permute-start.12
  23.3 2.1 %increment_rows.8 = bf16[64,512]{1,0:T(8,128)(2,1)S(1)} custom-call(s32[16,32]{1,0:T(8,128)S(1)} %copy-done.2, bf16[64,512]{1,0:T(8,128)(2,1)S(1)} %collective-permute-done.4.refs_1_.refs_0_, bf16[128,512]{1,0:T(8,128)(2,1)S(1)} %collective-permute-done.6.refs_5_.refs_1_, bf16[128,512]{1,0:T(8,128)(2,1)S(1)} %collective-permute-done.7.refs_6_.refs_2_, ...), custom_call_target="tpu_custom_call" | custom-call | flops 1073741824 | bytes 524288 | tf_op jit(solution)/shard_map/increment_rows/pallas_call | solution.py:103
  25.4 1.5 %collective-permute-start.11 = (bf16[64,512]{1,0:T(8,128)(2,1)S(1)}, bf16[64,512]{1,0:T(8,128)(2,1)S(1)}, u32[]{:S(2)}, u32[]{:S(2)}) collective-permute-start(bf16[64,512]{1,0:T(8,128)(2,1)S(1)} %increment_rows.8), channel_id=1, source_target_pairs={{0,2},{1,3},{2,0},{3,1},{4,6},{5,7},{6,4},{7,5},{8,10},{9,11},{10,... | collective-permute-start | bytes 196616 | tf_op jit(solution)/shard_map/ppermute | solution.py:140
  26.9 2.0 %increment_rows.7 = bf16[64,512]{1,0:T(8,128)(2,1)S(1)} custom-call(s32[16,32]{1,0:T(8,128)S(1)} %copy-done.2, bf16[64,512]{1,0:T(8,128)(2,1)S(1)} %collective-permute-done.3.refs_0_, bf16[128,512]{1,0:T(8,128)(2,1)S(1)} %collective-permute-done.6.refs_5_.refs_1_, bf16[128,512]{1,0:T(8,128)(2,1)S(1)} %collective-permute-done.7.refs_6_.refs_2_, ...), custom_call_target="tpu_custom_call" | custom-call | flops 1073741824 | bytes 524288 | tf_op jit(solution)/shard_map/increment_rows/pallas_call | solution.py:103
  29.0 2.9 %collective-permute-start.10 = (bf16[64,512]{1,0:T(8,128)(2,1)S(1)}, bf16[64,512]{1,0:T(8,128)(2,1)S(1)}, u32[]{:S(2)}, u32[]{:S(2)}) collective-permute-start(bf16[64,512]{1,0:T(8,128)(2,1)S(1)} %increment_rows.7), channel_id=1, source_target_pairs={{0,3},{1,2},{2,1},{3,0},{4,7},{5,6},{6,5},{7,4},{8,11},{9,10},{10,... | collective-permute-start | bytes 196616 | tf_op jit(solution)/shard_map/ppermute | solution.py:140
  31.9 3.2 %increment_rows.5.refs_0_ = f32[64,512]{1,0:T(8,128)S(1)} custom-call(s32[16,32]{1,0:T(8,128)S(1)} %copy-done.2, bf16[64,512]{1,0:T(8,128)(2,1)S(1)} %bitcast.7, bf16[128,512]{1,0:T(8,128)(2,1)S(1)} %pad_maximum_fusion.refs_1_.refs_3_, bf16[128,512]{1,0:T(8,128)(2,1)S(1)} %collective-permute-done.refs_2_.refs_4_, ...), custom_call_target="tpu_custom_call" | custom-call | flops 2147483648 | bytes 1048576 | tf_op jit(solution)/shard_map/increment_rows/pallas_call | solution.py:103
  35.1 0.7 %copy-done = f32[64,512]{1,0:T(8,128)} copy-done((f32[64,512]{1,0:T(8,128)}, f32[64,512]{1,0:T(8,128)S(1)}, u32[]{:S(2)}) %copy-start) | copy-done | bytes 131096
  35.7 0.6 %copy-done.3 = bf16[64,512]{1,0:T(8,128)(2,1)} copy-done((bf16[64,512]{1,0:T(8,128)(2,1)}, bf16[64,512]{1,0:T(8,128)(2,1)S(1)}, u32[]{:S(2)}) %copy-start.3) | copy-done | bytes 65560
  36.4 0.6 %copy-done.5 = bf16[64,512]{1,0:T(8,128)(2,1)} copy-done((bf16[64,512]{1,0:T(8,128)(2,1)}, bf16[64,512]{1,0:T(8,128)(2,1)S(1)}, u32[]{:S(2)}) %copy-start.5) | copy-done | bytes 65560
  37.0 1.6 %add_up.1 = f32[64,512]{1,0:T(8,128)} custom-call(f32[64,512]{1,0:T(8,128)} %copy-done, bf16[64,512]{1,0:T(8,128)(2,1)} %copy-done.5, bf16[64,512]{1,0:T(8,128)(2,1)} %copy-done.4, bf16[64,512]{1,0:T(8,128)(2,1)} %copy-done.3), custom_call_target="tpu_custom_call" | custom-call | tf_op jit(solution)/shard_map/add_up/pallas_call | solution.py:130
  (22 shorter events, 0.1 us)
Async XLA Ops:
  0.0 9.5 %collective-permute-start.3 = (bf16[64,512]{1,0:T(8,128)(2,1)}, bf16[64,512]{1,0:T(8,128)(2,1)S(1)}, u32[]{:S(2)}, u32[]{:S(2)}) collective-permute-start(bf16[64,512]{1,0:T(8,128)(2,1)} %bitcast.3), channel_id=1, source_target_pairs={{0,3},{1,2},{2,1},{3,0},{4,7},{5,6},{6,5},{7,4},{8,11},{9,10},{10,... | collective-permute-start | bytes 196616 | tf_op jit(solution)/shard_map/ppermute | solution.py:140
  5.0 4.5 %copy-start.1 = (bf16[512,64]{0,1:T(8,128)(2,1)S(1)}, bf16[512,64]{0,1:T(8,128)(2,1)}, u32[]{:S(2)}) copy-start(bf16[512,64]{0,1:T(8,128)(2,1)} %param.6) | copy-start | bytes 196612
  6.0 8.9 %collective-permute-start = (bf16[128,512]{1,0:T(8,128)(2,1)S(1)}, bf16[128,512]{1,0:T(8,128)(2,1)S(1)}, u32[]{:S(2)}, u32[]{:S(2)}) collective-permute-start(bf16[128,512]{1,0:T(8,128)(2,1)S(1)} %pad_maximum_fusion.refs_1_.refs_3_), channel_id=1, source_target_pairs={{0,8},{4,12},{8,0},{12,4},{16,24},{20,28},{24,16},{28,20},{1,9},{5... | collective-permute-start | bytes 393224 | tf_op jit(solution)/shard_map/ppermute | solution.py:140
  7.5 7.8 %collective-permute-start.1 = (bf16[128,512]{1,0:T(8,128)(2,1)S(1)}, bf16[128,512]{1,0:T(8,128)(2,1)S(1)}, u32[]{:S(2)}, u32[]{:S(2)}) collective-permute-start(bf16[128,512]{1,0:T(8,128)(2,1)S(1)} %pad_maximum_fusion.refs_1_.refs_3_), channel_id=1, source_target_pairs={{0,16},{4,20},{8,24},{12,28},{16,0},{20,4},{24,8},{28,12},{1,17},{... | collective-permute-start | bytes 393224 | tf_op jit(solution)/shard_map/ppermute | solution.py:140
  9.0 6.3 %collective-permute-start.2 = (bf16[128,512]{1,0:T(8,128)(2,1)S(1)}, bf16[128,512]{1,0:T(8,128)(2,1)S(1)}, u32[]{:S(2)}, u32[]{:S(2)}) collective-permute-start(bf16[128,512]{1,0:T(8,128)(2,1)S(1)} %pad_maximum_fusion.refs_1_.refs_3_), channel_id=1, source_target_pairs={{0,24},{4,28},{8,16},{12,20},{16,8},{20,12},{24,0},{28,4},{1,25},{... | collective-permute-start | bytes 393224 | tf_op jit(solution)/shard_map/ppermute | solution.py:140
  9.5 5.4 %collective-permute-start.4 = (bf16[64,512]{1,0:T(8,128)(2,1)S(1)}, bf16[64,512]{1,0:T(8,128)(2,1)S(1)}, u32[]{:S(2)}, u32[]{:S(2)}) collective-permute-start(bf16[64,512]{1,0:T(8,128)(2,1)S(1)} %bitcast.5), channel_id=1, source_target_pairs={{0,2},{1,3},{2,0},{3,1},{4,6},{5,7},{6,4},{7,5},{8,10},{9,11},{10,... | collective-permute-start | bytes 196616 | tf_op jit(solution)/shard_map/ppermute | solution.py:140
  9.5 5.4 %collective-permute-start.5 = (bf16[64,512]{1,0:T(8,128)(2,1)S(1)}, bf16[64,512]{1,0:T(8,128)(2,1)S(1)}, u32[]{:S(2)}, u32[]{:S(2)}) collective-permute-start(bf16[64,512]{1,0:T(8,128)(2,1)S(1)} %bitcast.6), channel_id=1, source_target_pairs={{0,1},{1,0},{2,3},{3,2},{4,5},{5,4},{6,7},{7,6},{8,9},{9,8},{10,11... | collective-permute-start | bytes 196616 | tf_op jit(solution)/shard_map/ppermute | solution.py:140
  15.3 5.9 %collective-permute-start.6 = (bf16[128,512]{1,0:T(8,128)(2,1)S(1)}, bf16[128,512]{1,0:T(8,128)(2,1)S(1)}, u32[]{:S(2)}, u32[]{:S(2)}) collective-permute-start(bf16[128,512]{1,0:T(8,128)(2,1)S(1)} %pad_maximum_fusion.refs_1_.refs_3_), channel_id=1, source_target_pairs={{0,4},{4,0},{8,12},{12,8},{16,20},{20,16},{24,28},{28,24},{1,5},{5... | collective-permute-start | bytes 393224 | tf_op jit(solution)/shard_map/ppermute | solution.py:140
  15.3 5.9 %collective-permute-start.7 = (bf16[128,512]{1,0:T(8,128)(2,1)S(1)}, bf16[128,512]{1,0:T(8,128)(2,1)S(1)}, u32[]{:S(2)}, u32[]{:S(2)}) collective-permute-start(bf16[128,512]{1,0:T(8,128)(2,1)S(1)} %collective-permute-done.refs_2_.refs_4_), channel_id=1, source_target_pairs={{0,4},{4,0},{8,12},{12,8},{16,20},{20,16},{24,28},{28,24},{1,5},{5... | collective-permute-start | bytes 393224 | tf_op jit(solution)/shard_map/ppermute | solution.py:140
  15.8 5.4 %collective-permute-start.8 = (bf16[128,512]{1,0:T(8,128)(2,1)S(1)}, bf16[128,512]{1,0:T(8,128)(2,1)S(1)}, u32[]{:S(2)}, u32[]{:S(2)}) collective-permute-start(bf16[128,512]{1,0:T(8,128)(2,1)S(1)} %collective-permute-done.1.refs_3_.refs_5_), channel_id=1, source_target_pairs={{0,4},{4,0},{8,12},{12,8},{16,20},{20,16},{24,28},{28,24},{1,5},{5... | collective-permute-start | bytes 393224 | tf_op jit(solution)/shard_map/ppermute | solution.py:140
  15.8 5.4 %collective-permute-start.9 = (bf16[128,512]{1,0:T(8,128)(2,1)S(1)}, bf16[128,512]{1,0:T(8,128)(2,1)S(1)}, u32[]{:S(2)}, u32[]{:S(2)}) collective-permute-start(bf16[128,512]{1,0:T(8,128)(2,1)S(1)} %collective-permute-done.2.refs_4_.refs_6_), channel_id=1, source_target_pairs={{0,4},{4,0},{8,12},{12,8},{16,20},{20,16},{24,28},{28,24},{1,5},{5... | collective-permute-start | bytes 393224 | tf_op jit(solution)/shard_map/ppermute | solution.py:140
  16.3 0.7 %copy-start.2 = (s32[16,32]{1,0:T(8,128)S(1)}, s32[16,32]{1,0:T(8,128)}, u32[]{:S(2)}) copy-start(s32[16,32]{1,0:T(8,128)} %pair_table.1.table_ref) | copy-start | bytes 6148
  23.3 12.4 %collective-permute-start.12 = (bf16[64,512]{1,0:T(8,128)(2,1)S(1)}, bf16[64,512]{1,0:T(8,128)(2,1)S(1)}, u32[]{:S(2)}, u32[]{:S(2)}) collective-permute-start(bf16[64,512]{1,0:T(8,128)(2,1)S(1)} %increment_rows.9), channel_id=1, source_target_pairs={{0,1},{1,0},{2,3},{3,2},{4,5},{5,4},{6,7},{7,6},{8,9},{9,8},{10,11... | collective-permute-start | bytes 196616 | tf_op jit(solution)/shard_map/ppermute | solution.py:140
  25.4 10.3 %collective-permute-start.11 = (bf16[64,512]{1,0:T(8,128)(2,1)S(1)}, bf16[64,512]{1,0:T(8,128)(2,1)S(1)}, u32[]{:S(2)}, u32[]{:S(2)}) collective-permute-start(bf16[64,512]{1,0:T(8,128)(2,1)S(1)} %increment_rows.8), channel_id=1, source_target_pairs={{0,2},{1,3},{2,0},{3,1},{4,6},{5,7},{6,4},{7,5},{8,10},{9,11},{10,... | collective-permute-start | bytes 196616 | tf_op jit(solution)/shard_map/ppermute | solution.py:140
  29.0 6.7 %collective-permute-start.10 = (bf16[64,512]{1,0:T(8,128)(2,1)S(1)}, bf16[64,512]{1,0:T(8,128)(2,1)S(1)}, u32[]{:S(2)}, u32[]{:S(2)}) collective-permute-start(bf16[64,512]{1,0:T(8,128)(2,1)S(1)} %increment_rows.7), channel_id=1, source_target_pairs={{0,3},{1,2},{2,1},{3,0},{4,7},{5,6},{6,5},{7,4},{8,11},{9,10},{10,... | collective-permute-start | bytes 196616 | tf_op jit(solution)/shard_map/ppermute | solution.py:140
  35.0 0.7 %copy-start = (f32[64,512]{1,0:T(8,128)}, f32[64,512]{1,0:T(8,128)S(1)}, u32[]{:S(2)}) copy-start(f32[64,512]{1,0:T(8,128)S(1)} %increment_rows.5.refs_0_) | copy-start | bytes 393220
  35.7 0.6 %copy-start.3 = (bf16[64,512]{1,0:T(8,128)(2,1)}, bf16[64,512]{1,0:T(8,128)(2,1)S(1)}, u32[]{:S(2)}) copy-start(bf16[64,512]{1,0:T(8,128)(2,1)S(1)} %collective-permute-done.12.refs_3_) | copy-start | bytes 196612
  35.7 0.6 %copy-start.4 = (bf16[64,512]{1,0:T(8,128)(2,1)}, bf16[64,512]{1,0:T(8,128)(2,1)S(1)}, u32[]{:S(2)}) copy-start(bf16[64,512]{1,0:T(8,128)(2,1)S(1)} %collective-permute-done.11.refs_2_) | copy-start | bytes 196612
  36.4 0.6 %copy-start.5 = (bf16[64,512]{1,0:T(8,128)(2,1)}, bf16[64,512]{1,0:T(8,128)(2,1)S(1)}, u32[]{:S(2)}) copy-start(bf16[64,512]{1,0:T(8,128)(2,1)S(1)} %collective-permute-done.10.refs_1_) | copy-start | bytes 196612

commit v3 on v2

--- a/solution.py
+++ b/solution.py
@@ -10,6 +10,7 @@
 DIST_SCALE = 4.0
 DMAX = 8
 HALF = 256
+SMALL = pltpu.CompilerParams(vmem_limit_bytes=4 * 2**20)
 
 F32 = jnp.float32
 BF16 = jnp.bfloat16
@@ -17,7 +18,7 @@
 SMEM = pl.BlockSpec(memory_space=pltpu.SMEM)
 
 
-def pair_table(pair_rows, pair_cols, pair_dist, pair_counts, row_blocks, col_blocks, per_dev):
+def pair_table(pair_rows, pair_cols, pair_dist, pair_counts, row_blocks, col_blocks, per_dev, members):
     def kernel(rows_ref, cols_ref, dist_ref, count_ref, table_ref):
         slots = rows_ref.shape[1]
         row_flip = lax.axis_index("cols") * per_dev
@@ -29,13 +30,18 @@
         left = jnp.where(row_place == (rows_ref[...] ^ row_flip), code, 0.0).astype(BF16)
         right = jnp.where(col_place == (cols_ref[...] ^ col_flip), 1.0, 0.0).astype(BF16)
         table = lax.dot_general(left, right, (((1,), (1,)), ((), ())), preferred_element_type=F32)
-        table_ref[...] = table.astype(jnp.int32)
+        spread = lax.broadcasted_iota(jnp.int32, (col_blocks, col_blocks * BLK), 1) // BLK
+        spread = (spread == lax.broadcasted_iota(jnp.int32, spread.shape, 0)).astype(F32).astype(BF16)
+        wide = jnp.dot(table.astype(BF16), spread, preferred_element_type=F32)
+        weight = jnp.exp((1.0 - wide) / DIST_SCALE) * (1.0 / (members - 1))
+        table_ref[...] = jnp.where(wide > 0.5, weight, 0.0)
 
     return pl.pallas_call(
         kernel,
-        out_shape=jax.ShapeDtypeStruct((row_blocks, col_blocks), jnp.int32),
+        out_shape=jax.ShapeDtypeStruct((row_blocks, col_blocks * BLK), F32),
         in_specs=[VMEM, VMEM, VMEM, SMEM],
         out_specs=VMEM,
+        compiler_params=SMALL,
         name="pair_table",
     )(pair_rows, pair_cols, pair_dist, pair_counts)
 
@@ -55,11 +61,7 @@
         )
         taper_ref, left_ref, total_ref = refs
         gap = lax.broadcasted_iota(jnp.int32, (BLK, BLK), 0) - lax.broadcasted_iota(jnp.int32, (BLK, BLK), 1)
-        base = jnp.exp(-jnp.abs(gap).astype(F32) / TAPER_CELLS) * (1.0 / (members - 1))
-        weights = jnp.exp(lax.broadcasted_iota(jnp.int32, (1, BLK), 1).astype(F32) / -DIST_SCALE)
-        taper_ref[0] = jnp.zeros((BLK, BLK), F32)
-        for dist in range(DMAX):
-            taper_ref[dist + 1] = base * weights[0:1, dist : dist + 1]
+        taper_ref[...] = jnp.exp(-jnp.abs(gap).astype(F32) / TAPER_CELLS)
         for row in range(n_row):
             left_ref[...] = row_refs[row][...].T
             sum_ref = total_ref if send is not None else out_refs[row]
@@ -77,7 +79,7 @@
                             jnp.concatenate(
                                 [
                                     products[a * BLK : (a + 1) * BLK, q * BLK : (q + 1) * BLK]
-                                    * taper_ref[table_ref[first_row + a, first_col + q]]
+                                    * (taper_ref[...] * table_ref[pl.ds(first_row + a, 1), pl.ds((first_col + q) * BLK, BLK)])
                                     for q in range(per_half)
                                 ],
                                 axis=1,
@@ -103,10 +105,10 @@
     return pl.pallas_call(
         kernel,
         out_shape=[jax.ShapeDtypeStruct(out, F32 if send is None else send)] * n_row,
-        in_specs=[SMEM] + [VMEM] * (n_row + n_col + n_before),
+        in_specs=[VMEM] + [VMEM] * (n_row + n_col + n_before),
         out_specs=[VMEM] * n_row,
         scratch_shapes=[
-            pltpu.VMEM((DMAX + 1, BLK, BLK), F32),
+            pltpu.VMEM((BLK, BLK), F32),
             pltpu.VMEM((cells, members), BF16),
             pltpu.VMEM((cells, columns), F32),
         ],
@@ -132,6 +134,7 @@
         out_shape=jax.ShapeDtypeStruct(own.shape, F32),
         in_specs=[VMEM] * (1 + len(received)),
         out_specs=VMEM,
+        compiler_params=SMALL,
         name="add_up",
     )(own, *received)
 
@@ -153,16 +156,24 @@
         others = list(range(n_cols - 1, 0, -1))
         row_parts = [swap(anom, "cols", n_cols, flip) for flip in others]
         table = pair_table(
-            pair_rows, pair_cols, pair_dist, pair_counts, n_cols * per_dev, n_rows * per_dev, per_dev
+            pair_rows, pair_cols, pair_dist, pair_counts, n_cols * per_dev, n_rows * per_dev, per_dev, anomalies.shape[1]
         )
         *near_parts, table = lax.optimization_barrier((*near_parts, *row_parts, table))
         near_parts, row_parts = near_parts[: len(near)], near_parts[len(near) :]
         far_parts = [swap(part, "rows", n_rows, 1) for part in near_parts]
         before = increment_rows(table, row_parts, near_parts, others, near, [], None)
         received = []
-        for i, flip in enumerate(others):
-            (part,) = increment_rows(table, [row_parts[i]], far_parts, [flip], far, [before[i]], BF16)
-            received.append(swap(part, "cols", n_cols, flip))
+        for group in [[i] for i in range(len(others))]:
+            parts = increment_rows(
+                table,
+                [row_parts[i] for i in group],
+                far_parts,
+                [others[i] for i in group],
+                far,
+                [before[i] for i in group],
+                BF16,
+            )
+            received += [swap(part, "cols", n_cols, others[i]) for i, part in zip(group, parts)]
         (own,) = increment_rows(table, [anom], near_parts + far_parts, [0], near + far, [], F32)
         return add_up(own, received).T
 

time: 38.9 us -> 32.7 us (0.84)
  Pallas kernels: 16.6 us -> 11.2 us
  local copies, waits for them, and re-layouts: 2.6 us -> 0.01 us
  waiting for transfers between devices: 3.12 us -> 4.95 us
    pallas_call x5, Pallas kernels: 13.5 us -> 10.1 us  [increment_rows(): pl.pallas_call(kernel, out_shape=[jax.ShapeDtypeStruct(out, F32 if send i...]
    unnamed x12 -> x8, local copies, waits for them, and re-layouts: 2.6 us -> 0.01 us
    ppermute x13, waiting for transfers between devices: 3.12 us -> 4.95 us  [swap(): return lax.ppermute(x, axis, [(i, i ^ flip) for i in range(size)])]
    pallas_call x1, Pallas kernels: 1.45 us -> 0.34 us  [pair_table(): pl.pallas_call(kernel, out_shape=jax.ShapeDtypeStruct((row_blocks, col_bl...]
    pallas_call x1, Pallas kernels: 1.65 us -> 0.68 us  [add_up(): pl.pallas_call(kernel, out_shape=jax.ShapeDtypeStruct(own.shape, F32), in...]
  transfers between devices with their start and end apart: 13 -> 13, of which waited for: 2 -> 3; matrix products, arithmetic and copies ran while one was open for 2% -> 3% of each run, Pallas kernels for 33% -> 28%
where the time goes in v3:
time: 32.7 us; the launch traced here: 32.5 us
  starting transfers between devices  14.7 us (45%)
  Pallas kernels  11.2 us (34%)
  waiting for transfers between devices  4.95 us (15%)
  other arithmetic  0.95 us (3%)
  between operations  0.76 us (2%)
    ppermute x13, starting transfers between devices, swap(): return lax.ppermute(x, axis, [(i, i ^ flip) for i in range(size)])  14.7 us
    pallas_call x5, Pallas kernels, increment_rows(): pl.pallas_call(kernel, out_shape=[jax.ShapeDtypeStruct(out, F32 if send i...  10.1 us
    ppermute x13, waiting for transfers between devices, swap(): return lax.ppermute(x, axis, [(i, i ^ flip) for i in range(size)])  4.95 us
    concatenate x1, other arithmetic, local(): packed = jnp.concatenate([anom, innov], axis=0)  0.95 us
    pallas_call x1, Pallas kernels, add_up(): pl.pallas_call(kernel, out_shape=jax.ShapeDtypeStruct(own.shape, F32), in...  0.68 us
  transfers between devices with their start and end apart: 13, of which 3 were waited for; matrix products, arithmetic and copies ran while one was open for 3% of the time, Pallas kernels for 28%

profile of v3, /device:TPU:0, one launch (start us, length us, event | category | flops | bytes accessed | tf_op | source)
XLA Modules:
  0.0 32.5 jit_solution(13738330929375419441)
XLA Ops:
  0.0 5.0 %collective-permute-start.3 = (bf16[64,512]{1,0:T(8,128)(2,1)}, bf16[64,512]{1,0:T(8,128)(2,1)S(1)}, u32[]{:S(2)}, u32[]{:S(2)}) collective-permute-start(bf16[64,512]{1,0:T(8,128)(2,1)} %bitcast.3), channel_id=1, source_target_pairs={{0,3},{1,2},{2,1},{3,0},{4,7},{5,6},{6,5},{7,4},{8,11},{9,10},{10,... | collective-permute-start | bytes 196616 | tf_op jit(solution)/shard_map/ppermute | solution.py:143
  5.1 0.9 %pad_maximum_fusion.refs_1_.refs_3_ = bf16[128,512]{1,0:T(8,128)(2,1)S(1)} fusion(bf16[64,512]{1,0:T(8,128)(2,1)} %bitcast.8, bf16[64,512]{1,0:T(8,128)(2,1)} %bitcast.4), kind=kLoop, calls=%fused_computation | loop fusion | flops 262144 | bytes 262144 | tf_op jit(solution)/shard_map/concatenate | solution.py:152
  6.0 1.6 %collective-permute-start = (bf16[128,512]{1,0:T(8,128)(2,1)S(1)}, bf16[128,512]{1,0:T(8,128)(2,1)S(1)}, u32[]{:S(2)}, u32[]{:S(2)}) collective-permute-start(bf16[128,512]{1,0:T(8,128)(2,1)S(1)} %pad_maximum_fusion.refs_1_.refs_3_), channel_id=1, source_target_pairs={{0,8},{4,12},{8,0},{12,4},{16,24},{20,28},{24,16},{28,20},{1,9},{5... | collective-permute-start | bytes 393224 | tf_op jit(solution)/shard_map/ppermute | solution.py:143
  7.6 1.5 %collective-permute-start.1 = (bf16[128,512]{1,0:T(8,128)(2,1)S(1)}, bf16[128,512]{1,0:T(8,128)(2,1)S(1)}, u32[]{:S(2)}, u32[]{:S(2)}) collective-permute-start(bf16[128,512]{1,0:T(8,128)(2,1)S(1)} %pad_maximum_fusion.refs_1_.refs_3_), channel_id=1, source_target_pairs={{0,16},{4,20},{8,24},{12,28},{16,0},{20,4},{24,8},{28,12},{1,17},{... | collective-permute-start | bytes 393224 | tf_op jit(solution)/shard_map/ppermute | solution.py:143
  9.1 0.5 %collective-permute-start.2 = (bf16[128,512]{1,0:T(8,128)(2,1)S(1)}, bf16[128,512]{1,0:T(8,128)(2,1)S(1)}, u32[]{:S(2)}, u32[]{:S(2)}) collective-permute-start(bf16[128,512]{1,0:T(8,128)(2,1)S(1)} %pad_maximum_fusion.refs_1_.refs_3_), channel_id=1, source_target_pairs={{0,24},{4,28},{8,16},{12,20},{16,8},{20,12},{24,0},{28,4},{1,25},{... | collective-permute-start | bytes 393224 | tf_op jit(solution)/shard_map/ppermute | solution.py:143
  9.6 0.6 %collective-permute-start.5 = (bf16[64,512]{1,0:T(8,128)(2,1)S(1)}, bf16[64,512]{1,0:T(8,128)(2,1)S(1)}, u32[]{:S(2)}, u32[]{:S(2)}) collective-permute-start(bf16[64,512]{1,0:T(8,128)(2,1)S(1)} %bitcast.6), channel_id=1, source_target_pairs={{0,1},{1,0},{2,3},{3,2},{4,5},{5,4},{6,7},{7,6},{8,9},{9,8},{10,11... | collective-permute-start | bytes 196616 | tf_op jit(solution)/shard_map/ppermute | solution.py:143
  10.8 0.3 %pair_table.1.table_ref = f32[16,4096]{1,0:T(8,128)S(1)} custom-call(s32[1,512]{1,0:T(1,128)S(1)} %copy-done.1, s32[1,512]{1,0:T(1,128)S(1)} %copy-done.2, s32[1,512]{1,0:T(1,128)S(1)} %copy-done.3, s32[1,1]{1,0:T(1,128)S(6)} %copy.7.count_ref), custom_call_target="tpu_custom_call" | custom-call | tf_op jit(solution)/shard_map/pair_table/pallas_call | solution.py:39
  11.2 3.8 %collective-permute-done.4.refs_1_.refs_0_ = bf16[64,512]{1,0:T(8,128)(2,1)S(1)} collective-permute-done((bf16[64,512]{1,0:T(8,128)(2,1)S(1)}, bf16[64,512]{1,0:T(8,128)(2,1)S(1)}, u32[]{:S(2)}, u32[]{:S(2)}) %collective-permute-start.4) | collective-permute-done | bytes 65568 | tf_op jit(solution)/shard_map/ppermute | solution.py:143
  14.9 0.0 collective-permute-done.5.refs_2_.refs_0_
  14.9 0.0 collective-permute-done.refs_2_.refs_4_
  14.9 0.4 %collective-permute-done.1.refs_3_.refs_5_ = bf16[128,512]{1,0:T(8,128)(2,1)S(1)} collective-permute-done((bf16[128,512]{1,0:T(8,128)(2,1)S(1)}, bf16[128,512]{1,0:T(8,128)(2,1)S(1)}, u32[]{:S(2)}, u32[]{:S(2)}) %collective-permute-start.1) | collective-permute-done | bytes 131104 | tf_op jit(solution)/shard_map/ppermute | solution.py:143
  15.3 0.5 %collective-permute-start.7 = (bf16[128,512]{1,0:T(8,128)(2,1)S(1)}, bf16[128,512]{1,0:T(8,128)(2,1)S(1)}, u32[]{:S(2)}, u32[]{:S(2)}) collective-permute-start(bf16[128,512]{1,0:T(8,128)(2,1)S(1)} %collective-permute-done.refs_2_.refs_4_), channel_id=1, source_target_pairs={{0,4},{4,0},{8,12},{12,8},{16,20},{20,16},{24,28},{28,24},{1,5},{5... | collective-permute-start | bytes 393224 | tf_op jit(solution)/shard_map/ppermute | solution.py:143
  15.9 0.0 collective-permute-start.8
  15.9 0.5 %collective-permute-start.9 = (bf16[128,512]{1,0:T(8,128)(2,1)S(1)}, bf16[128,512]{1,0:T(8,128)(2,1)S(1)}, u32[]{:S(2)}, u32[]{:S(2)}) collective-permute-start(bf16[128,512]{1,0:T(8,128)(2,1)S(1)} %collective-permute-done.2.refs_4_.refs_6_), channel_id=1, source_target_pairs={{0,4},{4,0},{8,12},{12,8},{16,20},{20,16},{24,28},{28,24},{1,5},{5... | collective-permute-start | bytes 393224 | tf_op jit(solution)/shard_map/ppermute | solution.py:143
  16.4 3.5 %increment_rows.6 = (f32[512,64]{1,0:T(8,128)S(1)}, f32[512,64]{1,0:T(8,128)S(1)}, f32[512,64]{1,0:T(8,128)S(1)}) custom-call(f32[16,4096]{1,0:T(8,128)S(1)} %pair_table.1.table_ref, bf16[64,512]{1,0:T(8,128)(2,1)S(1)} %collective-permute-done.3.refs_0_, bf16[64,512]{1,0:T(8,128)(2,1)S(1)} %collective-permute-done.4.refs_1_.refs_0_, ...), custom_call_target="tpu_custom_call" | custom-call | flops 3221225472 | bytes 524288 | tf_op jit(solution)/shard_map/increment_rows/pallas_call | solution.py:105
  19.9 1.4 %increment_rows.9 = bf16[64,512]{1,0:T(8,128)(2,1)S(1)} custom-call(f32[16,4096]{1,0:T(8,128)S(1)} %pair_table.1.table_ref, bf16[64,512]{1,0:T(8,128)(2,1)S(1)} %collective-permute-done.5.refs_2_.refs_0_, bf16[128,512]{1,0:T(8,128)(2,1)S(1)} %collective-permute-done.6.refs_5_.refs_1_, bf16[128,512]{1,0:T(8,128)(2,1)S(1)} %collective-permute-done.7.refs_6_.refs_2_, ...), custom_call_target="tpu_custom_call" | custom-call | flops 1073741824 | bytes 524288 | tf_op jit(solution)/shard_map/increment_rows/pallas_call | solution.py:105
  21.3 0.0 collective-permute-start.12
  21.3 1.4 %increment_rows.8 = bf16[64,512]{1,0:T(8,128)(2,1)S(1)} custom-call(f32[16,4096]{1,0:T(8,128)S(1)} %pair_table.1.table_ref, bf16[64,512]{1,0:T(8,128)(2,1)S(1)} %collective-permute-done.4.refs_1_.refs_0_, bf16[128,512]{1,0:T(8,128)(2,1)S(1)} %collective-permute-done.6.refs_5_.refs_1_, bf16[128,512]{1,0:T(8,128)(2,1)S(1)} %collective-permute-done.7.refs_6_.refs_2_, ...), custom_call_target="tpu_custom_call" | custom-call | flops 1073741824 | bytes 524288 | tf_op jit(solution)/shard_map/increment_rows/pallas_call | solution.py:105
  22.7 1.6 %collective-permute-start.11 = (bf16[64,512]{1,0:T(8,128)(2,1)S(1)}, bf16[64,512]{1,0:T(8,128)(2,1)S(1)}, u32[]{:S(2)}, u32[]{:S(2)}) collective-permute-start(bf16[64,512]{1,0:T(8,128)(2,1)S(1)} %increment_rows.8), channel_id=1, source_target_pairs={{0,2},{1,3},{2,0},{3,1},{4,6},{5,7},{6,4},{7,5},{8,10},{9,11},{10,... | collective-permute-start | bytes 196616 | tf_op jit(solution)/shard_map/ppermute | solution.py:143
  24.3 1.4 %increment_rows.7 = bf16[64,512]{1,0:T(8,128)(2,1)S(1)} custom-call(f32[16,4096]{1,0:T(8,128)S(1)} %pair_table.1.table_ref, bf16[64,512]{1,0:T(8,128)(2,1)S(1)} %collective-permute-done.3.refs_0_, bf16[128,512]{1,0:T(8,128)(2,1)S(1)} %collective-permute-done.6.refs_5_.refs_1_, bf16[128,512]{1,0:T(8,128)(2,1)S(1)} %collective-permute-done.7.refs_6_.refs_2_, ...), custom_call_target="tpu_custom_call" | custom-call | flops 1073741824 | bytes 524288 | tf_op jit(solution)/shard_map/increment_rows/pallas_call | solution.py:105
  25.7 2.9 %collective-permute-start.10 = (bf16[64,512]{1,0:T(8,128)(2,1)S(1)}, bf16[64,512]{1,0:T(8,128)(2,1)S(1)}, u32[]{:S(2)}, u32[]{:S(2)}) collective-permute-start(bf16[64,512]{1,0:T(8,128)(2,1)S(1)} %increment_rows.7), channel_id=1, source_target_pairs={{0,3},{1,2},{2,1},{3,0},{4,7},{5,6},{6,5},{7,4},{8,11},{9,10},{10,... | collective-permute-start | bytes 196616 | tf_op jit(solution)/shard_map/ppermute | solution.py:143
  28.6 2.5 %increment_rows.5.refs_0_ = f32[64,512]{1,0:T(8,128)S(1)} custom-call(f32[16,4096]{1,0:T(8,128)S(1)} %pair_table.1.table_ref, bf16[64,512]{1,0:T(8,128)(2,1)S(1)} %bitcast.7, bf16[128,512]{1,0:T(8,128)(2,1)S(1)} %pad_maximum_fusion.refs_1_.refs_3_, bf16[128,512]{1,0:T(8,128)(2,1)S(1)} %collective-permute-done.refs_2_.refs_4_, ...), custom_call_target="tpu_custom_call" | custom-call | flops 2147483648 | bytes 1048576 | tf_op jit(solution)/shard_map/increment_rows/pallas_call | solution.py:105
  31.1 0.8 %collective-permute-done.10.refs_1_ = bf16[64,512]{1,0:T(8,128)(2,1)S(1)} collective-permute-done((bf16[64,512]{1,0:T(8,128)(2,1)S(1)}, bf16[64,512]{1,0:T(8,128)(2,1)S(1)}, u32[]{:S(2)}, u32[]{:S(2)}) %collective-permute-start.10) | collective-permute-done | bytes 65568 | tf_op jit(solution)/shard_map/ppermute | solution.py:143
  31.8 0.7 %add_up.1 = f32[64,512]{1,0:T(8,128)} custom-call(f32[64,512]{1,0:T(8,128)S(1)} %increment_rows.5.refs_0_, bf16[64,512]{1,0:T(8,128)(2,1)S(1)} %collective-permute-done.10.refs_1_, bf16[64,512]{1,0:T(8,128)(2,1)S(1)} %collective-permute-done.11.refs_2_, bf16[64,512]{1,0:T(8,128)(2,1)S(1)} %collective-permute-done.12.refs_3_), custom_call_target="tpu_custom_call" | custom-call | tf_op jit(solution)/shard_map/add_up/pallas_call | solution.py:132
  (18 shorter events, 0.0 us)
Async XLA Ops:
  0.0 9.6 %collective-permute-start.3 = (bf16[64,512]{1,0:T(8,128)(2,1)}, bf16[64,512]{1,0:T(8,128)(2,1)S(1)}, u32[]{:S(2)}, u32[]{:S(2)}) collective-permute-start(bf16[64,512]{1,0:T(8,128)(2,1)} %bitcast.3), channel_id=1, source_target_pairs={{0,3},{1,2},{2,1},{3,0},{4,7},{5,6},{6,5},{7,4},{8,11},{9,10},{10,... | collective-permute-start | bytes 196616 | tf_op jit(solution)/shard_map/ppermute | solution.py:143
  5.0 4.5 %copy-start = (bf16[512,64]{0,1:T(8,128)(2,1)S(1)}, bf16[512,64]{0,1:T(8,128)(2,1)}, u32[]{:S(2)}) copy-start(bf16[512,64]{0,1:T(8,128)(2,1)} %param.6) | copy-start | bytes 196612
  5.1 5.7 %copy-start.1 = (s32[1,512]{1,0:T(1,128)S(1)}, s32[1,512]{1,0:T(1,128)}, u32[]{:S(2)}) copy-start(s32[1,512]{1,0:T(1,128)} %rows_ref.1) | copy-start | bytes 6148
  5.1 5.7 %copy-start.2 = (s32[1,512]{1,0:T(1,128)S(1)}, s32[1,512]{1,0:T(1,128)}, u32[]{:S(2)}) copy-start(s32[1,512]{1,0:T(1,128)} %cols_ref.1) | copy-start | bytes 6148
  5.1 5.8 %copy-start.3 = (s32[1,512]{1,0:T(1,128)S(1)}, s32[1,512]{1,0:T(1,128)}, u32[]{:S(2)}) copy-start(s32[1,512]{1,0:T(1,128)} %dist_ref.1) | copy-start | bytes 6148
  6.0 8.9 %collective-permute-start = (bf16[128,512]{1,0:T(8,128)(2,1)S(1)}, bf16[128,512]{1,0:T(8,128)(2,1)S(1)}, u32[]{:S(2)}, u32[]{:S(2)}) collective-permute-start(bf16[128,512]{1,0:T(8,128)(2,1)S(1)} %pad_maximum_fusion.refs_1_.refs_3_), channel_id=1, source_target_pairs={{0,8},{4,12},{8,0},{12,4},{16,24},{20,28},{24,16},{28,20},{1,9},{5... | collective-permute-start | bytes 393224 | tf_op jit(solution)/shard_map/ppermute | solution.py:143
  7.6 7.8 %collective-permute-start.1 = (bf16[128,512]{1,0:T(8,128)(2,1)S(1)}, bf16[128,512]{1,0:T(8,128)(2,1)S(1)}, u32[]{:S(2)}, u32[]{:S(2)}) collective-permute-start(bf16[128,512]{1,0:T(8,128)(2,1)S(1)} %pad_maximum_fusion.refs_1_.refs_3_), channel_id=1, source_target_pairs={{0,16},{4,20},{8,24},{12,28},{16,0},{20,4},{24,8},{28,12},{1,17},{... | collective-permute-start | bytes 393224 | tf_op jit(solution)/shard_map/ppermute | solution.py:143
  9.1 6.3 %collective-permute-start.2 = (bf16[128,512]{1,0:T(8,128)(2,1)S(1)}, bf16[128,512]{1,0:T(8,128)(2,1)S(1)}, u32[]{:S(2)}, u32[]{:S(2)}) collective-permute-start(bf16[128,512]{1,0:T(8,128)(2,1)S(1)} %pad_maximum_fusion.refs_1_.refs_3_), channel_id=1, source_target_pairs={{0,24},{4,28},{8,16},{12,20},{16,8},{20,12},{24,0},{28,4},{1,25},{... | collective-permute-start | bytes 393224 | tf_op jit(solution)/shard_map/ppermute | solution.py:143
  9.6 5.4 %collective-permute-start.4 = (bf16[64,512]{1,0:T(8,128)(2,1)S(1)}, bf16[64,512]{1,0:T(8,128)(2,1)S(1)}, u32[]{:S(2)}, u32[]{:S(2)}) collective-permute-start(bf16[64,512]{1,0:T(8,128)(2,1)S(1)} %bitcast.5), channel_id=1, source_target_pairs={{0,2},{1,3},{2,0},{3,1},{4,6},{5,7},{6,4},{7,5},{8,10},{9,11},{10,... | collective-permute-start | bytes 196616 | tf_op jit(solution)/shard_map/ppermute | solution.py:143
  9.6 5.4 %collective-permute-start.5 = (bf16[64,512]{1,0:T(8,128)(2,1)S(1)}, bf16[64,512]{1,0:T(8,128)(2,1)S(1)}, u32[]{:S(2)}, u32[]{:S(2)}) collective-permute-start(bf16[64,512]{1,0:T(8,128)(2,1)S(1)} %bitcast.6), channel_id=1, source_target_pairs={{0,1},{1,0},{2,3},{3,2},{4,5},{5,4},{6,7},{7,6},{8,9},{9,8},{10,11... | collective-permute-start | bytes 196616 | tf_op jit(solution)/shard_map/ppermute | solution.py:143
  15.3 4.5 %collective-permute-start.6 = (bf16[128,512]{1,0:T(8,128)(2,1)S(1)}, bf16[128,512]{1,0:T(8,128)(2,1)S(1)}, u32[]{:S(2)}, u32[]{:S(2)}) collective-permute-start(bf16[128,512]{1,0:T(8,128)(2,1)S(1)} %pad_maximum_fusion.refs_1_.refs_3_), channel_id=1, source_target_pairs={{0,4},{4,0},{8,12},{12,8},{16,20},{20,16},{24,28},{28,24},{1,5},{5... | collective-permute-start | bytes 393224 | tf_op jit(solution)/shard_map/ppermute | solution.py:143
  15.3 4.5 %collective-permute-start.7 = (bf16[128,512]{1,0:T(8,128)(2,1)S(1)}, bf16[128,512]{1,0:T(8,128)(2,1)S(1)}, u32[]{:S(2)}, u32[]{:S(2)}) collective-permute-start(bf16[128,512]{1,0:T(8,128)(2,1)S(1)} %collective-permute-done.refs_2_.refs_4_), channel_id=1, source_target_pairs={{0,4},{4,0},{8,12},{12,8},{16,20},{20,16},{24,28},{28,24},{1,5},{5... | collective-permute-start | bytes 393224 | tf_op jit(solution)/shard_map/ppermute | solution.py:143
  15.9 4.0 %collective-permute-start.8 = (bf16[128,512]{1,0:T(8,128)(2,1)S(1)}, bf16[128,512]{1,0:T(8,128)(2,1)S(1)}, u32[]{:S(2)}, u32[]{:S(2)}) collective-permute-start(bf16[128,512]{1,0:T(8,128)(2,1)S(1)} %collective-permute-done.1.refs_3_.refs_5_), channel_id=1, source_target_pairs={{0,4},{4,0},{8,12},{12,8},{16,20},{20,16},{24,28},{28,24},{1,5},{5... | collective-permute-start | bytes 393224 | tf_op jit(solution)/shard_map/ppermute | solution.py:143
  15.9 4.0 %collective-permute-start.9 = (bf16[128,512]{1,0:T(8,128)(2,1)S(1)}, bf16[128,512]{1,0:T(8,128)(2,1)S(1)}, u32[]{:S(2)}, u32[]{:S(2)}) collective-permute-start(bf16[128,512]{1,0:T(8,128)(2,1)S(1)} %collective-permute-done.2.refs_4_.refs_6_), channel_id=1, source_target_pairs={{0,4},{4,0},{8,12},{12,8},{16,20},{20,16},{24,28},{28,24},{1,5},{5... | collective-permute-start | bytes 393224 | tf_op jit(solution)/shard_map/ppermute | solution.py:143
  21.3 9.8 %collective-permute-start.12 = (bf16[64,512]{1,0:T(8,128)(2,1)S(1)}, bf16[64,512]{1,0:T(8,128)(2,1)S(1)}, u32[]{:S(2)}, u32[]{:S(2)}) collective-permute-start(bf16[64,512]{1,0:T(8,128)(2,1)S(1)} %increment_rows.9), channel_id=1, source_target_pairs={{0,1},{1,0},{2,3},{3,2},{4,5},{5,4},{6,7},{7,6},{8,9},{9,8},{10,11... | collective-permute-start | bytes 196616 | tf_op jit(solution)/shard_map/ppermute | solution.py:143
  22.7 8.4 %collective-permute-start.11 = (bf16[64,512]{1,0:T(8,128)(2,1)S(1)}, bf16[64,512]{1,0:T(8,128)(2,1)S(1)}, u32[]{:S(2)}, u32[]{:S(2)}) collective-permute-start(bf16[64,512]{1,0:T(8,128)(2,1)S(1)} %increment_rows.8), channel_id=1, source_target_pairs={{0,2},{1,3},{2,0},{3,1},{4,6},{5,7},{6,4},{7,5},{8,10},{9,11},{10,... | collective-permute-start | bytes 196616 | tf_op jit(solution)/shard_map/ppermute | solution.py:143
  25.7 6.2 %collective-permute-start.10 = (bf16[64,512]{1,0:T(8,128)(2,1)S(1)}, bf16[64,512]{1,0:T(8,128)(2,1)S(1)}, u32[]{:S(2)}, u32[]{:S(2)}) collective-permute-start(bf16[64,512]{1,0:T(8,128)(2,1)S(1)} %increment_rows.7), channel_id=1, source_target_pairs={{0,3},{1,2},{2,1},{3,0},{4,7},{5,6},{6,5},{7,4},{8,11},{9,10},{10,... | collective-permute-start | bytes 196616 | tf_op jit(solution)/shard_map/ppermute | solution.py:143

commit v4 on v3

--- a/solution.py
+++ b/solution.py
@@ -46,24 +46,31 @@
     )(pair_rows, pair_cols, pair_dist, pair_counts)
 
 
-def increment_rows(table, row_parts, col_parts, row_flips, col_flips, before, send):
-    members, cells = row_parts[0].shape
+def increment_rows(table, places, row_flips, members, col_parts, col_flips, before, send):
+    cells = col_parts[0].shape[1]
     columns = col_parts[0].shape[0] - members
     blocks = cells // BLK
     halves = cells // HALF
     per_half = HALF // BLK
-    n_row, n_col, n_before = len(row_parts), len(col_parts), len(before)
+    row_stacks = []
+    for stacked, _ in places:
+        if all(stacked is not known for known in row_stacks):
+            row_stacks.append(stacked)
+    spots = [
+        ([stacked is known for known in row_stacks].index(True), start) for stacked, start in places
+    ]
+    n_row, n_stack, n_col, n_before = len(places), len(row_stacks), len(col_parts), len(before)
 
     def kernel(table_ref, *refs):
         refs = list(refs)
         row_refs, col_refs, before_refs, out_refs = (
-            [refs.pop(0) for _ in range(n)] for n in (n_row, n_col, n_before, n_row)
+            [refs.pop(0) for _ in range(n)] for n in (n_stack, n_col, n_before, n_row)
         )
         taper_ref, left_ref, total_ref = refs
         gap = lax.broadcasted_iota(jnp.int32, (BLK, BLK), 0) - lax.broadcasted_iota(jnp.int32, (BLK, BLK), 1)
         taper_ref[...] = jnp.exp(-jnp.abs(gap).astype(F32) / TAPER_CELLS)
         for row in range(n_row):
-            left_ref[...] = row_refs[row][...].T
+            left_ref[...] = row_refs[spots[row][0]][pl.ds(spots[row][1], members), :].T
             sum_ref = total_ref if send is not None else out_refs[row]
             for col in range(n_col):
                 total = None
@@ -105,7 +112,7 @@
     return pl.pallas_call(
         kernel,
         out_shape=[jax.ShapeDtypeStruct(out, F32 if send is None else send)] * n_row,
-        in_specs=[VMEM] + [VMEM] * (n_row + n_col + n_before),
+        in_specs=[VMEM] + [VMEM] * (n_stack + n_col + n_before),
         out_specs=[VMEM] * n_row,
         scratch_shapes=[
             pltpu.VMEM((BLK, BLK), F32),
@@ -119,7 +126,27 @@
             transcendentals=BLK * BLK,
         ),
         name="increment_rows",
-    )(table, *row_parts, *col_parts, *before)
+    )(table, *row_stacks, *col_parts, *before)
+
+
+def stack(parts):
+    heights = [part.shape[0] for part in parts]
+
+    def kernel(*refs):
+        start = 0
+        for ref, height in zip(refs, heights):
+            refs[-1][pl.ds(start, height), :] = ref[...]
+            start += height
+
+    return pl.pallas_call(
+        kernel,
+        out_shape=jax.ShapeDtypeStruct((sum(heights), parts[0].shape[1]), parts[0].dtype),
+        in_specs=[VMEM] * len(parts),
+        out_specs=VMEM,
+        compiler_params=SMALL,
+        cost_estimate=pl.CostEstimate(flops=1000000000, bytes_accessed=0, transcendentals=0),
+        name="stack",
+    )(*parts)
 
 
 def add_up(own, received):
@@ -148,33 +175,42 @@
 
     def local(anomalies, innovations, pair_rows, pair_cols, pair_dist, pair_counts):
         per_dev = anomalies.shape[0] // BLK
+        members = anomalies.shape[1]
         anom, innov = anomalies.T, innovations.T
         packed = jnp.concatenate([anom, innov], axis=0)
         near = list(range(0, n_rows, 2))
         far = [flip + 1 for flip in near]
+        places, held = [(anom, 0)], [anom]
+        while len(places) < n_cols:
+            outgoing = held[0] if len(held) == 1 else stack(held)
+            arrived = swap(outgoing, "cols", n_cols, len(places))
+            places += [(arrived, i * members) for i in range(len(places))]
+            held.append(arrived)
         near_parts = [packed] + [swap(packed, "rows", n_rows, flip) for flip in near[1:]]
-        others = list(range(n_cols - 1, 0, -1))
-        row_parts = [swap(anom, "cols", n_cols, flip) for flip in others]
         table = pair_table(
-            pair_rows, pair_cols, pair_dist, pair_counts, n_cols * per_dev, n_rows * per_dev, per_dev, anomalies.shape[1]
-        )
-        *near_parts, table = lax.optimization_barrier((*near_parts, *row_parts, table))
-        near_parts, row_parts = near_parts[: len(near)], near_parts[len(near) :]
+            pair_rows, pair_cols, pair_dist, pair_counts, n_cols * per_dev, n_rows * per_dev, per_dev, members
+        )
+
         far_parts = [swap(part, "rows", n_rows, 1) for part in near_parts]
-        before = increment_rows(table, row_parts, near_parts, others, near, [], None)
+        others = list(range(1, n_cols))
+        early = len(near) // 2
+        first = increment_rows(table, places[1:2], [1], members, near_parts[:early], near[:early], [], None)
+        before = dict(
+            zip(
+                others[:1],
+                increment_rows(table, places[1:2], [1], members, near_parts[early:], near[early:], first, None),
+            )
+        )
+        before.update(
+            zip(others[1:], increment_rows(table, places[2:], others[1:], members, near_parts, near, [], None))
+        )
         received = []
-        for group in [[i] for i in range(len(others))]:
-            parts = increment_rows(
-                table,
-                [row_parts[i] for i in group],
-                far_parts,
-                [others[i] for i in group],
-                far,
-                [before[i] for i in group],
-                BF16,
-            )
-            received += [swap(part, "cols", n_cols, others[i]) for i, part in zip(group, parts)]
-        (own,) = increment_rows(table, [anom], near_parts + far_parts, [0], near + far, [], F32)
+        for flip in others:
+            (part,) = increment_rows(table, [places[flip]], [flip], members, far_parts, far, [before[flip]], BF16)
+            received.append(swap(part, "cols", n_cols, flip))
+        (own,) = increment_rows(
+            table, [places[0]], [0], members, near_parts + far_parts, near + far, [], F32
+        )
         return add_up(own, received).T
 
     spread = P(("rows", "cols"), None)

time: 32.7 us -> 30.4 us (0.930)
  waiting for transfers between devices: 4.95 us -> 2.14 us
  Pallas kernels: 11.2 us -> 11.6 us
    ppermute x13 -> x12, waiting for transfers between devices: 4.95 us -> 2.14 us  [swap(): return lax.ppermute(x, axis, [(i, i ^ flip) for i in range(size)])]
    pallas_call x5 -> x7, Pallas kernels: 10.1 us -> 10.6 us  [increment_rows(): pl.pallas_call(kernel, out_shape=[jax.ShapeDtypeStruct(out, F32 if send i...]
    ppermute x13 -> x12, starting transfers between devices: 14.7 us -> 14.8 us  [swap(): return lax.ppermute(x, axis, [(i, i ^ flip) for i in range(size)])]
  transfers between devices with their start and end apart: 13 -> 12, of which waited for: 3 -> 3; matrix products, arithmetic and copies ran while one was open for 3% -> 3% of each run, Pallas kernels for 28% -> 31%
where the time goes in v4:
time: 30.4 us; the launch traced here: 30.3 us
  starting transfers between devices  14.8 us (49%)
  Pallas kernels  11.6 us (38%)
  waiting for transfers between devices  2.14 us (7%)
  other arithmetic  0.92 us (3%)
  between operations  0.79 us (3%)
    ppermute x12, starting transfers between devices, swap(): return lax.ppermute(x, axis, [(i, i ^ flip) for i in range(size)])  14.8 us
    pallas_call x7, Pallas kernels, increment_rows(): pl.pallas_call(kernel, out_shape=[jax.ShapeDtypeStruct(out, F32 if send i...  10.6 us
    ppermute x12, waiting for transfers between devices, swap(): return lax.ppermute(x, axis, [(i, i ^ flip) for i in range(size)])  2.14 us
    concatenate x1, other arithmetic, local(): packed = jnp.concatenate([anom, innov], axis=0)  0.92 us
    pallas_call x1, Pallas kernels, add_up(): pl.pallas_call(kernel, out_shape=jax.ShapeDtypeStruct(own.shape, F32), in...  0.68 us
  transfers between devices with their start and end apart: 12, of which 3 were waited for; matrix products, arithmetic and copies ran while one was open for 3% of the time, Pallas kernels for 31%

profile of v4, /device:TPU:0, one launch (start us, length us, event | category | flops | bytes accessed | tf_op | source)
XLA Modules:
  0.0 30.3 jit_solution(17111355664171344571)
XLA Ops:
  0.0 3.0 %collective-permute-start.7 = (bf16[64,512]{1,0:T(8,128)(2,1)}, bf16[64,512]{1,0:T(8,128)(2,1)S(1)}, u32[]{:S(2)}, u32[]{:S(2)}) collective-permute-start(bf16[64,512]{1,0:T(8,128)(2,1)} %bitcast.3), channel_id=1, source_target_pairs={{0,1},{1,0},{2,3},{3,2},{4,5},{5,4},{6,7},{7,6},{8,9},{9,8},{10,11... | collective-permute-start | bytes 196616 | tf_op jit(solution)/shard_map/ppermute | solution.py:170
  3.0 0.9 %pad_maximum_fusion.refs_1_ = bf16[128,512]{1,0:T(8,128)(2,1)S(1)} fusion(bf16[64,512]{1,0:T(8,128)(2,1)} %bitcast.7, bf16[64,512]{1,0:T(8,128)(2,1)} %bitcast.4), kind=kLoop, calls=%fused_computation | loop fusion | flops 262144 | bytes 262144 | tf_op jit(solution)/shard_map/concatenate | solution.py:180
  3.9 1.6 %collective-permute-start = (bf16[128,512]{1,0:T(8,128)(2,1)S(1)}, bf16[128,512]{1,0:T(8,128)(2,1)S(1)}, u32[]{:S(2)}, u32[]{:S(2)}) collective-permute-start(bf16[128,512]{1,0:T(8,128)(2,1)S(1)} %pad_maximum_fusion.refs_1_), channel_id=1, source_target_pairs={{0,8},{4,12},{8,0},{12,4},{16,24},{20,28},{24,16},{28,20},{1,9},{5... | collective-permute-start | bytes 393224 | tf_op jit(solution)/shard_map/ppermute | solution.py:170
  5.5 1.5 %collective-permute-start.1 = (bf16[128,512]{1,0:T(8,128)(2,1)S(1)}, bf16[128,512]{1,0:T(8,128)(2,1)S(1)}, u32[]{:S(2)}, u32[]{:S(2)}) collective-permute-start(bf16[128,512]{1,0:T(8,128)(2,1)S(1)} %pad_maximum_fusion.refs_1_), channel_id=1, source_target_pairs={{0,16},{4,20},{8,24},{12,28},{16,0},{20,4},{24,8},{28,12},{1,17},{... | collective-permute-start | bytes 393224 | tf_op jit(solution)/shard_map/ppermute | solution.py:170
  7.0 0.5 %collective-permute-start.2 = (bf16[128,512]{1,0:T(8,128)(2,1)S(1)}, bf16[128,512]{1,0:T(8,128)(2,1)S(1)}, u32[]{:S(2)}, u32[]{:S(2)}) collective-permute-start(bf16[128,512]{1,0:T(8,128)(2,1)S(1)} %pad_maximum_fusion.refs_1_), channel_id=1, source_target_pairs={{0,24},{4,28},{8,16},{12,20},{16,8},{20,12},{24,0},{28,4},{1,25},{... | collective-permute-start | bytes 393224 | tf_op jit(solution)/shard_map/ppermute | solution.py:170
  7.5 0.0 copy-start.3
  7.5 2.7 %collective-permute-start.9 = (bf16[128,512]{1,0:T(8,128)(2,1)S(1)}, bf16[128,512]{1,0:T(8,128)(2,1)S(1)}, u32[]{:S(2)}, u32[]{:S(2)}) collective-permute-start(bf16[128,512]{1,0:T(8,128)(2,1)S(1)} %stack.1), channel_id=1, source_target_pairs={{0,2},{1,3},{2,0},{3,1},{4,6},{5,7},{6,4},{7,5},{8,10},{9,11},{10,... | collective-permute-start | bytes 393224 | tf_op jit(solution)/shard_map/ppermute | solution.py:170
  10.9 0.3 %pair_table.1.table_ref = f32[16,4096]{1,0:T(8,128)S(1)} custom-call(s32[1,512]{1,0:T(1,128)S(1)} %copy-done.1, s32[1,512]{1,0:T(1,128)S(1)} %copy-done.2, s32[1,512]{1,0:T(1,128)S(1)} %copy-done.3, s32[1,1]{1,0:T(1,128)S(6)} %copy.7.count_ref), custom_call_target="tpu_custom_call" | custom-call | tf_op jit(solution)/shard_map/pair_table/pallas_call | solution.py:39
  11.2 0.6 %collective-permute-start.4 = (bf16[128,512]{1,0:T(8,128)(2,1)S(1)}, bf16[128,512]{1,0:T(8,128)(2,1)S(1)}, u32[]{:S(2)}, u32[]{:S(2)}) collective-permute-start(bf16[128,512]{1,0:T(8,128)(2,1)S(1)} %collective-permute-done.refs_2_), channel_id=1, source_target_pairs={{0,4},{4,0},{8,12},{12,8},{16,20},{20,16},{24,28},{28,24},{1,5},{5... | collective-permute-start | bytes 393224 | tf_op jit(solution)/shard_map/ppermute | solution.py:170
  11.8 1.5 %collective-permute-done.1.refs_3_.refs_1_ = bf16[128,512]{1,0:T(8,128)(2,1)S(1)} collective-permute-done((bf16[128,512]{1,0:T(8,128)(2,1)S(1)}, bf16[128,512]{1,0:T(8,128)(2,1)S(1)}, u32[]{:S(2)}, u32[]{:S(2)}) %collective-permute-start.1) | collective-permute-done | bytes 131104 | tf_op jit(solution)/shard_map/ppermute | solution.py:170
  13.3 0.5 %collective-permute-start.6 = (bf16[128,512]{1,0:T(8,128)(2,1)S(1)}, bf16[128,512]{1,0:T(8,128)(2,1)S(1)}, u32[]{:S(2)}, u32[]{:S(2)}) collective-permute-start(bf16[128,512]{1,0:T(8,128)(2,1)S(1)} %collective-permute-done.2.refs_4_.refs_2_), channel_id=1, source_target_pairs={{0,4},{4,0},{8,12},{12,8},{16,20},{20,16},{24,28},{28,24},{1,5},{5... | collective-permute-start | bytes 393224 | tf_op jit(solution)/shard_map/ppermute | solution.py:170
  13.8 0.8 %increment_rows.8.refs_3_ = f32[512,64]{1,0:T(8,128)S(1)} custom-call(f32[16,4096]{1,0:T(8,128)S(1)} %pair_table.1.table_ref, bf16[64,512]{1,0:T(8,128)(2,1)S(1)} %collective-permute-done.7.refs_0_.refs_1_, bf16[128,512]{1,0:T(8,128)(2,1)S(1)} %pad_maximum_fusion.refs_1_, bf16[128,512]{1,0:T(8,128)(2,1)S(1)} %collective-permute-done.refs_2_), custom_call_target="tpu_custom_call" | custom-call | flops 536870912 | bytes 262144 | tf_op jit(solution)/shard_map/increment_rows/pallas_call | solution.py:112
  14.5 0.8 %increment_rows.9.refs_5_ = f32[512,64]{1,0:T(8,128)S(1)} custom-call(f32[16,4096]{1,0:T(8,128)S(1)} %pair_table.1.table_ref, bf16[64,512]{1,0:T(8,128)(2,1)S(1)} %collective-permute-done.7.refs_0_.refs_1_, bf16[128,512]{1,0:T(8,128)(2,1)S(1)} %collective-permute-done.1.refs_3_.refs_1_, bf16[128,512]{1,0:T(8,128)(2,1)S(1)} %collective-permute-done.2.refs_4_.refs_2_, ...), custom_call_target="tpu_custom_call" | custom-call | flops 536870912 | bytes 262144 | tf_op jit(solution)/shard_map/increment_rows/pallas_call | solution.py:112
  15.3 2.4 %increment_rows.11 = (f32[512,64]{1,0:T(8,128)S(1)}, f32[512,64]{1,0:T(8,128)S(1)}) custom-call(f32[16,4096]{1,0:T(8,128)S(1)} %pair_table.1.table_ref, bf16[128,512]{1,0:T(8,128)(2,1)S(1)} %collective-permute-done.9.refs_0_, bf16[128,512]{1,0:T(8,128)(2,1)S(1)} %pad_maximum_fusion.refs_1_, bf16[128,512]{1,0:T(8,128)(2,1)S(1)} %collective-permute-done.refs_2_, ...), custom_call_target="tpu_custom_call" | custom-call | flops 2147483648 | bytes 524288 | tf_op jit(solution)/shard_map/increment_rows/pallas_call | solution.py:112
  17.8 1.4 %increment_rows.13 = bf16[64,512]{1,0:T(8,128)(2,1)S(1)} custom-call(f32[16,4096]{1,0:T(8,128)S(1)} %pair_table.1.table_ref, bf16[128,512]{1,0:T(8,128)(2,1)S(1)} %collective-permute-done.9.refs_0_, bf16[128,512]{1,0:T(8,128)(2,1)S(1)} %collective-permute-done.3.refs_5_.refs_1_, bf16[128,512]{1,0:T(8,128)(2,1)S(1)} %collective-permute-done.4.refs_6_.refs_2_, ...), custom_call_target="tpu_custom_call" | custom-call | flops 1073741824 | bytes 524288 | tf_op jit(solution)/shard_map/increment_rows/pallas_call | solution.py:112
  19.1 2.6 %collective-permute-start.11 = (bf16[64,512]{1,0:T(8,128)(2,1)S(1)}, bf16[64,512]{1,0:T(8,128)(2,1)S(1)}, u32[]{:S(2)}, u32[]{:S(2)}) collective-permute-start(bf16[64,512]{1,0:T(8,128)(2,1)S(1)} %increment_rows.13), channel_id=1, source_target_pairs={{0,3},{1,2},{2,1},{3,0},{4,7},{5,6},{6,5},{7,4},{8,11},{9,10},{10,... | collective-permute-start | bytes 196616 | tf_op jit(solution)/shard_map/ppermute | solution.py:170
  21.8 1.4 %increment_rows.12 = bf16[64,512]{1,0:T(8,128)(2,1)S(1)} custom-call(f32[16,4096]{1,0:T(8,128)S(1)} %pair_table.1.table_ref, bf16[128,512]{1,0:T(8,128)(2,1)S(1)} %collective-permute-done.9.refs_0_, bf16[128,512]{1,0:T(8,128)(2,1)S(1)} %collective-permute-done.3.refs_5_.refs_1_, bf16[128,512]{1,0:T(8,128)(2,1)S(1)} %collective-permute-done.4.refs_6_.refs_2_, ...), custom_call_target="tpu_custom_call" | custom-call | flops 1073741824 | bytes 524288 | tf_op jit(solution)/shard_map/increment_rows/pallas_call | solution.py:112
  23.2 0.0 collective-permute-start.10
  23.2 1.4 %increment_rows.10 = bf16[64,512]{1,0:T(8,128)(2,1)S(1)} custom-call(f32[16,4096]{1,0:T(8,128)S(1)} %pair_table.1.table_ref, bf16[64,512]{1,0:T(8,128)(2,1)S(1)} %collective-permute-done.7.refs_0_.refs_1_, bf16[128,512]{1,0:T(8,128)(2,1)S(1)} %collective-permute-done.3.refs_5_.refs_1_, bf16[128,512]{1,0:T(8,128)(2,1)S(1)} %collective-permute-done.4.refs_6_.refs_2_, ...), custom_call_target="tpu_custom_call" | custom-call | flops 1073741824 | bytes 524288 | tf_op jit(solution)/shard_map/increment_rows/pallas_call | solution.py:112
  24.6 1.8 %collective-permute-start.8 = (bf16[64,512]{1,0:T(8,128)(2,1)S(1)}, bf16[64,512]{1,0:T(8,128)(2,1)S(1)}, u32[]{:S(2)}, u32[]{:S(2)}) collective-permute-start(bf16[64,512]{1,0:T(8,128)(2,1)S(1)} %increment_rows.10), channel_id=1, source_target_pairs={{0,1},{1,0},{2,3},{3,2},{4,5},{5,4},{6,7},{7,6},{8,9},{9,8},{10,11... | collective-permute-start | bytes 196616 | tf_op jit(solution)/shard_map/ppermute | solution.py:170
  26.4 2.5 %increment_rows.7.refs_0_ = f32[64,512]{1,0:T(8,128)S(1)} custom-call(f32[16,4096]{1,0:T(8,128)S(1)} %pair_table.1.table_ref, bf16[64,512]{1,0:T(8,128)(2,1)S(1)} %bitcast.6, bf16[128,512]{1,0:T(8,128)(2,1)S(1)} %pad_maximum_fusion.refs_1_, bf16[128,512]{1,0:T(8,128)(2,1)S(1)} %collective-permute-done.refs_2_, ...), custom_call_target="tpu_custom_call" | custom-call | flops 2147483648 | bytes 1048576 | tf_op jit(solution)/shard_map/increment_rows/pallas_call | solution.py:112
  28.9 0.2 collective-permute-done.10.refs_2_
  29.2 0.4 %collective-permute-done.8.refs_1_ = bf16[64,512]{1,0:T(8,128)(2,1)S(1)} collective-permute-done((bf16[64,512]{1,0:T(8,128)(2,1)S(1)}, bf16[64,512]{1,0:T(8,128)(2,1)S(1)}, u32[]{:S(2)}, u32[]{:S(2)}) %collective-permute-start.8) | collective-permute-done | bytes 65568 | tf_op jit(solution)/shard_map/ppermute | solution.py:170
  29.6 0.7 %add_up.1 = f32[64,512]{1,0:T(8,128)} custom-call(f32[64,512]{1,0:T(8,128)S(1)} %increment_rows.7.refs_0_, bf16[64,512]{1,0:T(8,128)(2,1)S(1)} %collective-permute-done.8.refs_1_, bf16[64,512]{1,0:T(8,128)(2,1)S(1)} %collective-permute-done.10.refs_2_, bf16[64,512]{1,0:T(8,128)(2,1)S(1)} %collective-permute-done.11.refs_3_), custom_call_target="tpu_custom_call" | custom-call | tf_op jit(solution)/shard_map/add_up/pallas_call | solution.py:159
  (19 shorter events, 0.1 us)
Async XLA Ops:
  0.0 7.5 %collective-permute-start.7 = (bf16[64,512]{1,0:T(8,128)(2,1)}, bf16[64,512]{1,0:T(8,128)(2,1)S(1)}, u32[]{:S(2)}, u32[]{:S(2)}) collective-permute-start(bf16[64,512]{1,0:T(8,128)(2,1)} %bitcast.3), channel_id=1, source_target_pairs={{0,1},{1,0},{2,3},{3,2},{4,5},{5,4},{6,7},{7,6},{8,9},{9,8},{10,11... | collective-permute-start | bytes 196616 | tf_op jit(solution)/shard_map/ppermute | solution.py:170
  3.0 4.5 %copy-start = (bf16[512,64]{0,1:T(8,128)(2,1)S(1)}, bf16[512,64]{0,1:T(8,128)(2,1)}, u32[]{:S(2)}) copy-start(bf16[512,64]{0,1:T(8,128)(2,1)} %param.6) | copy-start | bytes 196612
  3.9 7.3 %collective-permute-start = (bf16[128,512]{1,0:T(8,128)(2,1)S(1)}, bf16[128,512]{1,0:T(8,128)(2,1)S(1)}, u32[]{:S(2)}, u32[]{:S(2)}) collective-permute-start(bf16[128,512]{1,0:T(8,128)(2,1)S(1)} %pad_maximum_fusion.refs_1_), channel_id=1, source_target_pairs={{0,8},{4,12},{8,0},{12,4},{16,24},{20,28},{24,16},{28,20},{1,9},{5... | collective-permute-start | bytes 393224 | tf_op jit(solution)/shard_map/ppermute | solution.py:170
  5.5 7.8 %collective-permute-start.1 = (bf16[128,512]{1,0:T(8,128)(2,1)S(1)}, bf16[128,512]{1,0:T(8,128)(2,1)S(1)}, u32[]{:S(2)}, u32[]{:S(2)}) collective-permute-start(bf16[128,512]{1,0:T(8,128)(2,1)S(1)} %pad_maximum_fusion.refs_1_), channel_id=1, source_target_pairs={{0,16},{4,20},{8,24},{12,28},{16,0},{20,4},{24,8},{28,12},{1,17},{... | collective-permute-start | bytes 393224 | tf_op jit(solution)/shard_map/ppermute | solution.py:170
  7.0 6.3 %collective-permute-start.2 = (bf16[128,512]{1,0:T(8,128)(2,1)S(1)}, bf16[128,512]{1,0:T(8,128)(2,1)S(1)}, u32[]{:S(2)}, u32[]{:S(2)}) collective-permute-start(bf16[128,512]{1,0:T(8,128)(2,1)S(1)} %pad_maximum_fusion.refs_1_), channel_id=1, source_target_pairs={{0,24},{4,28},{8,16},{12,20},{16,8},{20,12},{24,0},{28,4},{1,25},{... | collective-permute-start | bytes 393224 | tf_op jit(solution)/shard_map/ppermute | solution.py:170
  7.5 3.4 %copy-start.1 = (s32[1,512]{1,0:T(1,128)S(1)}, s32[1,512]{1,0:T(1,128)}, u32[]{:S(2)}) copy-start(s32[1,512]{1,0:T(1,128)} %rows_ref.1) | copy-start | bytes 6148
  7.5 3.4 %copy-start.2 = (s32[1,512]{1,0:T(1,128)S(1)}, s32[1,512]{1,0:T(1,128)}, u32[]{:S(2)}) copy-start(s32[1,512]{1,0:T(1,128)} %cols_ref.1) | copy-start | bytes 6148
  7.5 3.4 %copy-start.3 = (s32[1,512]{1,0:T(1,128)S(1)}, s32[1,512]{1,0:T(1,128)}, u32[]{:S(2)}) copy-start(s32[1,512]{1,0:T(1,128)} %dist_ref.1) | copy-start | bytes 6148
  7.5 7.8 %collective-permute-start.9 = (bf16[128,512]{1,0:T(8,128)(2,1)S(1)}, bf16[128,512]{1,0:T(8,128)(2,1)S(1)}, u32[]{:S(2)}, u32[]{:S(2)}) collective-permute-start(bf16[128,512]{1,0:T(8,128)(2,1)S(1)} %stack.1), channel_id=1, source_target_pairs={{0,2},{1,3},{2,0},{3,1},{4,6},{5,7},{6,4},{7,5},{8,10},{9,11},{10,... | collective-permute-start | bytes 393224 | tf_op jit(solution)/shard_map/ppermute | solution.py:170
  10.2 7.5 %collective-permute-start.3 = (bf16[128,512]{1,0:T(8,128)(2,1)S(1)}, bf16[128,512]{1,0:T(8,128)(2,1)S(1)}, u32[]{:S(2)}, u32[]{:S(2)}) collective-permute-start(bf16[128,512]{1,0:T(8,128)(2,1)S(1)} %pad_maximum_fusion.refs_1_), channel_id=1, source_target_pairs={{0,4},{4,0},{8,12},{12,8},{16,20},{20,16},{24,28},{28,24},{1,5},{5... | collective-permute-start | bytes 393224 | tf_op jit(solution)/shard_map/ppermute | solution.py:170
  11.2 6.5 %collective-permute-start.4 = (bf16[128,512]{1,0:T(8,128)(2,1)S(1)}, bf16[128,512]{1,0:T(8,128)(2,1)S(1)}, u32[]{:S(2)}, u32[]{:S(2)}) collective-permute-start(bf16[128,512]{1,0:T(8,128)(2,1)S(1)} %collective-permute-done.refs_2_), channel_id=1, source_target_pairs={{0,4},{4,0},{8,12},{12,8},{16,20},{20,16},{24,28},{28,24},{1,5},{5... | collective-permute-start | bytes 393224 | tf_op jit(solution)/shard_map/ppermute | solution.py:170
  13.3 4.5 %collective-permute-start.5 = (bf16[128,512]{1,0:T(8,128)(2,1)S(1)}, bf16[128,512]{1,0:T(8,128)(2,1)S(1)}, u32[]{:S(2)}, u32[]{:S(2)}) collective-permute-start(bf16[128,512]{1,0:T(8,128)(2,1)S(1)} %collective-permute-done.1.refs_3_.refs_1_), channel_id=1, source_target_pairs={{0,4},{4,0},{8,12},{12,8},{16,20},{20,16},{24,28},{28,24},{1,5},{5... | collective-permute-start | bytes 393224 | tf_op jit(solution)/shard_map/ppermute | solution.py:170
  13.3 4.5 %collective-permute-start.6 = (bf16[128,512]{1,0:T(8,128)(2,1)S(1)}, bf16[128,512]{1,0:T(8,128)(2,1)S(1)}, u32[]{:S(2)}, u32[]{:S(2)}) collective-permute-start(bf16[128,512]{1,0:T(8,128)(2,1)S(1)} %collective-permute-done.2.refs_4_.refs_2_), channel_id=1, source_target_pairs={{0,4},{4,0},{8,12},{12,8},{16,20},{20,16},{24,28},{28,24},{1,5},{5... | collective-permute-start | bytes 393224 | tf_op jit(solution)/shard_map/ppermute | solution.py:170
  19.1 9.8 %collective-permute-start.11 = (bf16[64,512]{1,0:T(8,128)(2,1)S(1)}, bf16[64,512]{1,0:T(8,128)(2,1)S(1)}, u32[]{:S(2)}, u32[]{:S(2)}) collective-permute-start(bf16[64,512]{1,0:T(8,128)(2,1)S(1)} %increment_rows.13), channel_id=1, source_target_pairs={{0,3},{1,2},{2,1},{3,0},{4,7},{5,6},{6,5},{7,4},{8,11},{9,10},{10,... | collective-permute-start | bytes 196616 | tf_op jit(solution)/shard_map/ppermute | solution.py:170
  23.2 6.0 %collective-permute-start.10 = (bf16[64,512]{1,0:T(8,128)(2,1)S(1)}, bf16[64,512]{1,0:T(8,128)(2,1)S(1)}, u32[]{:S(2)}, u32[]{:S(2)}) collective-permute-start(bf16[64,512]{1,0:T(8,128)(2,1)S(1)} %increment_rows.12), channel_id=1, source_target_pairs={{0,2},{1,3},{2,0},{3,1},{4,6},{5,7},{6,4},{7,5},{8,10},{9,11},{10,... | collective-permute-start | bytes 196616 | tf_op jit(solution)/shard_map/ppermute | solution.py:170
  24.6 5.0 %collective-permute-start.8 = (bf16[64,512]{1,0:T(8,128)(2,1)S(1)}, bf16[64,512]{1,0:T(8,128)(2,1)S(1)}, u32[]{:S(2)}, u32[]{:S(2)}) collective-permute-start(bf16[64,512]{1,0:T(8,128)(2,1)S(1)} %increment_rows.10), channel_id=1, source_target_pairs={{0,1},{1,0},{2,3},{3,2},{4,5},{5,4},{6,7},{7,6},{8,9},{9,8},{10,11... | collective-permute-start | bytes 196616 | tf_op jit(solution)/shard_map/ppermute | solution.py:170

commit v5 on v4

--- a/solution.py
+++ b/solution.py
@@ -8,8 +8,7 @@
 BLK = 128
 TAPER_CELLS = 8
 DIST_SCALE = 4.0
-DMAX = 8
-HALF = 256
+HALF = BLK // 2
 SMALL = pltpu.CompilerParams(vmem_limit_bytes=4 * 2**20)
 
 F32 = jnp.float32
@@ -30,7 +29,7 @@
         left = jnp.where(row_place == (rows_ref[...] ^ row_flip), code, 0.0).astype(BF16)
         right = jnp.where(col_place == (cols_ref[...] ^ col_flip), 1.0, 0.0).astype(BF16)
         table = lax.dot_general(left, right, (((1,), (1,)), ((), ())), preferred_element_type=F32)
-        spread = lax.broadcasted_iota(jnp.int32, (col_blocks, col_blocks * BLK), 1) // BLK
+        spread = lax.broadcasted_iota(jnp.int32, (col_blocks, col_blocks * HALF), 1) // HALF
         spread = (spread == lax.broadcasted_iota(jnp.int32, spread.shape, 0)).astype(F32).astype(BF16)
         wide = jnp.dot(table.astype(BF16), spread, preferred_element_type=F32)
         weight = jnp.exp((1.0 - wide) / DIST_SCALE) * (1.0 / (members - 1))
@@ -38,7 +37,7 @@
 
     return pl.pallas_call(
         kernel,
-        out_shape=jax.ShapeDtypeStruct((row_blocks, col_blocks * BLK), F32),
+        out_shape=jax.ShapeDtypeStruct((row_blocks, col_blocks * HALF), F32),
         in_specs=[VMEM, VMEM, VMEM, SMEM],
         out_specs=VMEM,
         compiler_params=SMALL,
@@ -46,12 +45,71 @@
     )(pair_rows, pair_cols, pair_dist, pair_counts)
 
 
-def increment_rows(table, places, row_flips, members, col_parts, col_flips, before, send):
+def halves_apart(packed):
+    height, cells = packed.shape
+    wide = cells // 2
+
+    def kernel(in_ref, out_ref):
+        source = lax.broadcasted_iota(jnp.int32, (cells, cells), 0)
+        lane = lax.broadcasted_iota(jnp.int32, (cells, cells), 1)
+        inner = lane % wide
+        wanted = inner // HALF * BLK + lane // wide * HALF + inner % HALF
+        order = (source == wanted).astype(F32).astype(BF16)
+        out_ref[...] = jnp.dot(in_ref[...], order, preferred_element_type=F32).astype(BF16)
+
+    return pl.pallas_call(
+        kernel,
+        out_shape=jax.ShapeDtypeStruct((height, cells), BF16),
+        in_specs=[VMEM],
+        out_specs=VMEM,
+        compiler_params=SMALL,
+        name="halves_apart",
+    )(packed)
+
+
+def fade(shape, axis, rising):
+    place = lax.broadcasted_iota(jnp.int32, shape, axis) % HALF
+    return jnp.exp((place - HALF if rising else -place).astype(F32) / TAPER_CELLS)
+
+
+def half_states(col_parts, members):
+    columns = col_parts[0].shape[0] - members
+    cells = col_parts[0].shape[1]
+    wide = cells // 2
+    blocks = cells // BLK
+    count = len(col_parts)
+
+    def kernel(*refs):
+        owner = lax.broadcasted_iota(jnp.int32, (1, wide), 1) // HALF
+        for col_ref, out_ref in zip(refs[:count], refs[count:]):
+            for half in range(2):
+                span = pl.ds(half * wide, wide)
+                right = col_ref[pl.ds(0, members), span]
+                innov = col_ref[pl.ds(members, columns), span].astype(F32)
+                innov = (innov * fade((1, wide), 1, half == 0)).astype(BF16)
+                spaced = jnp.concatenate(
+                    [right * (owner == q).astype(F32).astype(BF16) for q in range(blocks)], axis=0
+                )
+                out_ref[pl.ds(half * columns, columns), :] = lax.dot_general(
+                    innov, spaced, (((1,), (1,)), ((), ())), preferred_element_type=F32
+                )
+
+    return pl.pallas_call(
+        kernel,
+        out_shape=[jax.ShapeDtypeStruct((2 * columns, blocks * members), F32)] * count,
+        in_specs=[VMEM] * count,
+        out_specs=[VMEM] * count,
+        compiler_params=SMALL,
+        name="half_states",
+    )(*col_parts)
+
+
+def increment_rows(table, places, row_flips, members, col_parts, states, col_flips, before, send):
     cells = col_parts[0].shape[1]
     columns = col_parts[0].shape[0] - members
     blocks = cells // BLK
-    halves = cells // HALF
-    per_half = HALF // BLK
+    wide = cells // 2
+    lanes = 2 * members
     row_stacks = []
     for stacked, _ in places:
         if all(stacked is not known for known in row_stacks):
@@ -63,34 +121,34 @@
 
     def kernel(table_ref, *refs):
         refs = list(refs)
-        row_refs, col_refs, before_refs, out_refs = (
-            [refs.pop(0) for _ in range(n)] for n in (n_stack, n_col, n_before, n_row)
-        )
-        taper_ref, left_ref, total_ref = refs
-        gap = lax.broadcasted_iota(jnp.int32, (BLK, BLK), 0) - lax.broadcasted_iota(jnp.int32, (BLK, BLK), 1)
-        taper_ref[...] = jnp.exp(-jnp.abs(gap).astype(F32) / TAPER_CELLS)
+        row_refs, col_refs, state_refs, before_refs, out_refs = (
+            [refs.pop(0) for _ in range(n)] for n in (n_stack, n_col, n_col, n_before, n_row)
+        )
+        tile_ref, fade_ref, left_ref, total_ref, sum_ref = refs
+        gap = lax.broadcasted_iota(jnp.int32, (HALF, wide), 0)
+        gap = gap - lax.broadcasted_iota(jnp.int32, (HALF, wide), 1) % HALF
+        tile_ref[...] = jnp.exp(-jnp.abs(gap).astype(F32) / TAPER_CELLS)
+        for half in range(2):
+            fade_ref[half] = fade((HALF, columns), 0, half == 0)
         for row in range(n_row):
-            left_ref[...] = row_refs[spots[row][0]][pl.ds(spots[row][1], members), :].T
-            sum_ref = total_ref if send is not None else out_refs[row]
+            left = row_refs[spots[row][0]][pl.ds(spots[row][1], members), :].T
+            for a in range(blocks):
+                for half in range(2):
+                    left_ref[half, pl.ds(a * HALF, HALF), :] = left[a * BLK + half * HALF : a * BLK + (half + 1) * HALF]
+            first_row = row_flips[row] * blocks
             for col in range(n_col):
-                total = None
-                for half in range(halves):
-                    span = pl.ds(half * HALF, HALF)
+                weights = [
+                    tile_ref[...] * table_ref[pl.ds(first_row + a, 1), pl.ds(col_flips[col] * wide, wide)]
+                    for a in range(blocks)
+                ]
+                for half in range(2):
+                    span = pl.ds(half * wide, wide)
                     right = col_refs[col][pl.ds(0, members), span]
                     innov = col_refs[col][pl.ds(members, columns), span]
-                    products = jnp.dot(left_ref[...], right, preferred_element_type=F32)
-                    first_row = row_flips[row] * blocks
-                    first_col = col_flips[col] * blocks + half * per_half
+                    products = jnp.dot(left_ref[half], right, preferred_element_type=F32)
                     tapered = jnp.concatenate(
                         [
-                            jnp.concatenate(
-                                [
-                                    products[a * BLK : (a + 1) * BLK, q * BLK : (q + 1) * BLK]
-                                    * (taper_ref[...] * table_ref[pl.ds(first_row + a, 1), pl.ds((first_col + q) * BLK, BLK)])
-                                    for q in range(per_half)
-                                ],
-                                axis=1,
-                            ).astype(BF16)
+                            (products[a * HALF : (a + 1) * HALF] * weights[a]).astype(BF16)
                             for a in range(blocks)
                         ],
                         axis=0,
@@ -98,12 +156,31 @@
                     applied = lax.dot_general(
                         tapered, innov, (((1,), (1,)), ((), ())), preferred_element_type=F32
                     )
-                    total = applied if total is None else total + applied
-                if col > 0:
-                    total = total + sum_ref[...]
-                elif n_before > 0:
-                    total = total + before_refs[row][...]
-                sum_ref[...] = total
+                    total_ref[half] = applied if col == 0 else total_ref[half] + applied
+            dest_ref = sum_ref if send is not None else out_refs[row]
+            for a in range(blocks):
+                for half in range(2):
+                    cross = None
+                    for col in range(n_col):
+                        for group in range(blocks * members // lanes):
+                            start = col_flips[col] * wide + group * lanes
+                            term = (
+                                state_refs[col][pl.ds((1 - half) * columns, columns), pl.ds(group * lanes, lanes)]
+                                * table_ref[pl.ds(first_row + a, 1), pl.ds(start, lanes)]
+                            )
+                            cross = term if cross is None else cross + term
+                    cross = (cross[:, :members] + cross[:, members:]).astype(BF16)
+                    far_side = lax.dot_general(
+                        left_ref[half, pl.ds(a * HALF, HALF), :],
+                        cross,
+                        (((1,), (1,)), ((), ())),
+                        preferred_element_type=F32,
+                    )
+                    total = total_ref[half, pl.ds(a * HALF, HALF), :] + far_side * fade_ref[half]
+                    cells_here = pl.ds(a * BLK + half * HALF, HALF)
+                    if n_before > 0:
+                        total = total + before_refs[row][cells_here, :]
+                    dest_ref[cells_here, :] = total
             if send is not None:
                 out_refs[row][...] = sum_ref[...].astype(send).T
 
@@ -112,11 +189,13 @@
     return pl.pallas_call(
         kernel,
         out_shape=[jax.ShapeDtypeStruct(out, F32 if send is None else send)] * n_row,
-        in_specs=[VMEM] + [VMEM] * (n_stack + n_col + n_before),
+        in_specs=[VMEM] * (1 + n_stack + 2 * n_col + n_before),
         out_specs=[VMEM] * n_row,
         scratch_shapes=[
-            pltpu.VMEM((BLK, BLK), F32),
-            pltpu.VMEM((cells, members), BF16),
+            pltpu.VMEM((HALF, wide), F32),
+            pltpu.VMEM((2, HALF, columns), F32),
+            pltpu.VMEM((2, wide, members), BF16),
+            pltpu.VMEM((2, wide, columns), F32),
             pltpu.VMEM((cells, columns), F32),
         ],
         compiler_params=pltpu.CompilerParams(vmem_limit_bytes=24 * 2**20),
@@ -126,7 +205,7 @@
             transcendentals=BLK * BLK,
         ),
         name="increment_rows",
-    )(table, *row_stacks, *col_parts, *before)
+    )(table, *row_stacks, *col_parts, *states, *before)
 
 
 def stack(parts):
@@ -177,7 +256,7 @@
         per_dev = anomalies.shape[0] // BLK
         members = anomalies.shape[1]
         anom, innov = anomalies.T, innovations.T
-        packed = jnp.concatenate([anom, innov], axis=0)
+        packed = halves_apart(jnp.concatenate([anom, innov], axis=0))
         near = list(range(0, n_rows, 2))
         far = [flip + 1 for flip in near]
         places, held = [(anom, 0)], [anom]
@@ -194,22 +273,36 @@
         far_parts = [swap(part, "rows", n_rows, 1) for part in near_parts]
         others = list(range(1, n_cols))
         early = len(near) // 2
-        first = increment_rows(table, places[1:2], [1], members, near_parts[:early], near[:early], [], None)
+        near_states = half_states(near_parts[:early], members) + half_states(near_parts[early:], members)
         before = dict(
             zip(
                 others[:1],
-                increment_rows(table, places[1:2], [1], members, near_parts[early:], near[early:], first, None),
+                increment_rows(table, places[1:2], [1], members, near_parts, near_states, near, [], None),
             )
         )
         before.update(
-            zip(others[1:], increment_rows(table, places[2:], others[1:], members, near_parts, near, [], None))
-        )
+            zip(
+                others[1:],
+                increment_rows(table, places[2:], others[1:], members, near_parts, near_states, near, [], None),
+            )
+        )
+        far_states = half_states(far_parts, members)
         received = []
         for flip in others:
-            (part,) = increment_rows(table, [places[flip]], [flip], members, far_parts, far, [before[flip]], BF16)
+            (part,) = increment_rows(
+                table, [places[flip]], [flip], members, far_parts, far_states, far, [before[flip]], BF16
+            )
             received.append(swap(part, "cols", n_cols, flip))
         (own,) = increment_rows(
-            table, [places[0]], [0], members, near_parts + far_parts, near + far, [], F32
+            table,
+            [places[0]],
+            [0],
+            members,
+            near_parts + far_parts,
+            [*near_states, *far_states],
+            near + far,
+            [],
+            F32,
         )
         return add_up(own, received).T
 

time: 30.4 us -> 29.3 us (0.964)
  Pallas kernels: 11.6 us -> 9.52 us
  waiting for transfers between devices: 2.14 us -> 2.96 us
    pallas_call x7 -> x6, Pallas kernels: 10.6 us -> 7.29 us  [increment_rows(): pl.pallas_call(kernel, out_shape=[jax.ShapeDtypeStruct(out, F32 if send i...]
    pallas_call x0 -> x4, Pallas kernels: none -> 1.23 us  [the longest x3 0.99 us: half_states(): pl.pallas_call(kernel, out_shape=[jax.ShapeDtypeStruct((2 * columns, bloc...]
    ppermute x12, waiting for transfers between devices: 2.14 us -> 2.96 us  [swap(): return lax.ppermute(x, axis, [(i, i ^ flip) for i in range(size)])]
  transfers between devices with their start and end apart: 12 -> 12, of which waited for: 3 -> 4; matrix products, arithmetic and copies ran while one was open for 3% -> 3% of each run, Pallas kernels for 31% -> 25%
where the time goes in v5:
time: 29.3 us; the launch traced here: 29.1 us
  starting transfers between devices  14.9 us (51%)
  Pallas kernels  9.52 us (32%)
  waiting for transfers between devices  2.96 us (10%)
  other arithmetic  0.88 us (3%)
  between operations  0.82 us (3%)
    ppermute x12, starting transfers between devices, swap(): return lax.ppermute(x, axis, [(i, i ^ flip) for i in range(size)])  14.9 us
    pallas_call x6, Pallas kernels, increment_rows(): pl.pallas_call(kernel, out_shape=[jax.ShapeDtypeStruct(out, F32 if send i...  7.29 us
    ppermute x12, waiting for transfers between devices, swap(): return lax.ppermute(x, axis, [(i, i ^ flip) for i in range(size)])  2.96 us
    pallas_call x3, Pallas kernels, half_states(): pl.pallas_call(kernel, out_shape=[jax.ShapeDtypeStruct((2 * columns, bloc...  0.99 us
    concatenate x1, other arithmetic, local(): packed = halves_apart(jnp.concatenate([anom, innov], axis=0))  0.88 us
    pallas_call x1, Pallas kernels, add_up(): pl.pallas_call(kernel, out_shape=jax.ShapeDtypeStruct(own.shape, F32), in...  0.68 us
  transfers between devices with their start and end apart: 12, of which 4 were waited for; matrix products, arithmetic and copies ran while one was open for 3% of the time, Pallas kernels for 25%

profile of v5, /device:TPU:0, one launch (start us, length us, event | category | flops | bytes accessed | tf_op | source)
XLA Modules:
  0.0 29.1 jit_solution(3802700550619224443)
XLA Ops:
  0.0 3.0 %collective-permute-start.7 = (bf16[64,512]{1,0:T(8,128)(2,1)}, bf16[64,512]{1,0:T(8,128)(2,1)S(1)}, u32[]{:S(2)}, u32[]{:S(2)}) collective-permute-start(bf16[64,512]{1,0:T(8,128)(2,1)} %bitcast.3), channel_id=1, source_target_pairs={{0,1},{1,0},{2,3},{3,2},{4,5},{5,4},{6,7},{7,6},{8,9},{9,8},{10,11... | collective-permute-start | bytes 196616 | tf_op jit(solution)/shard_map/ppermute | solution.py:249
  3.0 0.9 %pad_maximum_fusion.in_ref = bf16[128,512]{1,0:T(8,128)(2,1)S(1)} fusion(bf16[64,512]{1,0:T(8,128)(2,1)} %bitcast.7, bf16[64,512]{1,0:T(8,128)(2,1)} %bitcast.4), kind=kLoop, calls=%fused_computation | loop fusion | flops 262144 | bytes 262144 | tf_op jit(solution)/shard_map/concatenate | solution.py:259
  4.2 1.6 %collective-permute-start = (bf16[128,512]{1,0:T(8,128)(2,1)S(1)}, bf16[128,512]{1,0:T(8,128)(2,1)S(1)}, u32[]{:S(2)}, u32[]{:S(2)}) collective-permute-start(bf16[128,512]{1,0:T(8,128)(2,1)S(1)} %halves_apart.1.refs_0_.refs_1_), channel_id=1, source_target_pairs={{0,8},{4,12},{8,0},{12,4},{16,24},{20,28},{24,16},{28,20},{1,9},{5... | collective-permute-start | bytes 393224 | tf_op jit(solution)/shard_map/ppermute | solution.py:249
  5.7 1.5 %collective-permute-start.1 = (bf16[128,512]{1,0:T(8,128)(2,1)S(1)}, bf16[128,512]{1,0:T(8,128)(2,1)S(1)}, u32[]{:S(2)}, u32[]{:S(2)}) collective-permute-start(bf16[128,512]{1,0:T(8,128)(2,1)S(1)} %halves_apart.1.refs_0_.refs_1_), channel_id=1, source_target_pairs={{0,16},{4,20},{8,24},{12,28},{16,0},{20,4},{24,8},{28,12},{1,17},{... | collective-permute-start | bytes 393224 | tf_op jit(solution)/shard_map/ppermute | solution.py:249
  7.2 0.5 %collective-permute-start.2 = (bf16[128,512]{1,0:T(8,128)(2,1)S(1)}, bf16[128,512]{1,0:T(8,128)(2,1)S(1)}, u32[]{:S(2)}, u32[]{:S(2)}) collective-permute-start(bf16[128,512]{1,0:T(8,128)(2,1)S(1)} %halves_apart.1.refs_0_.refs_1_), channel_id=1, source_target_pairs={{0,24},{4,28},{8,16},{12,20},{16,8},{20,12},{24,0},{28,4},{1,25},{... | collective-permute-start | bytes 393224 | tf_op jit(solution)/shard_map/ppermute | solution.py:249
  7.8 2.7 %collective-permute-start.9 = (bf16[128,512]{1,0:T(8,128)(2,1)S(1)}, bf16[128,512]{1,0:T(8,128)(2,1)S(1)}, u32[]{:S(2)}, u32[]{:S(2)}) collective-permute-start(bf16[128,512]{1,0:T(8,128)(2,1)S(1)} %stack.1), channel_id=1, source_target_pairs={{0,2},{1,3},{2,0},{3,1},{4,6},{5,7},{6,4},{7,5},{8,10},{9,11},{10,... | collective-permute-start | bytes 393224 | tf_op jit(solution)/shard_map/ppermute | solution.py:249
  11.1 0.3 %pair_table.1.table_ref = f32[16,2048]{1,0:T(8,128)S(1)} custom-call(s32[1,512]{1,0:T(1,128)S(1)} %copy-done.1, s32[1,512]{1,0:T(1,128)S(1)} %copy-done.2, s32[1,512]{1,0:T(1,128)S(1)} %copy-done.3, s32[1,1]{1,0:T(1,128)S(6)} %copy.7.count_ref), custom_call_target="tpu_custom_call" | custom-call | tf_op jit(solution)/shard_map/pair_table/pallas_call | solution.py:38
  11.4 0.3 half_states.3
  11.7 0.6 %collective-permute-start.4 = (bf16[128,512]{1,0:T(8,128)(2,1)S(1)}, bf16[128,512]{1,0:T(8,128)(2,1)S(1)}, u32[]{:S(2)}, u32[]{:S(2)}) collective-permute-start(bf16[128,512]{1,0:T(8,128)(2,1)S(1)} %collective-permute-done.refs_1_.refs_2_), channel_id=1, source_target_pairs={{0,4},{4,0},{8,12},{12,8},{16,20},{20,16},{24,28},{28,24},{1,5},{5... | collective-permute-start | bytes 393224 | tf_op jit(solution)/shard_map/ppermute | solution.py:249
  12.3 1.2 %collective-permute-done.1.refs_0_.refs_3_ = bf16[128,512]{1,0:T(8,128)(2,1)S(1)} collective-permute-done((bf16[128,512]{1,0:T(8,128)(2,1)S(1)}, bf16[128,512]{1,0:T(8,128)(2,1)S(1)}, u32[]{:S(2)}, u32[]{:S(2)}) %collective-permute-start.1) | collective-permute-done | bytes 131104 | tf_op jit(solution)/shard_map/ppermute | solution.py:249
  13.5 0.3 half_states.4
  13.8 0.6 %collective-permute-start.6 = (bf16[128,512]{1,0:T(8,128)(2,1)S(1)}, bf16[128,512]{1,0:T(8,128)(2,1)S(1)}, u32[]{:S(2)}, u32[]{:S(2)}) collective-permute-start(bf16[128,512]{1,0:T(8,128)(2,1)S(1)} %collective-permute-done.2.refs_1_.refs_4_), channel_id=1, source_target_pairs={{0,4},{4,0},{8,12},{12,8},{16,20},{20,16},{24,28},{28,24},{1,5},{5... | collective-permute-start | bytes 393224 | tf_op jit(solution)/shard_map/ppermute | solution.py:249
  14.4 1.0 %increment_rows.7.refs_9_ = f32[512,64]{1,0:T(8,128)S(1)} custom-call(f32[16,2048]{1,0:T(8,128)S(1)} %pair_table.1.table_ref, bf16[64,512]{1,0:T(8,128)(2,1)S(1)} %collective-permute-done.7.refs_0_.refs_1_, bf16[128,512]{1,0:T(8,128)(2,1)S(1)} %halves_apart.1.refs_0_.refs_1_, bf16[128,512]{1,0:T(8,128)(2,1)S(1)} %collective-permute-done.refs_1_.refs_2_, ...), custom_call_target="tpu_custom_call" | custom-call | flops 1073741824 | bytes 524288 | tf_op jit(solution)/shard_map/increment_rows/pallas_call | solution.py:189
  15.5 1.6 %increment_rows.9 = (f32[512,64]{1,0:T(8,128)S(1)}, f32[512,64]{1,0:T(8,128)S(1)}) custom-call(f32[16,2048]{1,0:T(8,128)S(1)} %pair_table.1.table_ref, bf16[128,512]{1,0:T(8,128)(2,1)S(1)} %collective-permute-done.9.refs_0_, bf16[128,512]{1,0:T(8,128)(2,1)S(1)} %halves_apart.1.refs_0_.refs_1_, bf16[128,512]{1,0:T(8,128)(2,1)S(1)} %collective-permute-done.refs_1_.refs_2_, ...), custom_call_target="tpu_custom_call" | custom-call | flops 2147483648 | bytes 524288 | tf_op jit(solution)/shard_map/increment_rows/pallas_call | solution.py:189
  17.1 0.4 %half_states.5 = (f32[128,256]{1,0:T(8,128)S(1)}, f32[128,256]{1,0:T(8,128)S(1)}, f32[128,256]{1,0:T(8,128)S(1)}, f32[128,256]{1,0:T(8,128)S(1)}) custom-call(bf16[128,512]{1,0:T(8,128)(2,1)S(1)} %collective-permute-done.3.refs_0_.refs_5_.refs_1_, bf16[128,512]{1,0:T(8,128)(2,1)S(1)} %collective-permute-done.4.refs_1_.refs_6_.refs_2_, ...), custom_call_target="tpu_custom_call" | custom-call | tf_op jit(solution)/shard_map/half_states/pallas_call | solution.py:97
  17.6 1.0 %increment_rows.11 = bf16[64,512]{1,0:T(8,128)(2,1)S(1)} custom-call(f32[16,2048]{1,0:T(8,128)S(1)} %pair_table.1.table_ref, bf16[128,512]{1,0:T(8,128)(2,1)S(1)} %collective-permute-done.9.refs_0_, bf16[128,512]{1,0:T(8,128)(2,1)S(1)} %collective-permute-done.3.refs_0_.refs_5_.refs_1_, bf16[128,512]{1,0:T(8,128)(2,1)S(1)} %collective-permute-done.4.refs_1_.refs_6_.refs_2_, ...), custom_call_target="tpu_custom_call" | custom-call | flops 1073741824 | bytes 524288 | tf_op jit(solution)/shard_map/increment_rows/pallas_call | solution.py:189
  18.6 2.7 %collective-permute-start.11 = (bf16[64,512]{1,0:T(8,128)(2,1)S(1)}, bf16[64,512]{1,0:T(8,128)(2,1)S(1)}, u32[]{:S(2)}, u32[]{:S(2)}) collective-permute-start(bf16[64,512]{1,0:T(8,128)(2,1)S(1)} %increment_rows.11), channel_id=1, source_target_pairs={{0,3},{1,2},{2,1},{3,0},{4,7},{5,6},{6,5},{7,4},{8,11},{9,10},{10,... | collective-permute-start | bytes 196616 | tf_op jit(solution)/shard_map/ppermute | solution.py:249
  21.3 1.0 %increment_rows.10 = bf16[64,512]{1,0:T(8,128)(2,1)S(1)} custom-call(f32[16,2048]{1,0:T(8,128)S(1)} %pair_table.1.table_ref, bf16[128,512]{1,0:T(8,128)(2,1)S(1)} %collective-permute-done.9.refs_0_, bf16[128,512]{1,0:T(8,128)(2,1)S(1)} %collective-permute-done.3.refs_0_.refs_5_.refs_1_, bf16[128,512]{1,0:T(8,128)(2,1)S(1)} %collective-permute-done.4.refs_1_.refs_6_.refs_2_, ...), custom_call_target="tpu_custom_call" | custom-call | flops 1073741824 | bytes 524288 | tf_op jit(solution)/shard_map/increment_rows/pallas_call | solution.py:189
  22.4 1.0 %increment_rows.8 = bf16[64,512]{1,0:T(8,128)(2,1)S(1)} custom-call(f32[16,2048]{1,0:T(8,128)S(1)} %pair_table.1.table_ref, bf16[64,512]{1,0:T(8,128)(2,1)S(1)} %collective-permute-done.7.refs_0_.refs_1_, bf16[128,512]{1,0:T(8,128)(2,1)S(1)} %collective-permute-done.3.refs_0_.refs_5_.refs_1_, ...), custom_call_target="tpu_custom_call" | custom-call | flops 1073741824 | bytes 524288 | tf_op jit(solution)/shard_map/increment_rows/pallas_call | solution.py:189
  23.4 1.8 %collective-permute-start.8 = (bf16[64,512]{1,0:T(8,128)(2,1)S(1)}, bf16[64,512]{1,0:T(8,128)(2,1)S(1)}, u32[]{:S(2)}, u32[]{:S(2)}) collective-permute-start(bf16[64,512]{1,0:T(8,128)(2,1)S(1)} %increment_rows.8), channel_id=1, source_target_pairs={{0,1},{1,0},{2,3},{3,2},{4,5},{5,4},{6,7},{7,6},{8,9},{9,8},{10,11... | collective-permute-start | bytes 196616 | tf_op jit(solution)/shard_map/ppermute | solution.py:249
  25.2 1.7 %increment_rows.6.refs_0_ = f32[64,512]{1,0:T(8,128)S(1)} custom-call(f32[16,2048]{1,0:T(8,128)S(1)} %pair_table.1.table_ref, bf16[64,512]{1,0:T(8,128)(2,1)S(1)} %bitcast.6, bf16[128,512]{1,0:T(8,128)(2,1)S(1)} %halves_apart.1.refs_0_.refs_1_, bf16[128,512]{1,0:T(8,128)(2,1)S(1)} %collective-permute-done.refs_1_.refs_2_, ...), custom_call_target="tpu_custom_call" | custom-call | flops 2147483648 | bytes 1048576 | tf_op jit(solution)/shard_map/increment_rows/pallas_call | solution.py:189
  26.9 1.3 %collective-permute-done.10.refs_2_ = bf16[64,512]{1,0:T(8,128)(2,1)S(1)} collective-permute-done((bf16[64,512]{1,0:T(8,128)(2,1)S(1)}, bf16[64,512]{1,0:T(8,128)(2,1)S(1)}, u32[]{:S(2)}, u32[]{:S(2)}) %collective-permute-start.10) | collective-permute-done | bytes 65568 | tf_op jit(solution)/shard_map/ppermute | solution.py:249
  28.2 0.3 collective-permute-done.8.refs_1_
  28.5 0.7 %add_up.1 = f32[64,512]{1,0:T(8,128)} custom-call(f32[64,512]{1,0:T(8,128)S(1)} %increment_rows.6.refs_0_, bf16[64,512]{1,0:T(8,128)(2,1)S(1)} %collective-permute-done.8.refs_1_, bf16[64,512]{1,0:T(8,128)(2,1)S(1)} %collective-permute-done.10.refs_2_, bf16[64,512]{1,0:T(8,128)(2,1)S(1)} %collective-permute-done.11.refs_3_), custom_call_target="tpu_custom_call" | custom-call | tf_op jit(solution)/shard_map/add_up/pallas_call | solution.py:238
  (22 shorter events, 0.5 us)
Async XLA Ops:
  0.0 7.7 %collective-permute-start.7 = (bf16[64,512]{1,0:T(8,128)(2,1)}, bf16[64,512]{1,0:T(8,128)(2,1)S(1)}, u32[]{:S(2)}, u32[]{:S(2)}) collective-permute-start(bf16[64,512]{1,0:T(8,128)(2,1)} %bitcast.3), channel_id=1, source_target_pairs={{0,1},{1,0},{2,3},{3,2},{4,5},{5,4},{6,7},{7,6},{8,9},{9,8},{10,11... | collective-permute-start | bytes 196616 | tf_op jit(solution)/shard_map/ppermute | solution.py:249
  3.9 3.8 %copy-start = (bf16[512,64]{0,1:T(8,128)(2,1)S(1)}, bf16[512,64]{0,1:T(8,128)(2,1)}, u32[]{:S(2)}) copy-start(bf16[512,64]{0,1:T(8,128)(2,1)} %param.6) | copy-start | bytes 196612
  4.2 7.3 %collective-permute-start = (bf16[128,512]{1,0:T(8,128)(2,1)S(1)}, bf16[128,512]{1,0:T(8,128)(2,1)S(1)}, u32[]{:S(2)}, u32[]{:S(2)}) collective-permute-start(bf16[128,512]{1,0:T(8,128)(2,1)S(1)} %halves_apart.1.refs_0_.refs_1_), channel_id=1, source_target_pairs={{0,8},{4,12},{8,0},{12,4},{16,24},{20,28},{24,16},{28,20},{1,9},{5... | collective-permute-start | bytes 393224 | tf_op jit(solution)/shard_map/ppermute | solution.py:249
  5.7 7.8 %collective-permute-start.1 = (bf16[128,512]{1,0:T(8,128)(2,1)S(1)}, bf16[128,512]{1,0:T(8,128)(2,1)S(1)}, u32[]{:S(2)}, u32[]{:S(2)}) collective-permute-start(bf16[128,512]{1,0:T(8,128)(2,1)S(1)} %halves_apart.1.refs_0_.refs_1_), channel_id=1, source_target_pairs={{0,16},{4,20},{8,24},{12,28},{16,0},{20,4},{24,8},{28,12},{1,17},{... | collective-permute-start | bytes 393224 | tf_op jit(solution)/shard_map/ppermute | solution.py:249
  7.2 6.3 %collective-permute-start.2 = (bf16[128,512]{1,0:T(8,128)(2,1)S(1)}, bf16[128,512]{1,0:T(8,128)(2,1)S(1)}, u32[]{:S(2)}, u32[]{:S(2)}) collective-permute-start(bf16[128,512]{1,0:T(8,128)(2,1)S(1)} %halves_apart.1.refs_0_.refs_1_), channel_id=1, source_target_pairs={{0,24},{4,28},{8,16},{12,20},{16,8},{20,12},{24,0},{28,4},{1,25},{... | collective-permute-start | bytes 393224 | tf_op jit(solution)/shard_map/ppermute | solution.py:249
  7.7 3.4 %copy-start.1 = (s32[1,512]{1,0:T(1,128)S(1)}, s32[1,512]{1,0:T(1,128)}, u32[]{:S(2)}) copy-start(s32[1,512]{1,0:T(1,128)} %rows_ref.1) | copy-start | bytes 6148
  7.7 3.4 %copy-start.2 = (s32[1,512]{1,0:T(1,128)S(1)}, s32[1,512]{1,0:T(1,128)}, u32[]{:S(2)}) copy-start(s32[1,512]{1,0:T(1,128)} %cols_ref.1) | copy-start | bytes 6148
  7.7 3.4 %copy-start.3 = (s32[1,512]{1,0:T(1,128)S(1)}, s32[1,512]{1,0:T(1,128)}, u32[]{:S(2)}) copy-start(s32[1,512]{1,0:T(1,128)} %dist_ref.1) | copy-start | bytes 6148
  7.8 7.7 %collective-permute-start.9 = (bf16[128,512]{1,0:T(8,128)(2,1)S(1)}, bf16[128,512]{1,0:T(8,128)(2,1)S(1)}, u32[]{:S(2)}, u32[]{:S(2)}) collective-permute-start(bf16[128,512]{1,0:T(8,128)(2,1)S(1)} %stack.1), channel_id=1, source_target_pairs={{0,2},{1,3},{2,0},{3,1},{4,6},{5,7},{6,4},{7,5},{8,10},{9,11},{10,... | collective-permute-start | bytes 393224 | tf_op jit(solution)/shard_map/ppermute | solution.py:249
  10.4 6.7 %collective-permute-start.3 = (bf16[128,512]{1,0:T(8,128)(2,1)S(1)}, bf16[128,512]{1,0:T(8,128)(2,1)S(1)}, u32[]{:S(2)}, u32[]{:S(2)}) collective-permute-start(bf16[128,512]{1,0:T(8,128)(2,1)S(1)} %halves_apart.1.refs_0_.refs_1_), channel_id=1, source_target_pairs={{0,4},{4,0},{8,12},{12,8},{16,20},{20,16},{24,28},{28,24},{1,5},{5... | collective-permute-start | bytes 393224 | tf_op jit(solution)/shard_map/ppermute | solution.py:249
  11.7 5.4 %collective-permute-start.4 = (bf16[128,512]{1,0:T(8,128)(2,1)S(1)}, bf16[128,512]{1,0:T(8,128)(2,1)S(1)}, u32[]{:S(2)}, u32[]{:S(2)}) collective-permute-start(bf16[128,512]{1,0:T(8,128)(2,1)S(1)} %collective-permute-done.refs_1_.refs_2_), channel_id=1, source_target_pairs={{0,4},{4,0},{8,12},{12,8},{16,20},{20,16},{24,28},{28,24},{1,5},{5... | collective-permute-start | bytes 393224 | tf_op jit(solution)/shard_map/ppermute | solution.py:249
  13.5 3.6 %collective-permute-start.5 = (bf16[128,512]{1,0:T(8,128)(2,1)S(1)}, bf16[128,512]{1,0:T(8,128)(2,1)S(1)}, u32[]{:S(2)}, u32[]{:S(2)}) collective-permute-start(bf16[128,512]{1,0:T(8,128)(2,1)S(1)} %collective-permute-done.1.refs_0_.refs_3_), channel_id=1, source_target_pairs={{0,4},{4,0},{8,12},{12,8},{16,20},{20,16},{24,28},{28,24},{1,5},{5... | collective-permute-start | bytes 393224 | tf_op jit(solution)/shard_map/ppermute | solution.py:249
  13.8 3.3 %collective-permute-start.6 = (bf16[128,512]{1,0:T(8,128)(2,1)S(1)}, bf16[128,512]{1,0:T(8,128)(2,1)S(1)}, u32[]{:S(2)}, u32[]{:S(2)}) collective-permute-start(bf16[128,512]{1,0:T(8,128)(2,1)S(1)} %collective-permute-done.2.refs_1_.refs_4_), channel_id=1, source_target_pairs={{0,4},{4,0},{8,12},{12,8},{16,20},{20,16},{24,28},{28,24},{1,5},{5... | collective-permute-start | bytes 393224 | tf_op jit(solution)/shard_map/ppermute | solution.py:249
  18.6 8.3 %collective-permute-start.11 = (bf16[64,512]{1,0:T(8,128)(2,1)S(1)}, bf16[64,512]{1,0:T(8,128)(2,1)S(1)}, u32[]{:S(2)}, u32[]{:S(2)}) collective-permute-start(bf16[64,512]{1,0:T(8,128)(2,1)S(1)} %increment_rows.11), channel_id=1, source_target_pairs={{0,3},{1,2},{2,1},{3,0},{4,7},{5,6},{6,5},{7,4},{8,11},{9,10},{10,... | collective-permute-start | bytes 196616 | tf_op jit(solution)/shard_map/ppermute | solution.py:249
  22.3 5.9 %collective-permute-start.10 = (bf16[64,512]{1,0:T(8,128)(2,1)S(1)}, bf16[64,512]{1,0:T(8,128)(2,1)S(1)}, u32[]{:S(2)}, u32[]{:S(2)}) collective-permute-start(bf16[64,512]{1,0:T(8,128)(2,1)S(1)} %increment_rows.10), channel_id=1, source_target_pairs={{0,2},{1,3},{2,0},{3,1},{4,6},{5,7},{6,4},{7,5},{8,10},{9,11},{10,... | collective-permute-start | bytes 196616 | tf_op jit(solution)/shard_map/ppermute | solution.py:249
  23.4 5.1 %collective-permute-start.8 = (bf16[64,512]{1,0:T(8,128)(2,1)S(1)}, bf16[64,512]{1,0:T(8,128)(2,1)S(1)}, u32[]{:S(2)}, u32[]{:S(2)}) collective-permute-start(bf16[64,512]{1,0:T(8,128)(2,1)S(1)} %increment_rows.8), channel_id=1, source_target_pairs={{0,1},{1,0},{2,3},{3,2},{4,5},{5,4},{6,7},{7,6},{8,9},{9,8},{10,11... | collective-permute-start | bytes 196616 | tf_op jit(solution)/shard_map/ppermute | solution.py:249

commit v6 on v5

--- a/solution.py
+++ b/solution.py
@@ -72,36 +72,21 @@
     return jnp.exp((place - HALF if rising else -place).astype(F32) / TAPER_CELLS)
 
 
-def half_states(col_parts, members):
-    columns = col_parts[0].shape[0] - members
-    cells = col_parts[0].shape[1]
-    wide = cells // 2
-    blocks = cells // BLK
-    count = len(col_parts)
-
-    def kernel(*refs):
-        owner = lax.broadcasted_iota(jnp.int32, (1, wide), 1) // HALF
-        for col_ref, out_ref in zip(refs[:count], refs[count:]):
-            for half in range(2):
-                span = pl.ds(half * wide, wide)
-                right = col_ref[pl.ds(0, members), span]
-                innov = col_ref[pl.ds(members, columns), span].astype(F32)
-                innov = (innov * fade((1, wide), 1, half == 0)).astype(BF16)
-                spaced = jnp.concatenate(
-                    [right * (owner == q).astype(F32).astype(BF16) for q in range(blocks)], axis=0
-                )
-                out_ref[pl.ds(half * columns, columns), :] = lax.dot_general(
-                    innov, spaced, (((1,), (1,)), ((), ())), preferred_element_type=F32
-                )
-
-    return pl.pallas_call(
-        kernel,
-        out_shape=[jax.ShapeDtypeStruct((2 * columns, blocks * members), F32)] * count,
-        in_specs=[VMEM] * count,
-        out_specs=[VMEM] * count,
-        compiler_params=SMALL,
-        name="half_states",
-    )(*col_parts)
+def fill_states(col_ref, out_ref, members):
+    columns = col_ref.shape[0] - members
+    wide = col_ref.shape[1] // 2
+    owner = lax.broadcasted_iota(jnp.int32, (1, wide), 1) // HALF
+    for half in range(2):
+        span = pl.ds(half * wide, wide)
+        right = col_ref[pl.ds(0, members), span]
+        innov = col_ref[pl.ds(members, columns), span].astype(F32)
+        innov = (innov * fade((1, wide), 1, half == 0)).astype(BF16)
+        spaced = jnp.concatenate(
+            [right * (owner == q).astype(F32).astype(BF16) for q in range(wide // HALF)], axis=0
+        )
+        out_ref[pl.ds(half * columns, columns), :] = lax.dot_general(
+            innov, spaced, (((1,), (1,)), ((), ())), preferred_element_type=F32
+        )
 
 
 def increment_rows(table, places, row_flips, members, col_parts, states, col_flips, before, send):
@@ -118,12 +103,18 @@
         ([stacked is known for known in row_stacks].index(True), start) for stacked, start in places
     ]
     n_row, n_stack, n_col, n_before = len(places), len(row_stacks), len(col_parts), len(before)
+    fresh = n_col if states is None else 0
+    states = [] if states is None else states
 
     def kernel(table_ref, *refs):
         refs = list(refs)
-        row_refs, col_refs, state_refs, before_refs, out_refs = (
-            [refs.pop(0) for _ in range(n)] for n in (n_stack, n_col, n_col, n_before, n_row)
-        )
+        row_refs, col_refs, state_refs, before_refs, out_refs, fresh_refs = (
+            [refs.pop(0) for _ in range(n)]
+            for n in (n_stack, n_col, len(states), n_before, n_row, fresh)
+        )
+        for col_ref, fresh_ref in zip(col_refs, fresh_refs):
+            fill_states(col_ref, fresh_ref, members)
+        state_refs = state_refs + fresh_refs
         tile_ref, fade_ref, left_ref, total_ref, sum_ref = refs
         gap = lax.broadcasted_iota(jnp.int32, (HALF, wide), 0)
         gap = gap - lax.broadcasted_iota(jnp.int32, (HALF, wide), 1) % HALF
@@ -188,9 +179,10 @@
     out = (cells, columns) if send is None else (columns, cells)
     return pl.pallas_call(
         kernel,
-        out_shape=[jax.ShapeDtypeStruct(out, F32 if send is None else send)] * n_row,
-        in_specs=[VMEM] * (1 + n_stack + 2 * n_col + n_before),
-        out_specs=[VMEM] * n_row,
+        out_shape=[jax.ShapeDtypeStruct(out, F32 if send is None else send)] * n_row
+        + [jax.ShapeDtypeStruct((2 * columns, blocks * members), F32)] * fresh,
+        in_specs=[VMEM] * (1 + n_stack + n_col + len(states) + n_before),
+        out_specs=[VMEM] * (n_row + fresh),
         scratch_shapes=[
             pltpu.VMEM((HALF, wide), F32),
             pltpu.VMEM((2, HALF, columns), F32),
@@ -269,29 +261,24 @@
         table = pair_table(
             pair_rows, pair_cols, pair_dist, pair_counts, n_cols * per_dev, n_rows * per_dev, per_dev, members
         )
-
         far_parts = [swap(part, "rows", n_rows, 1) for part in near_parts]
         others = list(range(1, n_cols))
-        early = len(near) // 2
-        near_states = half_states(near_parts[:early], members) + half_states(near_parts[early:], members)
-        before = dict(
-            zip(
-                others[:1],
-                increment_rows(table, places[1:2], [1], members, near_parts, near_states, near, [], None),
-            )
-        )
+        first, *near_states = increment_rows(table, places[1:2], [1], members, near_parts, None, near, [], None)
+        before = {1: first}
         before.update(
             zip(
                 others[1:],
                 increment_rows(table, places[2:], others[1:], members, near_parts, near_states, near, [], None),
             )
         )
-        far_states = half_states(far_parts, members)
-        received = []
-        for flip in others:
-            (part,) = increment_rows(
+        received, far_states = [], None
+        for flip in range(n_cols - 1, 0, -1):
+            part, *fresh = increment_rows(
                 table, [places[flip]], [flip], members, far_parts, far_states, far, [before[flip]], BF16
             )
+            far_states = far_states or fresh
+            if flip > 1:
+                before[flip - 1], _ = lax.optimization_barrier((before[flip - 1], part))
             received.append(swap(part, "cols", n_cols, flip))
         (own,) = increment_rows(
             table,

time: 29.3 us -> 28.9 us (0.986)
  Pallas kernels: 9.52 us -> 9.03 us
    pallas_call x3 -> x0, Pallas kernels: 0.99 us -> none  [half_states(): pl.pallas_call(kernel, out_shape=[jax.ShapeDtypeStruct((2 * columns, bloc...]
    pallas_call x6, Pallas kernels: 7.29 us -> 7.79 us  [increment_rows(): pl.pallas_call(kernel, out_shape=[jax.ShapeDtypeStruct(out, F32 if send i...]
where the time goes in v6:
time: 28.9 us; the launch traced here: 28.7 us
  starting transfers between devices  14.8 us (51%)
  Pallas kernels  9.03 us (31%)
  waiting for transfers between devices  3.18 us (11%)
  other arithmetic  0.88 us (3%)
  between operations  0.79 us (3%)
    ppermute x12, starting transfers between devices, swap(): return lax.ppermute(x, axis, [(i, i ^ flip) for i in range(size)])  14.8 us
    pallas_call x6, Pallas kernels, increment_rows(): pl.pallas_call(kernel, out_shape=[jax.ShapeDtypeStruct(out, F32 if send i...  7.79 us
    ppermute x12, waiting for transfers between devices, swap(): return lax.ppermute(x, axis, [(i, i ^ flip) for i in range(size)])  3.18 us
    concatenate x1, other arithmetic, local(): packed = halves_apart(jnp.concatenate([anom, innov], axis=0))  0.88 us
    pallas_call x1, Pallas kernels, add_up(): pl.pallas_call(kernel, out_shape=jax.ShapeDtypeStruct(own.shape, F32), in...  0.69 us
  transfers between devices with their start and end apart: 12, of which 4 were waited for; matrix products, arithmetic and copies ran while one was open for 3% of the time, Pallas kernels for 25%

profile of v6, /device:TPU:0, one launch (start us, length us, event | category | flops | bytes accessed | tf_op | source)
XLA Modules:
  0.0 28.7 jit_solution(6926850771189158747)
XLA Ops:
  0.0 3.0 %collective-permute-start.7 = (bf16[64,512]{1,0:T(8,128)(2,1)}, bf16[64,512]{1,0:T(8,128)(2,1)S(1)}, u32[]{:S(2)}, u32[]{:S(2)}) collective-permute-start(bf16[64,512]{1,0:T(8,128)(2,1)} %bitcast.3), channel_id=1, source_target_pairs={{0,1},{1,0},{2,3},{3,2},{4,5},{5,4},{6,7},{7,6},{8,9},{9,8},{10,11... | collective-permute-start | bytes 196616 | tf_op jit(solution)/shard_map/ppermute | solution.py:241
  3.0 0.9 %pad_maximum_fusion.in_ref = bf16[128,512]{1,0:T(8,128)(2,1)S(1)} fusion(bf16[64,512]{1,0:T(8,128)(2,1)} %bitcast.7, bf16[64,512]{1,0:T(8,128)(2,1)} %bitcast.4), kind=kLoop, calls=%fused_computation | loop fusion | flops 262144 | bytes 262144 | tf_op jit(solution)/shard_map/concatenate | solution.py:251
  3.9 0.2 halves_apart.1.refs_1_
  4.2 2.5 %collective-permute-start.2 = (bf16[128,512]{1,0:T(8,128)(2,1)S(1)}, bf16[128,512]{1,0:T(8,128)(2,1)S(1)}, u32[]{:S(2)}, u32[]{:S(2)}) collective-permute-start(bf16[128,512]{1,0:T(8,128)(2,1)S(1)} %halves_apart.1.refs_1_), channel_id=1, source_target_pairs={{0,24},{4,28},{8,16},{12,20},{16,8},{20,12},{24,0},{28,4},{1,25},{... | collective-permute-start | bytes 393224 | tf_op jit(solution)/shard_map/ppermute | solution.py:241
  6.7 0.5 %collective-permute-start.1 = (bf16[128,512]{1,0:T(8,128)(2,1)S(1)}, bf16[128,512]{1,0:T(8,128)(2,1)S(1)}, u32[]{:S(2)}, u32[]{:S(2)}) collective-permute-start(bf16[128,512]{1,0:T(8,128)(2,1)S(1)} %halves_apart.1.refs_1_), channel_id=1, source_target_pairs={{0,16},{4,20},{8,24},{12,28},{16,0},{20,4},{24,8},{28,12},{1,17},{... | collective-permute-start | bytes 393224 | tf_op jit(solution)/shard_map/ppermute | solution.py:241
  7.2 0.5 %collective-permute-start = (bf16[128,512]{1,0:T(8,128)(2,1)S(1)}, bf16[128,512]{1,0:T(8,128)(2,1)S(1)}, u32[]{:S(2)}, u32[]{:S(2)}) collective-permute-start(bf16[128,512]{1,0:T(8,128)(2,1)S(1)} %halves_apart.1.refs_1_), channel_id=1, source_target_pairs={{0,8},{4,12},{8,0},{12,4},{16,24},{20,28},{24,16},{28,20},{1,9},{5... | collective-permute-start | bytes 393224 | tf_op jit(solution)/shard_map/ppermute | solution.py:241
  7.8 2.7 %collective-permute-start.8 = (bf16[128,512]{1,0:T(8,128)(2,1)S(1)}, bf16[128,512]{1,0:T(8,128)(2,1)S(1)}, u32[]{:S(2)}, u32[]{:S(2)}) collective-permute-start(bf16[128,512]{1,0:T(8,128)(2,1)S(1)} %stack.1), channel_id=1, source_target_pairs={{0,2},{1,3},{2,0},{3,1},{4,6},{5,7},{6,4},{7,5},{8,10},{9,11},{10,... | collective-permute-start | bytes 393224 | tf_op jit(solution)/shard_map/ppermute | solution.py:241
  11.1 0.3 %pair_table.1.table_ref = f32[16,2048]{1,0:T(8,128)S(1)} custom-call(s32[1,512]{1,0:T(1,128)S(1)} %copy-done.1, s32[1,512]{1,0:T(1,128)S(1)} %copy-done.2, s32[1,512]{1,0:T(1,128)S(1)} %copy-done.3, s32[1,1]{1,0:T(1,128)S(6)} %copy.7.count_ref), custom_call_target="tpu_custom_call" | custom-call | tf_op jit(solution)/shard_map/pair_table/pallas_call | solution.py:38
  11.4 0.6 %collective-permute-start.6 = (bf16[128,512]{1,0:T(8,128)(2,1)S(1)}, bf16[128,512]{1,0:T(8,128)(2,1)S(1)}, u32[]{:S(2)}, u32[]{:S(2)}) collective-permute-start(bf16[128,512]{1,0:T(8,128)(2,1)S(1)} %collective-permute-done.2.refs_4_), channel_id=1, source_target_pairs={{0,4},{4,0},{8,12},{12,8},{16,20},{20,16},{24,28},{28,24},{1,5},{5... | collective-permute-start | bytes 393224 | tf_op jit(solution)/shard_map/ppermute | solution.py:241
  12.0 0.9 %collective-permute-done.1.refs_3_ = bf16[128,512]{1,0:T(8,128)(2,1)S(1)} collective-permute-done((bf16[128,512]{1,0:T(8,128)(2,1)S(1)}, bf16[128,512]{1,0:T(8,128)(2,1)S(1)}, u32[]{:S(2)}, u32[]{:S(2)}) %collective-permute-start.1) | collective-permute-done | bytes 131104 | tf_op jit(solution)/shard_map/ppermute | solution.py:241
  12.9 0.1 collective-permute-done.refs_2_
  13.0 0.4 %collective-permute-start.4 = (bf16[128,512]{1,0:T(8,128)(2,1)S(1)}, bf16[128,512]{1,0:T(8,128)(2,1)S(1)}, u32[]{:S(2)}, u32[]{:S(2)}) collective-permute-start(bf16[128,512]{1,0:T(8,128)(2,1)S(1)} %collective-permute-done.refs_2_), channel_id=1, source_target_pairs={{0,4},{4,0},{8,12},{12,8},{16,20},{20,16},{24,28},{28,24},{1,5},{5... | collective-permute-start | bytes 393224 | tf_op jit(solution)/shard_map/ppermute | solution.py:241
  13.4 1.2 %increment_rows.6 = (f32[512,64]{1,0:T(8,128)S(1)}, f32[128,256]{1,0:T(8,128)S(1)}, f32[128,256]{1,0:T(8,128)S(1)}, f32[128,256]{1,0:T(8,128)S(1)}, f32[128,256]{1,0:T(8,128)S(1)}) custom-call(f32[16,2048]{1,0:T(8,128)S(1)} %pair_table.1.table_ref, bf16[64,512]{1,0:T(8,128)(2,1)S(1)} %collective-permute-done.7.refs_0_.refs_1_, ...), custom_call_target="tpu_custom_call" | custom-call | flops 1073741824 | bytes 524288 | tf_op jit(solution)/shard_map/increment_rows/pallas_call | solution.py:180
  14.6 0.9 %collective-permute-done.8.refs_0_ = bf16[128,512]{1,0:T(8,128)(2,1)S(1)} collective-permute-done((bf16[128,512]{1,0:T(8,128)(2,1)S(1)}, bf16[128,512]{1,0:T(8,128)(2,1)S(1)}, u32[]{:S(2)}, u32[]{:S(2)}) %collective-permute-start.8) | collective-permute-done | bytes 131104 | tf_op jit(solution)/shard_map/ppermute | solution.py:241
  15.5 1.6 %increment_rows.7 = (f32[512,64]{1,0:T(8,128)S(1)}, f32[512,64]{1,0:T(8,128)S(1)}) custom-call(f32[16,2048]{1,0:T(8,128)S(1)} %pair_table.1.table_ref, bf16[128,512]{1,0:T(8,128)(2,1)S(1)} %collective-permute-done.8.refs_0_, bf16[128,512]{1,0:T(8,128)(2,1)S(1)} %halves_apart.1.refs_1_, bf16[128,512]{1,0:T(8,128)(2,1)S(1)} %collective-permute-done.refs_2_, ...), custom_call_target="tpu_custom_call" | custom-call | flops 2147483648 | bytes 524288 | tf_op jit(solution)/shard_map/increment_rows/pallas_call | solution.py:180
  17.1 1.3 %increment_rows.8 = (bf16[64,512]{1,0:T(8,128)(2,1)S(1)}, f32[128,256]{1,0:T(8,128)S(1)}, f32[128,256]{1,0:T(8,128)S(1)}, f32[128,256]{1,0:T(8,128)S(1)}, f32[128,256]{1,0:T(8,128)S(1)}) custom-call(f32[16,2048]{1,0:T(8,128)S(1)} %pair_table.1.table_ref, bf16[128,512]{1,0:T(8,128)(2,1)S(1)} %collective-permute-done.8.refs_0_, ...), custom_call_target="tpu_custom_call" | custom-call | flops 1073741824 | bytes 524288 | tf_op jit(solution)/shard_map/increment_rows/pallas_call | solution.py:180
  18.4 2.7 %collective-permute-start.9 = (bf16[64,512]{1,0:T(8,128)(2,1)S(1)}, bf16[64,512]{1,0:T(8,128)(2,1)S(1)}, u32[]{:S(2)}, u32[]{:S(2)}) collective-permute-start(bf16[64,512]{1,0:T(8,128)(2,1)S(1)} %get-tuple-element.28), channel_id=1, source_target_pairs={{0,3},{1,2},{2,1},{3,0},{4,7},{5,6},{6,5},{7,4},{8,11},{9,10},{10,... | collective-permute-start | bytes 196616 | tf_op jit(solution)/shard_map/ppermute | solution.py:241
  21.1 1.0 %increment_rows.10 = bf16[64,512]{1,0:T(8,128)(2,1)S(1)} custom-call(f32[16,2048]{1,0:T(8,128)S(1)} %pair_table.1.table_ref, bf16[128,512]{1,0:T(8,128)(2,1)S(1)} %collective-permute-done.8.refs_0_, bf16[128,512]{1,0:T(8,128)(2,1)S(1)} %collective-permute-done.3.refs_1_.refs_5_, bf16[128,512]{1,0:T(8,128)(2,1)S(1)} %collective-permute-done.4.refs_2_.refs_6_, ...), custom_call_target="tpu_custom_call" | custom-call | flops 1073741824 | bytes 524288 | tf_op jit(solution)/shard_map/increment_rows/pallas_call | solution.py:180
  22.1 0.1 collective-permute-start.10
  22.2 1.0 %increment_rows.11 = bf16[64,512]{1,0:T(8,128)(2,1)S(1)} custom-call(f32[16,2048]{1,0:T(8,128)S(1)} %pair_table.1.table_ref, bf16[64,512]{1,0:T(8,128)(2,1)S(1)} %collective-permute-done.7.refs_0_.refs_1_, bf16[128,512]{1,0:T(8,128)(2,1)S(1)} %collective-permute-done.3.refs_1_.refs_5_, bf16[128,512]{1,0:T(8,128)(2,1)S(1)} %collective-permute-done.4.refs_2_.refs_6_, ...), custom_call_target="tpu_custom_call" | custom-call | flops 1073741824 | bytes 524288 | tf_op jit(solution)/shard_map/increment_rows/pallas_call | solution.py:180
  23.2 1.8 %collective-permute-start.11 = (bf16[64,512]{1,0:T(8,128)(2,1)S(1)}, bf16[64,512]{1,0:T(8,128)(2,1)S(1)}, u32[]{:S(2)}, u32[]{:S(2)}) collective-permute-start(bf16[64,512]{1,0:T(8,128)(2,1)S(1)} %increment_rows.11), channel_id=1, source_target_pairs={{0,1},{1,0},{2,3},{3,2},{4,5},{5,4},{6,7},{7,6},{8,9},{9,8},{10,11... | collective-permute-start | bytes 196616 | tf_op jit(solution)/shard_map/ppermute | solution.py:241
  25.0 1.7 %increment_rows.9.refs_0_ = f32[64,512]{1,0:T(8,128)S(1)} custom-call(f32[16,2048]{1,0:T(8,128)S(1)} %pair_table.1.table_ref, bf16[64,512]{1,0:T(8,128)(2,1)S(1)} %bitcast.6, bf16[128,512]{1,0:T(8,128)(2,1)S(1)} %halves_apart.1.refs_1_, bf16[128,512]{1,0:T(8,128)(2,1)S(1)} %collective-permute-done.refs_2_, ...), custom_call_target="tpu_custom_call" | custom-call | flops 2147483648 | bytes 1048576 | tf_op jit(solution)/shard_map/increment_rows/pallas_call | solution.py:180
  26.7 1.3 %collective-permute-done.11.refs_3_ = bf16[64,512]{1,0:T(8,128)(2,1)S(1)} collective-permute-done((bf16[64,512]{1,0:T(8,128)(2,1)S(1)}, bf16[64,512]{1,0:T(8,128)(2,1)S(1)}, u32[]{:S(2)}, u32[]{:S(2)}) %collective-permute-start.11) | collective-permute-done | bytes 65568 | tf_op jit(solution)/shard_map/ppermute | solution.py:241
  28.0 0.7 %add_up.1 = f32[64,512]{1,0:T(8,128)} custom-call(f32[64,512]{1,0:T(8,128)S(1)} %increment_rows.9.refs_0_, bf16[64,512]{1,0:T(8,128)(2,1)S(1)} %collective-permute-done.9.refs_1_, bf16[64,512]{1,0:T(8,128)(2,1)S(1)} %collective-permute-done.10.refs_2_, bf16[64,512]{1,0:T(8,128)(2,1)S(1)} %collective-permute-done.11.refs_3_), custom_call_target="tpu_custom_call" | custom-call | tf_op jit(solution)/shard_map/add_up/pallas_call | solution.py:230
  (19 shorter events, 0.1 us)
Async XLA Ops:
  0.0 7.7 %collective-permute-start.7 = (bf16[64,512]{1,0:T(8,128)(2,1)}, bf16[64,512]{1,0:T(8,128)(2,1)S(1)}, u32[]{:S(2)}, u32[]{:S(2)}) collective-permute-start(bf16[64,512]{1,0:T(8,128)(2,1)} %bitcast.3), channel_id=1, source_target_pairs={{0,1},{1,0},{2,3},{3,2},{4,5},{5,4},{6,7},{7,6},{8,9},{9,8},{10,11... | collective-permute-start | bytes 196616 | tf_op jit(solution)/shard_map/ppermute | solution.py:241
  3.9 3.8 %copy-start = (bf16[512,64]{0,1:T(8,128)(2,1)S(1)}, bf16[512,64]{0,1:T(8,128)(2,1)}, u32[]{:S(2)}) copy-start(bf16[512,64]{0,1:T(8,128)(2,1)} %param.6) | copy-start | bytes 196612
  4.2 7.3 %collective-permute-start.2 = (bf16[128,512]{1,0:T(8,128)(2,1)S(1)}, bf16[128,512]{1,0:T(8,128)(2,1)S(1)}, u32[]{:S(2)}, u32[]{:S(2)}) collective-permute-start(bf16[128,512]{1,0:T(8,128)(2,1)S(1)} %halves_apart.1.refs_1_), channel_id=1, source_target_pairs={{0,24},{4,28},{8,16},{12,20},{16,8},{20,12},{24,0},{28,4},{1,25},{... | collective-permute-start | bytes 393224 | tf_op jit(solution)/shard_map/ppermute | solution.py:241
  6.7 6.2 %collective-permute-start.1 = (bf16[128,512]{1,0:T(8,128)(2,1)S(1)}, bf16[128,512]{1,0:T(8,128)(2,1)S(1)}, u32[]{:S(2)}, u32[]{:S(2)}) collective-permute-start(bf16[128,512]{1,0:T(8,128)(2,1)S(1)} %halves_apart.1.refs_1_), channel_id=1, source_target_pairs={{0,16},{4,20},{8,24},{12,28},{16,0},{20,4},{24,8},{28,12},{1,17},{... | collective-permute-start | bytes 393224 | tf_op jit(solution)/shard_map/ppermute | solution.py:241
  7.2 5.8 %collective-permute-start = (bf16[128,512]{1,0:T(8,128)(2,1)S(1)}, bf16[128,512]{1,0:T(8,128)(2,1)S(1)}, u32[]{:S(2)}, u32[]{:S(2)}) collective-permute-start(bf16[128,512]{1,0:T(8,128)(2,1)S(1)} %halves_apart.1.refs_1_), channel_id=1, source_target_pairs={{0,8},{4,12},{8,0},{12,4},{16,24},{20,28},{24,16},{28,20},{1,9},{5... | collective-permute-start | bytes 393224 | tf_op jit(solution)/shard_map/ppermute | solution.py:241
  7.7 3.4 %copy-start.1 = (s32[1,512]{1,0:T(1,128)S(1)}, s32[1,512]{1,0:T(1,128)}, u32[]{:S(2)}) copy-start(s32[1,512]{1,0:T(1,128)} %rows_ref.1) | copy-start | bytes 6148
  7.7 3.4 %copy-start.2 = (s32[1,512]{1,0:T(1,128)S(1)}, s32[1,512]{1,0:T(1,128)}, u32[]{:S(2)}) copy-start(s32[1,512]{1,0:T(1,128)} %cols_ref.1) | copy-start | bytes 6148
  7.7 3.4 %copy-start.3 = (s32[1,512]{1,0:T(1,128)S(1)}, s32[1,512]{1,0:T(1,128)}, u32[]{:S(2)}) copy-start(s32[1,512]{1,0:T(1,128)} %dist_ref.1) | copy-start | bytes 6148
  7.8 7.7 %collective-permute-start.8 = (bf16[128,512]{1,0:T(8,128)(2,1)S(1)}, bf16[128,512]{1,0:T(8,128)(2,1)S(1)}, u32[]{:S(2)}, u32[]{:S(2)}) collective-permute-start(bf16[128,512]{1,0:T(8,128)(2,1)S(1)} %stack.1), channel_id=1, source_target_pairs={{0,2},{1,3},{2,0},{3,1},{4,6},{5,7},{6,4},{7,5},{8,10},{9,11},{10,... | collective-permute-start | bytes 393224 | tf_op jit(solution)/shard_map/ppermute | solution.py:241
  10.4 6.7 %collective-permute-start.3 = (bf16[128,512]{1,0:T(8,128)(2,1)S(1)}, bf16[128,512]{1,0:T(8,128)(2,1)S(1)}, u32[]{:S(2)}, u32[]{:S(2)}) collective-permute-start(bf16[128,512]{1,0:T(8,128)(2,1)S(1)} %halves_apart.1.refs_1_), channel_id=1, source_target_pairs={{0,4},{4,0},{8,12},{12,8},{16,20},{20,16},{24,28},{28,24},{1,5},{5... | collective-permute-start | bytes 393224 | tf_op jit(solution)/shard_map/ppermute | solution.py:241
  11.4 5.7 %collective-permute-start.6 = (bf16[128,512]{1,0:T(8,128)(2,1)S(1)}, bf16[128,512]{1,0:T(8,128)(2,1)S(1)}, u32[]{:S(2)}, u32[]{:S(2)}) collective-permute-start(bf16[128,512]{1,0:T(8,128)(2,1)S(1)} %collective-permute-done.2.refs_4_), channel_id=1, source_target_pairs={{0,4},{4,0},{8,12},{12,8},{16,20},{20,16},{24,28},{28,24},{1,5},{5... | collective-permute-start | bytes 393224 | tf_op jit(solution)/shard_map/ppermute | solution.py:241
  12.9 4.2 %collective-permute-start.5 = (bf16[128,512]{1,0:T(8,128)(2,1)S(1)}, bf16[128,512]{1,0:T(8,128)(2,1)S(1)}, u32[]{:S(2)}, u32[]{:S(2)}) collective-permute-start(bf16[128,512]{1,0:T(8,128)(2,1)S(1)} %collective-permute-done.1.refs_3_), channel_id=1, source_target_pairs={{0,4},{4,0},{8,12},{12,8},{16,20},{20,16},{24,28},{28,24},{1,5},{5... | collective-permute-start | bytes 393224 | tf_op jit(solution)/shard_map/ppermute | solution.py:241
  13.0 4.2 %collective-permute-start.4 = (bf16[128,512]{1,0:T(8,128)(2,1)S(1)}, bf16[128,512]{1,0:T(8,128)(2,1)S(1)}, u32[]{:S(2)}, u32[]{:S(2)}) collective-permute-start(bf16[128,512]{1,0:T(8,128)(2,1)S(1)} %collective-permute-done.refs_2_), channel_id=1, source_target_pairs={{0,4},{4,0},{8,12},{12,8},{16,20},{20,16},{24,28},{28,24},{1,5},{5... | collective-permute-start | bytes 393224 | tf_op jit(solution)/shard_map/ppermute | solution.py:241
  18.4 9.6 %collective-permute-start.9 = (bf16[64,512]{1,0:T(8,128)(2,1)S(1)}, bf16[64,512]{1,0:T(8,128)(2,1)S(1)}, u32[]{:S(2)}, u32[]{:S(2)}) collective-permute-start(bf16[64,512]{1,0:T(8,128)(2,1)S(1)} %get-tuple-element.28), channel_id=1, source_target_pairs={{0,3},{1,2},{2,1},{3,0},{4,7},{5,6},{6,5},{7,4},{8,11},{9,10},{10,... | collective-permute-start | bytes 196616 | tf_op jit(solution)/shard_map/ppermute | solution.py:241
  22.1 5.9 %collective-permute-start.10 = (bf16[64,512]{1,0:T(8,128)(2,1)S(1)}, bf16[64,512]{1,0:T(8,128)(2,1)S(1)}, u32[]{:S(2)}, u32[]{:S(2)}) collective-permute-start(bf16[64,512]{1,0:T(8,128)(2,1)S(1)} %increment_rows.10), channel_id=1, source_target_pairs={{0,2},{1,3},{2,0},{3,1},{4,6},{5,7},{6,4},{7,5},{8,10},{9,11},{10,... | collective-permute-start | bytes 196616 | tf_op jit(solution)/shard_map/ppermute | solution.py:241
  23.2 4.9 %collective-permute-start.11 = (bf16[64,512]{1,0:T(8,128)(2,1)S(1)}, bf16[64,512]{1,0:T(8,128)(2,1)S(1)}, u32[]{:S(2)}, u32[]{:S(2)}) collective-permute-start(bf16[64,512]{1,0:T(8,128)(2,1)S(1)} %increment_rows.11), channel_id=1, source_target_pairs={{0,1},{1,0},{2,3},{3,2},{4,5},{5,4},{6,7},{7,6},{8,9},{9,8},{10,11... | collective-permute-start | bytes 196616 | tf_op jit(solution)/shard_map/ppermute | solution.py:241

commit v7 on v6

--- a/solution.py
+++ b/solution.py
@@ -89,7 +89,7 @@
         )
 
 
-def increment_rows(table, places, row_flips, members, col_parts, states, col_flips, before, send):
+def increment_rows(table, places, row_flips, members, col_parts, states, col_flips, before, send, lefts=None):
     cells = col_parts[0].shape[1]
     columns = col_parts[0].shape[0] - members
     blocks = cells // BLK
@@ -105,27 +105,36 @@
     n_row, n_stack, n_col, n_before = len(places), len(row_stacks), len(col_parts), len(before)
     fresh = n_col if states is None else 0
     states = [] if states is None else states
+    lefts = [] if lefts is None else lefts
+    handed = n_row if n_before == 0 and send is None else 0
+    if lefts:
+        row_stacks, n_stack = [], 0
 
     def kernel(table_ref, *refs):
         refs = list(refs)
-        row_refs, col_refs, state_refs, before_refs, out_refs, fresh_refs = (
+        row_refs, col_refs, state_refs, before_refs, known_refs, out_refs, handed_refs, fresh_refs = (
             [refs.pop(0) for _ in range(n)]
-            for n in (n_stack, n_col, len(states), n_before, n_row, fresh)
+            for n in (n_stack, n_col, len(states), n_before, len(lefts), n_row, handed, fresh)
         )
         for col_ref, fresh_ref in zip(col_refs, fresh_refs):
             fill_states(col_ref, fresh_ref, members)
         state_refs = state_refs + fresh_refs
-        tile_ref, fade_ref, left_ref, total_ref, sum_ref = refs
+        tile_ref, fade_ref, own_left_ref, total_ref, sum_ref = refs
         gap = lax.broadcasted_iota(jnp.int32, (HALF, wide), 0)
         gap = gap - lax.broadcasted_iota(jnp.int32, (HALF, wide), 1) % HALF
         tile_ref[...] = jnp.exp(-jnp.abs(gap).astype(F32) / TAPER_CELLS)
         for half in range(2):
             fade_ref[half] = fade((HALF, columns), 0, half == 0)
         for row in range(n_row):
-            left = row_refs[spots[row][0]][pl.ds(spots[row][1], members), :].T
-            for a in range(blocks):
-                for half in range(2):
-                    left_ref[half, pl.ds(a * HALF, HALF), :] = left[a * BLK + half * HALF : a * BLK + (half + 1) * HALF]
+            if lefts:
+                left_ref = known_refs[row]
+            else:
+                left_ref = handed_refs[row] if handed else own_left_ref
+                left = row_refs[spots[row][0]][pl.ds(spots[row][1], members), :].T
+                for a in range(blocks):
+                    for half in range(2):
+                        start = a * BLK + half * HALF
+                        left_ref[half, pl.ds(a * HALF, HALF), :] = left[start : start + HALF]
             first_row = row_flips[row] * blocks
             for col in range(n_col):
                 weights = [
@@ -180,9 +189,10 @@
     return pl.pallas_call(
         kernel,
         out_shape=[jax.ShapeDtypeStruct(out, F32 if send is None else send)] * n_row
+        + [jax.ShapeDtypeStruct((2, wide, members), BF16)] * handed
         + [jax.ShapeDtypeStruct((2 * columns, blocks * members), F32)] * fresh,
-        in_specs=[VMEM] * (1 + n_stack + n_col + len(states) + n_before),
-        out_specs=[VMEM] * (n_row + fresh),
+        in_specs=[VMEM] * (1 + n_stack + n_col + len(states) + n_before + len(lefts)),
+        out_specs=[VMEM] * (n_row + handed + fresh),
         scratch_shapes=[
             pltpu.VMEM((HALF, wide), F32),
             pltpu.VMEM((2, HALF, columns), F32),
@@ -197,7 +207,7 @@
             transcendentals=BLK * BLK,
         ),
         name="increment_rows",
-    )(table, *row_stacks, *col_parts, *states, *before)
+    )(table, *row_stacks, *col_parts, *states, *before, *lefts)
 
 
 def stack(parts):
@@ -263,18 +273,25 @@
         )
         far_parts = [swap(part, "rows", n_rows, 1) for part in near_parts]
         others = list(range(1, n_cols))
-        first, *near_states = increment_rows(table, places[1:2], [1], members, near_parts, None, near, [], None)
-        before = {1: first}
-        before.update(
-            zip(
-                others[1:],
-                increment_rows(table, places[2:], others[1:], members, near_parts, near_states, near, [], None),
-            )
-        )
+        first, left, *near_states = increment_rows(
+            table, places[1:2], [1], members, near_parts, None, near, [], None
+        )
+        rest = increment_rows(table, places[2:], others[1:], members, near_parts, near_states, near, [], None)
+        before = dict(zip(others, [first, *rest[: len(others) - 1]]))
+        lefts = dict(zip(others, [left, *rest[len(others) - 1 :]]))
         received, far_states = [], None
         for flip in range(n_cols - 1, 0, -1):
             part, *fresh = increment_rows(
-                table, [places[flip]], [flip], members, far_parts, far_states, far, [before[flip]], BF16
+                table,
+                [places[flip]],
+                [flip],
+                members,
+                far_parts,
+                far_states,
+                far,
+                [before[flip]],
+                BF16,
+                [lefts[flip]],
             )
             far_states = far_states or fresh
             if flip > 1:

time: 28.9 us -> 28.9 us (level)
  transfers between devices with their start and end apart: 12 -> 12, of which waited for: 4 -> 4; matrix products, arithmetic and copies ran while one was open for 3% -> 3% of each run, Pallas kernels for 25% -> 24%
where the time goes in v7:
time: 28.9 us; the launch traced here: 28.7 us
  starting transfers between devices  14.8 us (51%)
  Pallas kernels  8.89 us (31%)
  waiting for transfers between devices  3.32 us (11%)
  other arithmetic  0.88 us (3%)
  between operations  0.79 us (3%)
    ppermute x12, starting transfers between devices, swap(): return lax.ppermute(x, axis, [(i, i ^ flip) for i in range(size)])  14.8 us
    pallas_call x6, Pallas kernels, increment_rows(): pl.pallas_call(kernel, out_shape=[jax.ShapeDtypeStruct(out, F32 if send i...  7.65 us
    ppermute x12, waiting for transfers between devices, swap(): return lax.ppermute(x, axis, [(i, i ^ flip) for i in range(size)])  3.32 us
    concatenate x1, other arithmetic, local(): packed = halves_apart(jnp.concatenate([anom, innov], axis=0))  0.88 us
    pallas_call x1, Pallas kernels, add_up(): pl.pallas_call(kernel, out_shape=jax.ShapeDtypeStruct(own.shape, F32), in...  0.69 us
  transfers between devices with their start and end apart: 12, of which 4 were waited for; matrix products, arithmetic and copies ran while one was open for 3% of the time, Pallas kernels for 24%

profile of v7, /device:TPU:0, one launch (start us, length us, event | category | flops | bytes accessed | tf_op | source)
XLA Modules:
  0.0 28.7 jit_solution(17420219263010024431)
XLA Ops:
  0.0 3.0 %collective-permute-start.7 = (bf16[64,512]{1,0:T(8,128)(2,1)}, bf16[64,512]{1,0:T(8,128)(2,1)S(1)}, u32[]{:S(2)}, u32[]{:S(2)}) collective-permute-start(bf16[64,512]{1,0:T(8,128)(2,1)} %bitcast.3), channel_id=1, source_target_pairs={{0,1},{1,0},{2,3},{3,2},{4,5},{5,4},{6,7},{7,6},{8,9},{9,8},{10,11... | collective-permute-start | bytes 196616 | tf_op jit(solution)/shard_map/ppermute | solution.py:251
  3.0 0.9 %pad_maximum_fusion.in_ref = bf16[128,512]{1,0:T(8,128)(2,1)S(1)} fusion(bf16[64,512]{1,0:T(8,128)(2,1)} %bitcast.7, bf16[64,512]{1,0:T(8,128)(2,1)} %bitcast.4), kind=kLoop, calls=%fused_computation | loop fusion | flops 262144 | bytes 262144 | tf_op jit(solution)/shard_map/concatenate | solution.py:261
  3.9 0.2 halves_apart.1.refs_1_
  4.2 2.5 %collective-permute-start.2 = (bf16[128,512]{1,0:T(8,128)(2,1)S(1)}, bf16[128,512]{1,0:T(8,128)(2,1)S(1)}, u32[]{:S(2)}, u32[]{:S(2)}) collective-permute-start(bf16[128,512]{1,0:T(8,128)(2,1)S(1)} %halves_apart.1.refs_1_), channel_id=1, source_target_pairs={{0,24},{4,28},{8,16},{12,20},{16,8},{20,12},{24,0},{28,4},{1,25},{... | collective-permute-start | bytes 393224 | tf_op jit(solution)/shard_map/ppermute | solution.py:251
  6.7 0.5 %collective-permute-start.1 = (bf16[128,512]{1,0:T(8,128)(2,1)S(1)}, bf16[128,512]{1,0:T(8,128)(2,1)S(1)}, u32[]{:S(2)}, u32[]{:S(2)}) collective-permute-start(bf16[128,512]{1,0:T(8,128)(2,1)S(1)} %halves_apart.1.refs_1_), channel_id=1, source_target_pairs={{0,16},{4,20},{8,24},{12,28},{16,0},{20,4},{24,8},{28,12},{1,17},{... | collective-permute-start | bytes 393224 | tf_op jit(solution)/shard_map/ppermute | solution.py:251
  7.2 0.5 %collective-permute-start = (bf16[128,512]{1,0:T(8,128)(2,1)S(1)}, bf16[128,512]{1,0:T(8,128)(2,1)S(1)}, u32[]{:S(2)}, u32[]{:S(2)}) collective-permute-start(bf16[128,512]{1,0:T(8,128)(2,1)S(1)} %halves_apart.1.refs_1_), channel_id=1, source_target_pairs={{0,8},{4,12},{8,0},{12,4},{16,24},{20,28},{24,16},{28,20},{1,9},{5... | collective-permute-start | bytes 393224 | tf_op jit(solution)/shard_map/ppermute | solution.py:251
  7.8 2.7 %collective-permute-start.8 = (bf16[128,512]{1,0:T(8,128)(2,1)S(1)}, bf16[128,512]{1,0:T(8,128)(2,1)S(1)}, u32[]{:S(2)}, u32[]{:S(2)}) collective-permute-start(bf16[128,512]{1,0:T(8,128)(2,1)S(1)} %stack.1), channel_id=1, source_target_pairs={{0,2},{1,3},{2,0},{3,1},{4,6},{5,7},{6,4},{7,5},{8,10},{9,11},{10,... | collective-permute-start | bytes 393224 | tf_op jit(solution)/shard_map/ppermute | solution.py:251
  11.1 0.3 %pair_table.1.table_ref = f32[16,2048]{1,0:T(8,128)S(1)} custom-call(s32[1,512]{1,0:T(1,128)S(1)} %copy-done.1, s32[1,512]{1,0:T(1,128)S(1)} %copy-done.2, s32[1,512]{1,0:T(1,128)S(1)} %copy-done.3, s32[1,1]{1,0:T(1,128)S(6)} %copy.7.count_ref), custom_call_target="tpu_custom_call" | custom-call | tf_op jit(solution)/shard_map/pair_table/pallas_call | solution.py:38
  11.4 0.6 %collective-permute-start.6 = (bf16[128,512]{1,0:T(8,128)(2,1)S(1)}, bf16[128,512]{1,0:T(8,128)(2,1)S(1)}, u32[]{:S(2)}, u32[]{:S(2)}) collective-permute-start(bf16[128,512]{1,0:T(8,128)(2,1)S(1)} %collective-permute-done.2.refs_4_), channel_id=1, source_target_pairs={{0,4},{4,0},{8,12},{12,8},{16,20},{20,16},{24,28},{28,24},{1,5},{5... | collective-permute-start | bytes 393224 | tf_op jit(solution)/shard_map/ppermute | solution.py:251
  12.0 0.9 %collective-permute-done.1.refs_3_ = bf16[128,512]{1,0:T(8,128)(2,1)S(1)} collective-permute-done((bf16[128,512]{1,0:T(8,128)(2,1)S(1)}, bf16[128,512]{1,0:T(8,128)(2,1)S(1)}, u32[]{:S(2)}, u32[]{:S(2)}) %collective-permute-start.1) | collective-permute-done | bytes 131104 | tf_op jit(solution)/shard_map/ppermute | solution.py:251
  12.9 0.1 collective-permute-done.refs_2_
  13.0 0.4 %collective-permute-start.4 = (bf16[128,512]{1,0:T(8,128)(2,1)S(1)}, bf16[128,512]{1,0:T(8,128)(2,1)S(1)}, u32[]{:S(2)}, u32[]{:S(2)}) collective-permute-start(bf16[128,512]{1,0:T(8,128)(2,1)S(1)} %collective-permute-done.refs_2_), channel_id=1, source_target_pairs={{0,4},{4,0},{8,12},{12,8},{16,20},{20,16},{24,28},{28,24},{1,5},{5... | collective-permute-start | bytes 393224 | tf_op jit(solution)/shard_map/ppermute | solution.py:251
  13.4 1.2 %increment_rows.6 = (f32[512,64]{1,0:T(8,128)S(1)}, bf16[2,256,64]{2,1,0:T(8,128)(2,1)S(1)}, f32[128,256]{1,0:T(8,128)S(1)}, f32[128,256]{1,0:T(8,128)S(1)}, f32...) custom-call(f32[16,2048]{1,0:T(8,128)S(1)} %pair_table.1.table_ref, ...), custom_call_target="tpu_custom_call" | custom-call | flops 1073741824 | bytes 524288 | tf_op jit(solution)/shard_map/increment_rows/pallas_call | solution.py:189
  14.6 0.9 %collective-permute-done.8.refs_0_ = bf16[128,512]{1,0:T(8,128)(2,1)S(1)} collective-permute-done((bf16[128,512]{1,0:T(8,128)(2,1)S(1)}, bf16[128,512]{1,0:T(8,128)(2,1)S(1)}, u32[]{:S(2)}, u32[]{:S(2)}) %collective-permute-start.8) | collective-permute-done | bytes 131104 | tf_op jit(solution)/shard_map/ppermute | solution.py:251
  15.5 1.6 %increment_rows.7 = (f32[512,64]{1,0:T(8,128)S(1)}, f32[512,64]{1,0:T(8,128)S(1)}, bf16[2,256,64]{2,1,0:T(8,128)(2,1)S(1)}, bf16[2,256,64]{2,1,0:T(8,128)(2,1)S(1)}) custom-call(f32[16,2048]{1,0:T(8,128)S(1)} %pair_table.1.table_ref, bf16[128,512]{1,0:T(8,128)(2,1)S(1)} %collective-permute-done.8.refs_0_, bf16[128,512]{1,0:T(8,128)(2,1)S(1)} %halves_apart.1.refs_1_, ...), custom_call_target="tpu_custom_call" | custom-call | flops 2147483648 | bytes 524288 | tf_op jit(solution)/shard_map/increment_rows/pallas_call | solution.py:189
  17.1 1.3 %increment_rows.8 = (bf16[64,512]{1,0:T(8,128)(2,1)S(1)}, f32[128,256]{1,0:T(8,128)S(1)}, f32[128,256]{1,0:T(8,128)S(1)}, f32[128,256]{1,0:T(8,128)S(1)}, f32[128,256]{1,0:T(8,128)S(1)}) custom-call(f32[16,2048]{1,0:T(8,128)S(1)} %pair_table.1.table_ref, bf16[128,512]{1,0:T(8,128)(2,1)S(1)} %collective-permute-done.3.refs_0_.refs_5_, ...), custom_call_target="tpu_custom_call" | custom-call | flops 1073741824 | bytes 524288 | tf_op jit(solution)/shard_map/increment_rows/pallas_call | solution.py:189
  18.4 2.7 %collective-permute-start.9 = (bf16[64,512]{1,0:T(8,128)(2,1)S(1)}, bf16[64,512]{1,0:T(8,128)(2,1)S(1)}, u32[]{:S(2)}, u32[]{:S(2)}) collective-permute-start(bf16[64,512]{1,0:T(8,128)(2,1)S(1)} %get-tuple-element.32), channel_id=1, source_target_pairs={{0,3},{1,2},{2,1},{3,0},{4,7},{5,6},{6,5},{7,4},{8,11},{9,10},{10,... | collective-permute-start | bytes 196616 | tf_op jit(solution)/shard_map/ppermute | solution.py:251
  21.1 0.9 %increment_rows.10 = bf16[64,512]{1,0:T(8,128)(2,1)S(1)} custom-call(f32[16,2048]{1,0:T(8,128)S(1)} %pair_table.1.table_ref, bf16[128,512]{1,0:T(8,128)(2,1)S(1)} %collective-permute-done.3.refs_0_.refs_5_, bf16[128,512]{1,0:T(8,128)(2,1)S(1)} %collective-permute-done.4.refs_1_.refs_6_, bf16[128,512]{1,0:T(8,128)(2,1)S(1)} %collective-permute-done.5.refs_2_.refs_7_, ...), custom_call_target="tpu_custom_call" | custom-call | flops 1073741824 | bytes 524288 | tf_op jit(solution)/shard_map/increment_rows/pallas_call | solution.py:189
  22.0 0.1 collective-permute-start.10
  22.1 0.9 %increment_rows.11 = bf16[64,512]{1,0:T(8,128)(2,1)S(1)} custom-call(f32[16,2048]{1,0:T(8,128)S(1)} %pair_table.1.table_ref, bf16[128,512]{1,0:T(8,128)(2,1)S(1)} %collective-permute-done.3.refs_0_.refs_5_, bf16[128,512]{1,0:T(8,128)(2,1)S(1)} %collective-permute-done.4.refs_1_.refs_6_, bf16[128,512]{1,0:T(8,128)(2,1)S(1)} %collective-permute-done.5.refs_2_.refs_7_, ...), custom_call_target="tpu_custom_call" | custom-call | flops 1073741824 | bytes 524288 | tf_op jit(solution)/shard_map/increment_rows/pallas_call | solution.py:189
  23.0 1.8 %collective-permute-start.11 = (bf16[64,512]{1,0:T(8,128)(2,1)S(1)}, bf16[64,512]{1,0:T(8,128)(2,1)S(1)}, u32[]{:S(2)}, u32[]{:S(2)}) collective-permute-start(bf16[64,512]{1,0:T(8,128)(2,1)S(1)} %increment_rows.11), channel_id=1, source_target_pairs={{0,1},{1,0},{2,3},{3,2},{4,5},{5,4},{6,7},{7,6},{8,9},{9,8},{10,11... | collective-permute-start | bytes 196616 | tf_op jit(solution)/shard_map/ppermute | solution.py:251
  24.8 1.7 %increment_rows.9.refs_0_ = f32[64,512]{1,0:T(8,128)S(1)} custom-call(f32[16,2048]{1,0:T(8,128)S(1)} %pair_table.1.table_ref, bf16[64,512]{1,0:T(8,128)(2,1)S(1)} %bitcast.6, bf16[128,512]{1,0:T(8,128)(2,1)S(1)} %halves_apart.1.refs_1_, bf16[128,512]{1,0:T(8,128)(2,1)S(1)} %collective-permute-done.refs_2_, ...), custom_call_target="tpu_custom_call" | custom-call | flops 2147483648 | bytes 1048576 | tf_op jit(solution)/shard_map/increment_rows/pallas_call | solution.py:189
  26.6 1.5 %collective-permute-done.11.refs_3_ = bf16[64,512]{1,0:T(8,128)(2,1)S(1)} collective-permute-done((bf16[64,512]{1,0:T(8,128)(2,1)S(1)}, bf16[64,512]{1,0:T(8,128)(2,1)S(1)}, u32[]{:S(2)}, u32[]{:S(2)}) %collective-permute-start.11) | collective-permute-done | bytes 65568 | tf_op jit(solution)/shard_map/ppermute | solution.py:251
  28.0 0.7 %add_up.1 = f32[64,512]{1,0:T(8,128)} custom-call(f32[64,512]{1,0:T(8,128)S(1)} %increment_rows.9.refs_0_, bf16[64,512]{1,0:T(8,128)(2,1)S(1)} %collective-permute-done.9.refs_1_, bf16[64,512]{1,0:T(8,128)(2,1)S(1)} %collective-permute-done.10.refs_2_, bf16[64,512]{1,0:T(8,128)(2,1)S(1)} %collective-permute-done.11.refs_3_), custom_call_target="tpu_custom_call" | custom-call | tf_op jit(solution)/shard_map/add_up/pallas_call | solution.py:240
  (19 shorter events, 0.1 us)
Async XLA Ops:
  0.0 7.7 %collective-permute-start.7 = (bf16[64,512]{1,0:T(8,128)(2,1)}, bf16[64,512]{1,0:T(8,128)(2,1)S(1)}, u32[]{:S(2)}, u32[]{:S(2)}) collective-permute-start(bf16[64,512]{1,0:T(8,128)(2,1)} %bitcast.3), channel_id=1, source_target_pairs={{0,1},{1,0},{2,3},{3,2},{4,5},{5,4},{6,7},{7,6},{8,9},{9,8},{10,11... | collective-permute-start | bytes 196616 | tf_op jit(solution)/shard_map/ppermute | solution.py:251
  3.9 3.8 %copy-start = (bf16[512,64]{0,1:T(8,128)(2,1)S(1)}, bf16[512,64]{0,1:T(8,128)(2,1)}, u32[]{:S(2)}) copy-start(bf16[512,64]{0,1:T(8,128)(2,1)} %param.6) | copy-start | bytes 196612
  4.2 7.3 %collective-permute-start.2 = (bf16[128,512]{1,0:T(8,128)(2,1)S(1)}, bf16[128,512]{1,0:T(8,128)(2,1)S(1)}, u32[]{:S(2)}, u32[]{:S(2)}) collective-permute-start(bf16[128,512]{1,0:T(8,128)(2,1)S(1)} %halves_apart.1.refs_1_), channel_id=1, source_target_pairs={{0,24},{4,28},{8,16},{12,20},{16,8},{20,12},{24,0},{28,4},{1,25},{... | collective-permute-start | bytes 393224 | tf_op jit(solution)/shard_map/ppermute | solution.py:251
  6.7 6.2 %collective-permute-start.1 = (bf16[128,512]{1,0:T(8,128)(2,1)S(1)}, bf16[128,512]{1,0:T(8,128)(2,1)S(1)}, u32[]{:S(2)}, u32[]{:S(2)}) collective-permute-start(bf16[128,512]{1,0:T(8,128)(2,1)S(1)} %halves_apart.1.refs_1_), channel_id=1, source_target_pairs={{0,16},{4,20},{8,24},{12,28},{16,0},{20,4},{24,8},{28,12},{1,17},{... | collective-permute-start | bytes 393224 | tf_op jit(solution)/shard_map/ppermute | solution.py:251
  7.2 5.8 %collective-permute-start = (bf16[128,512]{1,0:T(8,128)(2,1)S(1)}, bf16[128,512]{1,0:T(8,128)(2,1)S(1)}, u32[]{:S(2)}, u32[]{:S(2)}) collective-permute-start(bf16[128,512]{1,0:T(8,128)(2,1)S(1)} %halves_apart.1.refs_1_), channel_id=1, source_target_pairs={{0,8},{4,12},{8,0},{12,4},{16,24},{20,28},{24,16},{28,20},{1,9},{5... | collective-permute-start | bytes 393224 | tf_op jit(solution)/shard_map/ppermute | solution.py:251
  7.7 3.4 %copy-start.1 = (s32[1,512]{1,0:T(1,128)S(1)}, s32[1,512]{1,0:T(1,128)}, u32[]{:S(2)}) copy-start(s32[1,512]{1,0:T(1,128)} %rows_ref.1) | copy-start | bytes 6148
  7.7 3.4 %copy-start.2 = (s32[1,512]{1,0:T(1,128)S(1)}, s32[1,512]{1,0:T(1,128)}, u32[]{:S(2)}) copy-start(s32[1,512]{1,0:T(1,128)} %cols_ref.1) | copy-start | bytes 6148
  7.7 3.4 %copy-start.3 = (s32[1,512]{1,0:T(1,128)S(1)}, s32[1,512]{1,0:T(1,128)}, u32[]{:S(2)}) copy-start(s32[1,512]{1,0:T(1,128)} %dist_ref.1) | copy-start | bytes 6148
  7.8 7.7 %collective-permute-start.8 = (bf16[128,512]{1,0:T(8,128)(2,1)S(1)}, bf16[128,512]{1,0:T(8,128)(2,1)S(1)}, u32[]{:S(2)}, u32[]{:S(2)}) collective-permute-start(bf16[128,512]{1,0:T(8,128)(2,1)S(1)} %stack.1), channel_id=1, source_target_pairs={{0,2},{1,3},{2,0},{3,1},{4,6},{5,7},{6,4},{7,5},{8,10},{9,11},{10,... | collective-permute-start | bytes 393224 | tf_op jit(solution)/shard_map/ppermute | solution.py:251
  10.4 6.7 %collective-permute-start.3 = (bf16[128,512]{1,0:T(8,128)(2,1)S(1)}, bf16[128,512]{1,0:T(8,128)(2,1)S(1)}, u32[]{:S(2)}, u32[]{:S(2)}) collective-permute-start(bf16[128,512]{1,0:T(8,128)(2,1)S(1)} %halves_apart.1.refs_1_), channel_id=1, source_target_pairs={{0,4},{4,0},{8,12},{12,8},{16,20},{20,16},{24,28},{28,24},{1,5},{5... | collective-permute-start | bytes 393224 | tf_op jit(solution)/shard_map/ppermute | solution.py:251
  11.4 5.7 %collective-permute-start.6 = (bf16[128,512]{1,0:T(8,128)(2,1)S(1)}, bf16[128,512]{1,0:T(8,128)(2,1)S(1)}, u32[]{:S(2)}, u32[]{:S(2)}) collective-permute-start(bf16[128,512]{1,0:T(8,128)(2,1)S(1)} %collective-permute-done.2.refs_4_), channel_id=1, source_target_pairs={{0,4},{4,0},{8,12},{12,8},{16,20},{20,16},{24,28},{28,24},{1,5},{5... | collective-permute-start | bytes 393224 | tf_op jit(solution)/shard_map/ppermute | solution.py:251
  12.9 4.2 %collective-permute-start.5 = (bf16[128,512]{1,0:T(8,128)(2,1)S(1)}, bf16[128,512]{1,0:T(8,128)(2,1)S(1)}, u32[]{:S(2)}, u32[]{:S(2)}) collective-permute-start(bf16[128,512]{1,0:T(8,128)(2,1)S(1)} %collective-permute-done.1.refs_3_), channel_id=1, source_target_pairs={{0,4},{4,0},{8,12},{12,8},{16,20},{20,16},{24,28},{28,24},{1,5},{5... | collective-permute-start | bytes 393224 | tf_op jit(solution)/shard_map/ppermute | solution.py:251
  13.0 4.2 %collective-permute-start.4 = (bf16[128,512]{1,0:T(8,128)(2,1)S(1)}, bf16[128,512]{1,0:T(8,128)(2,1)S(1)}, u32[]{:S(2)}, u32[]{:S(2)}) collective-permute-start(bf16[128,512]{1,0:T(8,128)(2,1)S(1)} %collective-permute-done.refs_2_), channel_id=1, source_target_pairs={{0,4},{4,0},{8,12},{12,8},{16,20},{20,16},{24,28},{28,24},{1,5},{5... | collective-permute-start | bytes 393224 | tf_op jit(solution)/shard_map/ppermute | solution.py:251
  18.4 9.6 %collective-permute-start.9 = (bf16[64,512]{1,0:T(8,128)(2,1)S(1)}, bf16[64,512]{1,0:T(8,128)(2,1)S(1)}, u32[]{:S(2)}, u32[]{:S(2)}) collective-permute-start(bf16[64,512]{1,0:T(8,128)(2,1)S(1)} %get-tuple-element.32), channel_id=1, source_target_pairs={{0,3},{1,2},{2,1},{3,0},{4,7},{5,6},{6,5},{7,4},{8,11},{9,10},{10,... | collective-permute-start | bytes 196616 | tf_op jit(solution)/shard_map/ppermute | solution.py:251
  22.0 6.0 %collective-permute-start.10 = (bf16[64,512]{1,0:T(8,128)(2,1)S(1)}, bf16[64,512]{1,0:T(8,128)(2,1)S(1)}, u32[]{:S(2)}, u32[]{:S(2)}) collective-permute-start(bf16[64,512]{1,0:T(8,128)(2,1)S(1)} %increment_rows.10), channel_id=1, source_target_pairs={{0,2},{1,3},{2,0},{3,1},{4,6},{5,7},{6,4},{7,5},{8,10},{9,11},{10,... | collective-permute-start | bytes 196616 | tf_op jit(solution)/shard_map/ppermute | solution.py:251
  23.0 5.0 %collective-permute-start.11 = (bf16[64,512]{1,0:T(8,128)(2,1)S(1)}, bf16[64,512]{1,0:T(8,128)(2,1)S(1)}, u32[]{:S(2)}, u32[]{:S(2)}) collective-permute-start(bf16[64,512]{1,0:T(8,128)(2,1)S(1)} %increment_rows.11), channel_id=1, source_target_pairs={{0,1},{1,0},{2,3},{3,2},{4,5},{5,4},{6,7},{7,6},{8,9},{9,8},{10,11... | collective-permute-start | bytes 196616 | tf_op jit(solution)/shard_map/ppermute | solution.py:251

commit v8 on v6

--- a/solution.py
+++ b/solution.py
@@ -43,28 +43,6 @@
         compiler_params=SMALL,
         name="pair_table",
     )(pair_rows, pair_cols, pair_dist, pair_counts)
-
-
-def halves_apart(packed):
-    height, cells = packed.shape
-    wide = cells // 2
-
-    def kernel(in_ref, out_ref):
-        source = lax.broadcasted_iota(jnp.int32, (cells, cells), 0)
-        lane = lax.broadcasted_iota(jnp.int32, (cells, cells), 1)
-        inner = lane % wide
-        wanted = inner // HALF * BLK + lane // wide * HALF + inner % HALF
-        order = (source == wanted).astype(F32).astype(BF16)
-        out_ref[...] = jnp.dot(in_ref[...], order, preferred_element_type=F32).astype(BF16)
-
-    return pl.pallas_call(
-        kernel,
-        out_shape=jax.ShapeDtypeStruct((height, cells), BF16),
-        in_specs=[VMEM],
-        out_specs=VMEM,
-        compiler_params=SMALL,
-        name="halves_apart",
-    )(packed)
 
 
 def fade(shape, axis, rising):
@@ -248,7 +226,8 @@
         per_dev = anomalies.shape[0] // BLK
         members = anomalies.shape[1]
         anom, innov = anomalies.T, innovations.T
-        packed = halves_apart(jnp.concatenate([anom, innov], axis=0))
+        both = jnp.concatenate([anom, innov], axis=0).reshape(-1, per_dev, 2, HALF)
+        packed = both.transpose(0, 2, 1, 3).reshape(both.shape[0], -1)
         near = list(range(0, n_rows, 2))
         far = [flip + 1 for flip in near]
         places, held = [(anom, 0)], [anom]

time: 28.9 us -> 28.9 us (level)
  transfers between devices with their start and end apart: 12 -> 12, of which waited for: 4 -> 4; matrix products, arithmetic and copies ran while one was open for 3% -> 4% of each run, Pallas kernels for 25% -> 24%
where the time goes in v8:
time: 28.9 us; the launch traced here: 28.7 us
  starting transfers between devices  14.8 us (51%)
  Pallas kernels  8.79 us (30%)
  waiting for transfers between devices  3.18 us (11%)
  other arithmetic  0.88 us (3%)
  between operations  0.8 us (3%)
    ppermute x12, starting transfers between devices, swap(): return lax.ppermute(x, axis, [(i, i ^ flip) for i in range(size)])  14.8 us
    pallas_call x6, Pallas kernels, increment_rows(): pl.pallas_call(kernel, out_shape=[jax.ShapeDtypeStruct(out, F32 if send i...  7.79 us
    ppermute x12, waiting for transfers between devices, swap(): return lax.ppermute(x, axis, [(i, i ^ flip) for i in range(size)])  3.18 us
    concatenate x1, other arithmetic, local(): both = jnp.concatenate([anom, innov], axis=0).reshape(-1, per_dev, 2, HALF)  0.88 us
    pallas_call x1, Pallas kernels, add_up(): pl.pallas_call(kernel, out_shape=jax.ShapeDtypeStruct(own.shape, F32), in...  0.69 us
  transfers between devices with their start and end apart: 12, of which 4 were waited for; matrix products, arithmetic and copies ran while one was open for 4% of the time, Pallas kernels for 24%

profile of v8, /device:TPU:0, one launch (start us, length us, event | category | flops | bytes accessed | tf_op | source)
XLA Modules:
  0.0 28.7 jit_solution(16860320107356205826)
XLA Ops:
  0.0 3.0 %collective-permute-start.7 = (bf16[64,512]{1,0:T(8,128)(2,1)}, bf16[64,512]{1,0:T(8,128)(2,1)S(1)}, u32[]{:S(2)}, u32[]{:S(2)}) collective-permute-start(bf16[64,512]{1,0:T(8,128)(2,1)} %bitcast.7), channel_id=1, source_target_pairs={{0,1},{1,0},{2,3},{3,2},{4,5},{5,4},{6,7},{7,6},{8,9},{9,8},{10,11... | collective-permute-start | bytes 196616 | tf_op jit(solution)/shard_map/ppermute | solution.py:219
  3.0 0.9 %pad_maximum_fusion = bf16[128,512]{1,0:T(8,128)(2,1)S(1)} fusion(bf16[64,512]{1,0:T(8,128)(2,1)} %bitcast.13, bf16[64,512]{1,0:T(8,128)(2,1)} %bitcast.8), kind=kLoop, calls=%fused_computation | loop fusion | flops 262144 | bytes 262144 | tf_op jit(solution)/shard_map/concatenate | solution.py:229
  3.9 0.1 copy.8
  4.1 0.1 copy.16.refs_1_
  4.2 2.5 %collective-permute-start.2 = (bf16[128,512]{1,0:T(8,128)(2,1)S(1)}, bf16[128,512]{1,0:T(8,128)(2,1)S(1)}, u32[]{:S(2)}, u32[]{:S(2)}) collective-permute-start(bf16[128,512]{1,0:T(8,128)(2,1)S(1)} %copy.16.refs_1_), channel_id=1, source_target_pairs={{0,24},{4,28},{8,16},{12,20},{16,8},{20,12},{24,0},{28,4},{1,25},{... | collective-permute-start | bytes 393224 | tf_op jit(solution)/shard_map/ppermute | solution.py:219
  6.7 0.5 %collective-permute-start.1 = (bf16[128,512]{1,0:T(8,128)(2,1)S(1)}, bf16[128,512]{1,0:T(8,128)(2,1)S(1)}, u32[]{:S(2)}, u32[]{:S(2)}) collective-permute-start(bf16[128,512]{1,0:T(8,128)(2,1)S(1)} %copy.16.refs_1_), channel_id=1, source_target_pairs={{0,16},{4,20},{8,24},{12,28},{16,0},{20,4},{24,8},{28,12},{1,17},{... | collective-permute-start | bytes 393224 | tf_op jit(solution)/shard_map/ppermute | solution.py:219
  7.2 0.5 %collective-permute-start = (bf16[128,512]{1,0:T(8,128)(2,1)S(1)}, bf16[128,512]{1,0:T(8,128)(2,1)S(1)}, u32[]{:S(2)}, u32[]{:S(2)}) collective-permute-start(bf16[128,512]{1,0:T(8,128)(2,1)S(1)} %copy.16.refs_1_), channel_id=1, source_target_pairs={{0,8},{4,12},{8,0},{12,4},{16,24},{20,28},{24,16},{28,20},{1,9},{5... | collective-permute-start | bytes 393224 | tf_op jit(solution)/shard_map/ppermute | solution.py:219
  7.8 2.7 %collective-permute-start.8 = (bf16[128,512]{1,0:T(8,128)(2,1)S(1)}, bf16[128,512]{1,0:T(8,128)(2,1)S(1)}, u32[]{:S(2)}, u32[]{:S(2)}) collective-permute-start(bf16[128,512]{1,0:T(8,128)(2,1)S(1)} %stack.1), channel_id=1, source_target_pairs={{0,2},{1,3},{2,0},{3,1},{4,6},{5,7},{6,4},{7,5},{8,10},{9,11},{10,... | collective-permute-start | bytes 393224 | tf_op jit(solution)/shard_map/ppermute | solution.py:219
  11.1 0.3 %pair_table.1.table_ref = f32[16,2048]{1,0:T(8,128)S(1)} custom-call(s32[1,512]{1,0:T(1,128)S(1)} %copy-done.1, s32[1,512]{1,0:T(1,128)S(1)} %copy-done.2, s32[1,512]{1,0:T(1,128)S(1)} %copy-done.3, s32[1,1]{1,0:T(1,128)S(6)} %copy.17.count_ref), custom_call_target="tpu_custom_call" | custom-call | tf_op jit(solution)/shard_map/pair_table/pallas_call | solution.py:38
  11.4 0.6 %collective-permute-start.6 = (bf16[128,512]{1,0:T(8,128)(2,1)S(1)}, bf16[128,512]{1,0:T(8,128)(2,1)S(1)}, u32[]{:S(2)}, u32[]{:S(2)}) collective-permute-start(bf16[128,512]{1,0:T(8,128)(2,1)S(1)} %collective-permute-done.2.refs_4_), channel_id=1, source_target_pairs={{0,4},{4,0},{8,12},{12,8},{16,20},{20,16},{24,28},{28,24},{1,5},{5... | collective-permute-start | bytes 393224 | tf_op jit(solution)/shard_map/ppermute | solution.py:219
  12.0 0.9 %collective-permute-done.1.refs_3_ = bf16[128,512]{1,0:T(8,128)(2,1)S(1)} collective-permute-done((bf16[128,512]{1,0:T(8,128)(2,1)S(1)}, bf16[128,512]{1,0:T(8,128)(2,1)S(1)}, u32[]{:S(2)}, u32[]{:S(2)}) %collective-permute-start.1) | collective-permute-done | bytes 131104 | tf_op jit(solution)/shard_map/ppermute | solution.py:219
  13.0 0.4 %collective-permute-start.4 = (bf16[128,512]{1,0:T(8,128)(2,1)S(1)}, bf16[128,512]{1,0:T(8,128)(2,1)S(1)}, u32[]{:S(2)}, u32[]{:S(2)}) collective-permute-start(bf16[128,512]{1,0:T(8,128)(2,1)S(1)} %collective-permute-done.refs_2_), channel_id=1, source_target_pairs={{0,4},{4,0},{8,12},{12,8},{16,20},{20,16},{24,28},{28,24},{1,5},{5... | collective-permute-start | bytes 393224 | tf_op jit(solution)/shard_map/ppermute | solution.py:219
  13.4 1.2 %increment_rows.6 = (f32[512,64]{1,0:T(8,128)S(1)}, f32[128,256]{1,0:T(8,128)S(1)}, f32[128,256]{1,0:T(8,128)S(1)}, f32[128,256]{1,0:T(8,128)S(1)}, f32[128,256]{1,0:T(8,128)S(1)}) custom-call(f32[16,2048]{1,0:T(8,128)S(1)} %pair_table.1.table_ref, bf16[64,512]{1,0:T(8,128)(2,1)S(1)} %collective-permute-done.7.refs_0_.refs_1_, ...), custom_call_target="tpu_custom_call" | custom-call | flops 1073741824 | bytes 524288 | tf_op jit(solution)/shard_map/increment_rows/pallas_call | solution.py:158
  14.6 0.9 %collective-permute-done.8.refs_0_ = bf16[128,512]{1,0:T(8,128)(2,1)S(1)} collective-permute-done((bf16[128,512]{1,0:T(8,128)(2,1)S(1)}, bf16[128,512]{1,0:T(8,128)(2,1)S(1)}, u32[]{:S(2)}, u32[]{:S(2)}) %collective-permute-start.8) | collective-permute-done | bytes 131104 | tf_op jit(solution)/shard_map/ppermute | solution.py:219
  15.5 1.6 %increment_rows.7 = (f32[512,64]{1,0:T(8,128)S(1)}, f32[512,64]{1,0:T(8,128)S(1)}) custom-call(f32[16,2048]{1,0:T(8,128)S(1)} %pair_table.1.table_ref, bf16[128,512]{1,0:T(8,128)(2,1)S(1)} %collective-permute-done.8.refs_0_, bf16[128,512]{1,0:T(8,128)(2,1)S(1)} %copy.16.refs_1_, bf16[128,512]{1,0:T(8,128)(2,1)S(1)} %collective-permute-done.refs_2_, ...), custom_call_target="tpu_custom_call" | custom-call | flops 2147483648 | bytes 524288 | tf_op jit(solution)/shard_map/increment_rows/pallas_call | solution.py:158
  17.1 1.3 %increment_rows.8 = (bf16[64,512]{1,0:T(8,128)(2,1)S(1)}, f32[128,256]{1,0:T(8,128)S(1)}, f32[128,256]{1,0:T(8,128)S(1)}, f32[128,256]{1,0:T(8,128)S(1)}, f32[128,256]{1,0:T(8,128)S(1)}) custom-call(f32[16,2048]{1,0:T(8,128)S(1)} %pair_table.1.table_ref, bf16[128,512]{1,0:T(8,128)(2,1)S(1)} %collective-permute-done.8.refs_0_, ...), custom_call_target="tpu_custom_call" | custom-call | flops 1073741824 | bytes 524288 | tf_op jit(solution)/shard_map/increment_rows/pallas_call | solution.py:158
  18.4 2.7 %collective-permute-start.9 = (bf16[64,512]{1,0:T(8,128)(2,1)S(1)}, bf16[64,512]{1,0:T(8,128)(2,1)S(1)}, u32[]{:S(2)}, u32[]{:S(2)}) collective-permute-start(bf16[64,512]{1,0:T(8,128)(2,1)S(1)} %get-tuple-element.28), channel_id=1, source_target_pairs={{0,3},{1,2},{2,1},{3,0},{4,7},{5,6},{6,5},{7,4},{8,11},{9,10},{10,... | collective-permute-start | bytes 196616 | tf_op jit(solution)/shard_map/ppermute | solution.py:219
  21.1 1.0 %increment_rows.10 = bf16[64,512]{1,0:T(8,128)(2,1)S(1)} custom-call(f32[16,2048]{1,0:T(8,128)S(1)} %pair_table.1.table_ref, bf16[128,512]{1,0:T(8,128)(2,1)S(1)} %collective-permute-done.8.refs_0_, bf16[128,512]{1,0:T(8,128)(2,1)S(1)} %collective-permute-done.3.refs_1_.refs_5_, bf16[128,512]{1,0:T(8,128)(2,1)S(1)} %collective-permute-done.4.refs_2_.refs_6_, ...), custom_call_target="tpu_custom_call" | custom-call | flops 1073741824 | bytes 524288 | tf_op jit(solution)/shard_map/increment_rows/pallas_call | solution.py:158
  22.1 0.1 collective-permute-start.10
  22.2 1.0 %increment_rows.11 = bf16[64,512]{1,0:T(8,128)(2,1)S(1)} custom-call(f32[16,2048]{1,0:T(8,128)S(1)} %pair_table.1.table_ref, bf16[64,512]{1,0:T(8,128)(2,1)S(1)} %collective-permute-done.7.refs_0_.refs_1_, bf16[128,512]{1,0:T(8,128)(2,1)S(1)} %collective-permute-done.3.refs_1_.refs_5_, bf16[128,512]{1,0:T(8,128)(2,1)S(1)} %collective-permute-done.4.refs_2_.refs_6_, ...), custom_call_target="tpu_custom_call" | custom-call | flops 1073741824 | bytes 524288 | tf_op jit(solution)/shard_map/increment_rows/pallas_call | solution.py:158
  23.2 1.8 %collective-permute-start.11 = (bf16[64,512]{1,0:T(8,128)(2,1)S(1)}, bf16[64,512]{1,0:T(8,128)(2,1)S(1)}, u32[]{:S(2)}, u32[]{:S(2)}) collective-permute-start(bf16[64,512]{1,0:T(8,128)(2,1)S(1)} %increment_rows.11), channel_id=1, source_target_pairs={{0,1},{1,0},{2,3},{3,2},{4,5},{5,4},{6,7},{7,6},{8,9},{9,8},{10,11... | collective-permute-start | bytes 196616 | tf_op jit(solution)/shard_map/ppermute | solution.py:219
  25.0 1.7 %increment_rows.9.refs_0_ = f32[64,512]{1,0:T(8,128)S(1)} custom-call(f32[16,2048]{1,0:T(8,128)S(1)} %pair_table.1.table_ref, bf16[64,512]{1,0:T(8,128)(2,1)S(1)} %bitcast.10, bf16[128,512]{1,0:T(8,128)(2,1)S(1)} %copy.16.refs_1_, bf16[128,512]{1,0:T(8,128)(2,1)S(1)} %collective-permute-done.refs_2_, bf16[128,512]{1,0:T(8,128)(2,1)S(1)} %collective-permute-done.1.refs_3_, ...), custom_call_target="tpu_custom_call" | custom-call | flops 2147483648 | bytes 1048576 | tf_op jit(solution)/shard_map/increment_rows/pallas_call | solution.py:158
  26.7 1.3 %collective-permute-done.11.refs_3_ = bf16[64,512]{1,0:T(8,128)(2,1)S(1)} collective-permute-done((bf16[64,512]{1,0:T(8,128)(2,1)S(1)}, bf16[64,512]{1,0:T(8,128)(2,1)S(1)}, u32[]{:S(2)}, u32[]{:S(2)}) %collective-permute-start.11) | collective-permute-done | bytes 65568 | tf_op jit(solution)/shard_map/ppermute | solution.py:219
  28.0 0.7 %add_up.1 = f32[64,512]{1,0:T(8,128)} custom-call(f32[64,512]{1,0:T(8,128)S(1)} %increment_rows.9.refs_0_, bf16[64,512]{1,0:T(8,128)(2,1)S(1)} %collective-permute-done.9.refs_1_, bf16[64,512]{1,0:T(8,128)(2,1)S(1)} %collective-permute-done.10.refs_2_, bf16[64,512]{1,0:T(8,128)(2,1)S(1)} %collective-permute-done.11.refs_3_), custom_call_target="tpu_custom_call" | custom-call | tf_op jit(solution)/shard_map/add_up/pallas_call | solution.py:208
  (21 shorter events, 0.1 us)
Async XLA Ops:
  0.0 7.7 %collective-permute-start.7 = (bf16[64,512]{1,0:T(8,128)(2,1)}, bf16[64,512]{1,0:T(8,128)(2,1)S(1)}, u32[]{:S(2)}, u32[]{:S(2)}) collective-permute-start(bf16[64,512]{1,0:T(8,128)(2,1)} %bitcast.7), channel_id=1, source_target_pairs={{0,1},{1,0},{2,3},{3,2},{4,5},{5,4},{6,7},{7,6},{8,9},{9,8},{10,11... | collective-permute-start | bytes 196616 | tf_op jit(solution)/shard_map/ppermute | solution.py:219
  4.1 3.7 %copy-start = (bf16[512,64]{0,1:T(8,128)(2,1)S(1)}, bf16[512,64]{0,1:T(8,128)(2,1)}, u32[]{:S(2)}) copy-start(bf16[512,64]{0,1:T(8,128)(2,1)} %param.6) | copy-start | bytes 196612
  4.2 7.3 %collective-permute-start.2 = (bf16[128,512]{1,0:T(8,128)(2,1)S(1)}, bf16[128,512]{1,0:T(8,128)(2,1)S(1)}, u32[]{:S(2)}, u32[]{:S(2)}) collective-permute-start(bf16[128,512]{1,0:T(8,128)(2,1)S(1)} %copy.16.refs_1_), channel_id=1, source_target_pairs={{0,24},{4,28},{8,16},{12,20},{16,8},{20,12},{24,0},{28,4},{1,25},{... | collective-permute-start | bytes 393224 | tf_op jit(solution)/shard_map/ppermute | solution.py:219
  6.7 6.2 %collective-permute-start.1 = (bf16[128,512]{1,0:T(8,128)(2,1)S(1)}, bf16[128,512]{1,0:T(8,128)(2,1)S(1)}, u32[]{:S(2)}, u32[]{:S(2)}) collective-permute-start(bf16[128,512]{1,0:T(8,128)(2,1)S(1)} %copy.16.refs_1_), channel_id=1, source_target_pairs={{0,16},{4,20},{8,24},{12,28},{16,0},{20,4},{24,8},{28,12},{1,17},{... | collective-permute-start | bytes 393224 | tf_op jit(solution)/shard_map/ppermute | solution.py:219
  7.2 5.8 %collective-permute-start = (bf16[128,512]{1,0:T(8,128)(2,1)S(1)}, bf16[128,512]{1,0:T(8,128)(2,1)S(1)}, u32[]{:S(2)}, u32[]{:S(2)}) collective-permute-start(bf16[128,512]{1,0:T(8,128)(2,1)S(1)} %copy.16.refs_1_), channel_id=1, source_target_pairs={{0,8},{4,12},{8,0},{12,4},{16,24},{20,28},{24,16},{28,20},{1,9},{5... | collective-permute-start | bytes 393224 | tf_op jit(solution)/shard_map/ppermute | solution.py:219
  7.7 3.4 %copy-start.1 = (s32[1,512]{1,0:T(1,128)S(1)}, s32[1,512]{1,0:T(1,128)}, u32[]{:S(2)}) copy-start(s32[1,512]{1,0:T(1,128)} %rows_ref.1) | copy-start | bytes 6148
  7.7 3.4 %copy-start.2 = (s32[1,512]{1,0:T(1,128)S(1)}, s32[1,512]{1,0:T(1,128)}, u32[]{:S(2)}) copy-start(s32[1,512]{1,0:T(1,128)} %cols_ref.1) | copy-start | bytes 6148
  7.8 3.4 %copy-start.3 = (s32[1,512]{1,0:T(1,128)S(1)}, s32[1,512]{1,0:T(1,128)}, u32[]{:S(2)}) copy-start(s32[1,512]{1,0:T(1,128)} %dist_ref.1) | copy-start | bytes 6148
  7.8 7.7 %collective-permute-start.8 = (bf16[128,512]{1,0:T(8,128)(2,1)S(1)}, bf16[128,512]{1,0:T(8,128)(2,1)S(1)}, u32[]{:S(2)}, u32[]{:S(2)}) collective-permute-start(bf16[128,512]{1,0:T(8,128)(2,1)S(1)} %stack.1), channel_id=1, source_target_pairs={{0,2},{1,3},{2,0},{3,1},{4,6},{5,7},{6,4},{7,5},{8,10},{9,11},{10,... | collective-permute-start | bytes 393224 | tf_op jit(solution)/shard_map/ppermute | solution.py:219
  10.4 6.7 %collective-permute-start.3 = (bf16[128,512]{1,0:T(8,128)(2,1)S(1)}, bf16[128,512]{1,0:T(8,128)(2,1)S(1)}, u32[]{:S(2)}, u32[]{:S(2)}) collective-permute-start(bf16[128,512]{1,0:T(8,128)(2,1)S(1)} %copy.16.refs_1_), channel_id=1, source_target_pairs={{0,4},{4,0},{8,12},{12,8},{16,20},{20,16},{24,28},{28,24},{1,5},{5... | collective-permute-start | bytes 393224 | tf_op jit(solution)/shard_map/ppermute | solution.py:219
  11.4 5.7 %collective-permute-start.6 = (bf16[128,512]{1,0:T(8,128)(2,1)S(1)}, bf16[128,512]{1,0:T(8,128)(2,1)S(1)}, u32[]{:S(2)}, u32[]{:S(2)}) collective-permute-start(bf16[128,512]{1,0:T(8,128)(2,1)S(1)} %collective-permute-done.2.refs_4_), channel_id=1, source_target_pairs={{0,4},{4,0},{8,12},{12,8},{16,20},{20,16},{24,28},{28,24},{1,5},{5... | collective-permute-start | bytes 393224 | tf_op jit(solution)/shard_map/ppermute | solution.py:219
  12.9 4.2 %collective-permute-start.5 = (bf16[128,512]{1,0:T(8,128)(2,1)S(1)}, bf16[128,512]{1,0:T(8,128)(2,1)S(1)}, u32[]{:S(2)}, u32[]{:S(2)}) collective-permute-start(bf16[128,512]{1,0:T(8,128)(2,1)S(1)} %collective-permute-done.1.refs_3_), channel_id=1, source_target_pairs={{0,4},{4,0},{8,12},{12,8},{16,20},{20,16},{24,28},{28,24},{1,5},{5... | collective-permute-start | bytes 393224 | tf_op jit(solution)/shard_map/ppermute | solution.py:219
  13.0 4.2 %collective-permute-start.4 = (bf16[128,512]{1,0:T(8,128)(2,1)S(1)}, bf16[128,512]{1,0:T(8,128)(2,1)S(1)}, u32[]{:S(2)}, u32[]{:S(2)}) collective-permute-start(bf16[128,512]{1,0:T(8,128)(2,1)S(1)} %collective-permute-done.refs_2_), channel_id=1, source_target_pairs={{0,4},{4,0},{8,12},{12,8},{16,20},{20,16},{24,28},{28,24},{1,5},{5... | collective-permute-start | bytes 393224 | tf_op jit(solution)/shard_map/ppermute | solution.py:219
  18.4 9.6 %collective-permute-start.9 = (bf16[64,512]{1,0:T(8,128)(2,1)S(1)}, bf16[64,512]{1,0:T(8,128)(2,1)S(1)}, u32[]{:S(2)}, u32[]{:S(2)}) collective-permute-start(bf16[64,512]{1,0:T(8,128)(2,1)S(1)} %get-tuple-element.28), channel_id=1, source_target_pairs={{0,3},{1,2},{2,1},{3,0},{4,7},{5,6},{6,5},{7,4},{8,11},{9,10},{10,... | collective-permute-start | bytes 196616 | tf_op jit(solution)/shard_map/ppermute | solution.py:219
  22.1 5.9 %collective-permute-start.10 = (bf16[64,512]{1,0:T(8,128)(2,1)S(1)}, bf16[64,512]{1,0:T(8,128)(2,1)S(1)}, u32[]{:S(2)}, u32[]{:S(2)}) collective-permute-start(bf16[64,512]{1,0:T(8,128)(2,1)S(1)} %increment_rows.10), channel_id=1, source_target_pairs={{0,2},{1,3},{2,0},{3,1},{4,6},{5,7},{6,4},{7,5},{8,10},{9,11},{10,... | collective-permute-start | bytes 196616 | tf_op jit(solution)/shard_map/ppermute | solution.py:219
  23.2 4.9 %collective-permute-start.11 = (bf16[64,512]{1,0:T(8,128)(2,1)S(1)}, bf16[64,512]{1,0:T(8,128)(2,1)S(1)}, u32[]{:S(2)}, u32[]{:S(2)}) collective-permute-start(bf16[64,512]{1,0:T(8,128)(2,1)S(1)} %increment_rows.11), channel_id=1, source_target_pairs={{0,1},{1,0},{2,3},{3,2},{4,5},{5,4},{6,7},{7,6},{8,9},{9,8},{10,11... | collective-permute-start | bytes 196616 | tf_op jit(solution)/shard_map/ppermute | solution.py:219
